TPU v7x, 32 devices: a whole 2x2x4 slice. The times are simulated.
32 devices in a mesh: seg: 2 (over y), ep: 16 (over z, x, core).
Axes of the slice: x: 2, y: 2, z: 4, core: 2. Of those that a mesh axis runs over, the one named last changes fastest.
Arguments:
- frames_in: bfloat16 [4096, 2048], P(('seg', 'ep')), may hold values from -36 to 36
- expert_ids: int32 [4096, 6], P(('seg', 'ep')), may hold values from 0 to 15, all different within a row
- gate_values: float32 [4096, 6], P(('seg', 'ep')), may hold values from 0.02 to 0.3
- gate_weight: bfloat16 [16, 2048, 768], P('ep'), may hold values from -0.125 to 0.125
- up_weight: bfloat16 [16, 2048, 768], P('ep'), may hold values from -0.125 to 0.125
- down_weight: bfloat16 [16, 768, 2048], P('ep'), may hold values from -0.21875 to 0.21875
- norm_gain: float32 [2048], replicated, may hold values from 0.5 to 1.5
- pose_weight: bfloat16 [2048, 256], replicated, may hold values from -0.125 to 0.125
- target_pose: float32 [4096, 256], P(('seg', 'ep')), may hold values from -6 to 6
- foot_contact: int32 [4096, 4], P(('seg', 'ep')), may hold values 0 or 1
Outputs:
- grad_input: bfloat16 [4096, 2048], P(('seg', 'ep'))
- grad_gates: float32 [4096, 6], P(('seg', 'ep'))
- loss_value: float32 [], replicated
Inputs may be any that keep to these rules, and one draw needn't show every extreme that they name: `expert_ids`: each row names 6 different experts.
All inputs are finite; a program needn't handle non-finite values. No bound on the sum of `foot_contact` on one device may be relied on, other than what follows from the above.
Results may differ from a plain program's by a relative error of at most 0.011.
Values may be sent and summed in bfloat16 or wider, within the bound.
No kernel may reach another device: no remote copies, remote signals or barrier semaphores. Data moves between devices by JAX's collectives and lax.ppermute only.
A program may use at most 128 MiB of HBM per device.

v0:
```python
import jax
import jax.numpy as jnp
from jax import lax
from jax.sharding import PartitionSpec as P

epsilon = 1e-06
foot_weight = 2.0


def from_behind(block, axis, distance):
    devices = range(lax.axis_size(axis))
    route = [(i - distance, i) for i in devices if i - distance in devices]
    return lax.ppermute(block, axis, route)


def silu_parts(pre_act):
    gate_sigmoid = jax.nn.sigmoid(pre_act)
    return (pre_act * gate_sigmoid, gate_sigmoid * (1.0 + pre_act * (1.0 - gate_sigmoid)))


def foot_term(horizon, contact_rep, velocity):
    return foot_weight * horizon[:, None] * contact_rep * velocity


def slot_tables(expert_ids, experts, capacity):
    pair_count = expert_ids.shape[0] * expert_ids.shape[1]
    flat_ids = expert_ids.reshape(-1)
    onehot = (flat_ids[:, None] == jnp.arange(experts, dtype=jnp.int32)[None, :]).astype(jnp.int32)
    earlier_hits = jnp.cumsum(onehot, axis=0) - onehot
    slot_rank = jnp.sum(earlier_hits * onehot, axis=1)
    kept_mask = slot_rank < capacity
    spare_slot = experts * capacity
    position = jnp.where(kept_mask, flat_ids * capacity + slot_rank, spare_slot)
    pair_of_slot = (
        jnp.full((spare_slot + 1,), pair_count, jnp.int32)
        .at[position]
        .set(jnp.arange(pair_count, dtype=jnp.int32))[:spare_slot]
    )
    return (position, pair_of_slot)


def per_device(
    frames_in,
    expert_ids,
    gate_values,
    gate_weight,
    up_weight,
    down_weight,
    norm_gain,
    pose_weight,
    target_pose,
    foot_contact,
):
    tok_rows, model_width = frames_in.shape
    top_count = expert_ids.shape[1]
    local_experts = gate_weight.shape[0]
    ep_count = lax.axis_size("ep")
    experts = local_experts * ep_count
    capacity = tok_rows * top_count // experts
    position, pair_of_slot = slot_tables(expert_ids, experts, capacity)
    token_of_slot = pair_of_slot // top_count
    zero_row = jnp.zeros((1, model_width), jnp.bfloat16)
    padded_in = jnp.concatenate([frames_in, zero_row], 0)
    send_rows = padded_in[token_of_slot].reshape(experts, capacity, model_width)
    received = lax.all_to_all(send_rows, "ep", split_axis=0, concat_axis=0, tiled=True)
    slot_count = received.shape[1]
    grouped = received.reshape(ep_count, local_experts, slot_count, model_width)
    gate_pre = jnp.einsum(
        "sexd,edf->sexf", grouped, gate_weight, preferred_element_type=jnp.float32
    )
    up_pre = jnp.einsum("sexd,edf->sexf", grouped, up_weight, preferred_element_type=jnp.float32)
    activated = silu_parts(gate_pre)[0]
    hidden = (activated * up_pre).astype(jnp.bfloat16)
    produced = jnp.einsum(
        "sexf,efd->sexd", hidden, down_weight, preferred_element_type=jnp.float32
    ).astype(jnp.bfloat16)
    produced = produced.reshape(experts, slot_count, model_width)
    returned = lax.all_to_all(produced, "ep", split_axis=0, concat_axis=0, tiled=True)
    hidden_width = gate_pre.shape[-1]
    returned, produced_local, gate_keep, up_keep = (
        returned,
        produced,
        gate_pre.reshape(experts, slot_count, hidden_width),
        up_pre.reshape(experts, slot_count, hidden_width),
    )
    back_flat = jnp.concatenate([returned.reshape(experts * capacity, model_width), zero_row], 0)
    picked = back_flat[position].reshape(tok_rows, top_count, model_width)
    mixed_rows = jnp.sum(gate_values[:, :, None] * picked, axis=1)
    state_rows = frames_in.astype(jnp.float32) + mixed_rows
    inverse_rms = lax.rsqrt(jnp.mean(state_rows * state_rows, axis=1, keepdims=True) + epsilon)
    unit_rows = state_rows * inverse_rms
    normed = (unit_rows * norm_gain).astype(jnp.bfloat16)
    pose_out = jnp.dot(normed, pose_weight, preferred_element_type=jnp.float32)
    pose_cols = pose_out.shape[1]
    device = lax.axis_index("seg") * ep_count + lax.axis_index("ep")
    frames_all = lax.axis_size("seg") * ep_count * tok_rows
    frame_index = device * tok_rows + jnp.arange(tok_rows, dtype=jnp.int32)
    horizon = 0.5 + frame_index.astype(jnp.float32) / (frames_all - 1)
    feet_count = foot_contact.shape[1]
    foot_cols = 3 * feet_count
    foot_pos = pose_out[:, :foot_cols]
    contact_float = foot_contact.astype(jnp.float32)
    contact_rep = jnp.repeat(contact_float, 3, axis=1)
    before = from_behind(foot_pos[tok_rows - 1 :], ("seg", "ep"), 1)
    earlier = jnp.concatenate([before, foot_pos[:-1]], 0)
    velocity = jnp.where((frame_index > 0)[:, None], foot_pos - earlier, 0.0)
    foot_pull = foot_term(horizon, contact_rep, velocity)
    next_pull = from_behind(foot_pull[:1], ("seg", "ep"), -1)
    pose_error = pose_out - target_pose
    local_sum = 0.5 * jnp.sum(horizon[:, None] * pose_error * pose_error) + 0.5 * jnp.sum(
        foot_pull * velocity
    )
    summed = lax.psum(local_sum, ("seg", "ep"))
    loss_value = summed / (frames_all * pose_cols)
    later_pull = jnp.concatenate([foot_pull[1:], next_pull], 0)
    grad_pose = horizon[:, None] * pose_error
    grad_pose = jnp.concatenate(
        [grad_pose[:, :foot_cols] + (foot_pull - later_pull), grad_pose[:, foot_cols:]], 1
    )
    grad_normed = jnp.einsum(
        "tp,dp->td", grad_pose.astype(jnp.bfloat16), pose_weight, preferred_element_type=jnp.float32
    )
    scaled = grad_normed * norm_gain
    grad_state = inverse_rms * (
        scaled - unit_rows * jnp.mean(scaled * unit_rows, axis=1, keepdims=True)
    )
    moe_grad = grad_state.astype(jnp.bfloat16)
    pair_grad = (gate_values[:, :, None] * moe_grad[:, None, :]).astype(jnp.bfloat16)
    pair_flat = jnp.concatenate([pair_grad.reshape(tok_rows * top_count, model_width), zero_row], 0)
    grad_send = pair_flat[pair_of_slot].reshape(experts, capacity, model_width)
    arrived = lax.all_to_all(grad_send, "ep", split_axis=0, concat_axis=0, tiled=True)
    slot_count = arrived.shape[1]
    hidden_width = gate_keep.shape[-1]
    grouped = arrived.reshape(ep_count, local_experts, slot_count, model_width)
    gate_pre = gate_keep.reshape(ep_count, local_experts, slot_count, hidden_width)
    up_pre = up_keep.reshape(ep_count, local_experts, slot_count, hidden_width)
    grad_hidden = jnp.einsum(
        "sexd,efd->sexf", grouped, down_weight, preferred_element_type=jnp.float32
    )
    activated, silu_slope = silu_parts(gate_pre)
    grad_gate_pre = (grad_hidden * up_pre * silu_slope).astype(jnp.bfloat16)
    grad_up_pre = (grad_hidden * activated).astype(jnp.bfloat16)
    grad_rows = jnp.einsum(
        "sexf,edf->sexd", grad_gate_pre, gate_weight, preferred_element_type=jnp.float32
    )
    grad_rows = grad_rows + jnp.einsum(
        "sexf,edf->sexd", grad_up_pre, up_weight, preferred_element_type=jnp.float32
    )
    grad_rows = grad_rows.astype(jnp.bfloat16).reshape(experts, slot_count, model_width)
    grad_back = lax.all_to_all(grad_rows, "ep", split_axis=0, concat_axis=0, tiled=True)
    grad_gates = jnp.einsum("tkd,td->tk", picked, moe_grad, preferred_element_type=jnp.float32)
    grad_flat = jnp.concatenate([grad_back.reshape(experts * capacity, model_width), zero_row], 0)
    grad_picked = grad_flat[position].reshape(tok_rows, top_count, model_width)
    grad_input = (grad_state + jnp.sum(grad_picked.astype(jnp.float32), axis=1)).astype(
        jnp.bfloat16
    )
    return (grad_input, grad_gates, loss_value)


def solution(mesh):
    in_specs = (
        P(("seg", "ep"), None),
        P(("seg", "ep"), None),
        P(("seg", "ep"), None),
        P("ep", None, None),
        P("ep", None, None),
        P("ep", None, None),
        P(),
        P(),
        P(("seg", "ep"), None),
        P(("seg", "ep"), None),
    )
    out_specs = (P(("seg", "ep"), None), P(("seg", "ep"), None), P())
    return jax.shard_map(
        per_device, mesh=mesh, in_specs=in_specs, out_specs=out_specs, check_vma=False
    )
```

profile of v0, /device:TPU:0, one launch (start us, length us, event | category | flops | bytes accessed | tf_op | source)
XLA Modules:
  0.0 469.5 jit_solution(862500075467647736)
XLA Ops:
  5.1 3.4 scatter_custom_fusion
  10.4 8.2 %gather_fusion = bf16[768,2048]{1,0:T(8,128)(2,1)} fusion(bf16[129,2048]{1,0:T(8,128)(2,1)} %concatenate.22, s32[1024]{0:T(1024)S(1)} %get-tuple-element.15), kind=kCustom, calls=%fused_computation | custom fusion | bytes 6294528 | tf_op jit(solution)/shard_map/gather | solution.py:64
  18.6 77.4 %all_to_all.20 = bf16[16,48,2048]{2,1,0:T(8,128)(2,1)S(1)} all-to-all(bf16[16,48,2048]{2,1,0:T(8,128)(2,1)} %bitcast.130), channel_id=1, replica_groups=mesh['seg'=2,'ep'=16] {'ep'}, dimensions={0} | all-to-all | bytes 6291456 | tf_op jit(solution)/shard_map/all_to_all | solution.py:65
  102.7 4.1 convolution_convert_fusion
  106.8 5.4 %all-to-all-start.1 = ((bf16[16,48,2048]{2,1,0:T(8,128)(2,1)}), bf16[16,48,2048]{2,1,0:T(8,128)(2,1)}, u32[]{:S(2)}, u32[]{:S(2)}) async-start(bf16[16,48,2048]{2,1,0:T(8,128)(2,1)} %convolution_convert_fusion), calls=%async_computation.1 | async-start | bytes 6291456 | tf_op jit(solution)/shard_map/all_to_all | solution.py:78
  112.6 58.9 %all-to-all-done.1 = bf16[16,48,2048]{2,1,0:T(8,128)(2,1)} async-done(((bf16[16,48,2048]{2,1,0:T(8,128)(2,1)}), bf16[16,48,2048]{2,1,0:T(8,128)(2,1)}, u32[]{:S(2)}, u32[]{:S(2)}) %all-to-all-start.1) | async-done | bytes 3145760 | tf_op jit(solution)/shard_map/all_to_all | solution.py:78
  171.6 4.0 concatenate.23
  175.5 9.4 %gather_fusion.1 = bf16[768,2048]{1,0:T(8,128)(2,1)} fusion(bf16[769,2048]{1,0:T(8,128)(2,1)} %concatenate.23, s32[1024]{0:T(1024)S(1)} %pad_clamp_fusion.1), kind=kCustom, calls=%fused_computation.1 | custom fusion | bytes 6294528 | tf_op jit(solution)/shard_map/gather | solution.py:87
  185.0 6.3 %reshape.159 = bf16[128,6,2048]{2,1,0:T(8,128)(2,1)} reshape(bf16[768,2048]{1,0:T(8,128)(2,1)} %gather_fusion.1) | data formatting | bytes 6291456 | tf_op jit(solution)/shard_map/reshape | solution.py:87
  191.2 5.7 %multiply_reduce_fusion = f32[128,2048]{1,0:T(8,128)S(1)} fusion(bf16[128,6,2048]{2,1,0:T(8,128)(2,1)} %reshape.159, f32[128,6]{1,0:T(8,128)S(1)} %copy.35), kind=kLoop, calls=%fused_computation.5 | loop fusion | flops 4456448 | bytes 4197376 | tf_op jit(solution)/shard_map/reduce_sum | solution.py:88
  203.9 5.0 %collective-permute-done.1 = f32[1,12]{1,0:T(1,128)S(1)} collective-permute-done((f32[1,12]{1,0:T(1,128)S(1)}, f32[1,12]{1,0:T(1,128)S(1)}, u32[]{:S(2)}, u32[]{:S(2)}) %collective-permute-start.1) | collective-permute-done | bytes 80 | tf_op jit(solution)/shard_map/ppermute | solution.py:13
  211.7 4.3 mul.184
  216.0 8.3 %mul.185 = f32[768,2048]{1,0:T(8,128)} reshape(f32[128,6,2048]{2,1,0:T(8,128)} %mul.184) | data formatting | bytes 12582912 | tf_op jit(solution)/shard_map/mul | solution.py:128
  229.5 9.4 %gather_fusion.2 = bf16[768,2048]{1,0:T(8,128)(2,1)} fusion(bf16[769,2048]{1,0:T(8,128)(2,1)} %concatenate.27, s32[1024]{0:T(1024)S(1)} %get-tuple-element.14), kind=kCustom, calls=%fused_computation.2 | custom fusion | bytes 6294528 | tf_op jit(solution)/shard_map/gather | solution.py:130
  238.9 86.7 %all_to_all.21 = bf16[16,48,2048]{2,1,0:T(8,128)(2,1)S(1)} all-to-all(bf16[16,48,2048]{2,1,0:T(8,128)(2,1)} %bitcast.131), channel_id=1, replica_groups=mesh['seg'=2,'ep'=16] {'ep'}, dimensions={0} | all-to-all | bytes 6291456 | tf_op jit(solution)/shard_map/all_to_all | solution.py:131
  328.9 3.2 fusion.6
  332.2 4.1 add_convert_fusion
  336.3 5.2 %all-to-all-start.3 = ((bf16[16,48,2048]{2,1,0:T(8,128)(2,1)}), bf16[16,48,2048]{2,1,0:T(8,128)(2,1)}, u32[]{:S(2)}, u32[]{:S(2)}) async-start(bf16[16,48,2048]{2,1,0:T(8,128)(2,1)} %add_convert_fusion), calls=%async_computation.3 | async-start | bytes 6291456 | tf_op jit(solution)/shard_map/all_to_all | solution.py:150
  342.8 89.6 %psum.7 = f32[]{:T(128)} all-reduce(f32[]{:T(128)S(6)} %add.129), channel_id=1, replica_groups=mesh['seg'=2,'ep'=16] {'seg','ep'}, use_global_device_ids=true, to_apply=%region_10.11 | all-reduce | flops 1 | bytes 8 | tf_op jit(solution)/shard_map/psum | solution.py:113
  433.1 5.2 %fusion.25 = f32[128,1,6]{2,1,0:T(1,128)S(1)} fusion(bf16[128,6,2048]{2,1,0:T(8,128)(2,1)} %reshape.159, bf16[128,2048,1]{1,0,2:T(8,128)(2,1)} %get-tuple-element.5), kind=kOutput, calls=%fused_computation.38 | convolution fusion | flops 3145728 | bytes 3673088 | tf_op jit(solution)/shard_map/tkd,td->tk/dot_general | solution.py:151
  438.9 4.0 concatenate.28
  442.9 9.4 %gather_fusion.3 = bf16[768,2048]{1,0:T(8,128)(2,1)} fusion(bf16[769,2048]{1,0:T(8,128)(2,1)} %concatenate.28, s32[1024]{0:T(1024)S(1)} %pad_clamp_fusion.1), kind=kCustom, calls=%fused_computation.3 | custom fusion | bytes 6294528 | tf_op jit(solution)/shard_map/gather | solution.py:153
  452.3 6.6 %reshape.165 = f32[128,6,2048]{2,1,0:T(8,128)} reshape(bf16[768,2048]{1,0:T(8,128)(2,1)} %gather_fusion.3) | data formatting | bytes 9437184 | tf_op jit(solution)/shard_map/convert_element_type | solution.py:154
  458.8 7.1 %reduce_sum.70 = f32[128,2048]{1,0:T(8,128)} reduce(f32[128,6,2048]{2,1,0:T(8,128)} %reshape.165, f32[]{:T(128)} %constant.19.clone.1), dimensions={1}, to_apply=%region_7.8 | reduce | flops 1310720 | bytes 7340036 | tf_op jit(solution)/shard_map/reduce_sum | solution.py:154
  (83 shorter events, 34.7 us)
Async XLA Ops:
  0.6 102.1 %copy-start = (bf16[1,768,2048]{2,1,0:T(8,128)(2,1)S(1)}, bf16[1,768,2048]{2,1,0:T(8,128)(2,1)}, u32[]{:S(2)}) copy-start(bf16[1,768,2048]{2,1,0:T(8,128)(2,1)} %param.15) | copy-start | bytes 9437188
  18.6 77.4 %copy-start.8 = (bf16[1,2048,768]{2,1,0:T(8,128)(2,1)S(1)}, bf16[1,2048,768]{2,1,0:T(8,128)(2,1)}, u32[]{:S(2)}) copy-start(bf16[1,2048,768]{2,1,0:T(8,128)(2,1)} %param.13) | copy-start | bytes 9437188
  96.0 2.6 copy-start.10
  98.7 2.6 copy-start.12
  101.3 1.4 copy-start.14
  106.8 5.4 %copy-start.7 = (s32[128,4]{0,1:T(4,128)S(1)}, s32[128,4]{0,1:T(4,128)}, u32[]{:S(2)}) copy-start(s32[128,4]{0,1:T(4,128)} %param.19) | copy-start | bytes 6148
  106.8 5.5 %copy-start.6 = (f32[128,6]{0,1:T(8,128)S(1)}, f32[128,6]{0,1:T(8,128)}, u32[]{:S(2)}) copy-start(f32[128,6]{0,1:T(8,128)} %param.12) | copy-start | bytes 9220
  106.8 64.8 %all-to-all-start.1 = ((bf16[16,48,2048]{2,1,0:T(8,128)(2,1)}), bf16[16,48,2048]{2,1,0:T(8,128)(2,1)}, u32[]{:S(2)}, u32[]{:S(2)}) async-start(bf16[16,48,2048]{2,1,0:T(8,128)(2,1)} %convolution_convert_fusion), calls=%async_computation.1 | async-start | bytes 6291456 | tf_op jit(solution)/shard_map/all_to_all | solution.py:78
  191.2 5.7 %copy-start.1 = (bf16[128,2048]{1,0:T(8,128)(2,1)S(1)}, bf16[128,2048]{1,0:T(8,128)(2,1)}, u32[]{:S(2)}) copy-start(bf16[128,2048]{1,0:T(8,128)(2,1)} %param.10) | copy-start | bytes 1572868
  191.2 5.9 %copy-start.3 = (bf16[2048,256]{1,0:T(8,128)(2,1)S(1)}, bf16[2048,256]{1,0:T(8,128)(2,1)}, u32[]{:S(2)}) copy-start(bf16[2048,256]{1,0:T(8,128)(2,1)} %param.17) | copy-start | bytes 3145732
  191.2 6.0 %copy-start.4 = (f32[128,256]{1,0:T(8,128)S(1)}, f32[128,256]{1,0:T(8,128)}, u32[]{:S(2)}) copy-start(f32[128,256]{1,0:T(8,128)} %param.18) | copy-start | bytes 393220
  191.2 6.0 %copy-start.5 = (f32[2048]{0:T(1024)S(1)}, f32[2048]{0:T(1024)}, u32[]{:S(2)}) copy-start(f32[2048]{0:T(1024)} %param.16) | copy-start | bytes 24580
  198.2 3.5 collective-permute-start
  202.4 6.5 %collective-permute-start.1 = (f32[1,12]{1,0:T(1,128)S(1)}, f32[1,12]{1,0:T(1,128)S(1)}, u32[]{:S(2)}, u32[]{:S(2)}) collective-permute-start(f32[1,12]{1,0:T(1,128)S(1)} %slice.57), channel_id=1, source_target_pairs={{1,0},{2,1},{3,2},{4,3},{5,4},{6,5},{7,6},{8,7},{9,8},{10,9},{11,1... | collective-permute-start | bytes 152 | tf_op jit(solution)/shard_map/ppermute | solution.py:13
  210.7 1.0 copy-start.2
  325.6 2.7 copy-start.9
  325.6 2.7 copy-start.13
  325.6 3.3 copy-start.15
  328.9 3.2 copy-start.11
  336.3 102.6 %all-to-all-start.3 = ((bf16[16,48,2048]{2,1,0:T(8,128)(2,1)}), bf16[16,48,2048]{2,1,0:T(8,128)(2,1)}, u32[]{:S(2)}, u32[]{:S(2)}) async-start(bf16[16,48,2048]{2,1,0:T(8,128)(2,1)} %add_convert_fusion), calls=%async_computation.3 | async-start | bytes 6291456 | tf_op jit(solution)/shard_map/all_to_all | solution.py:150
where the time goes:
time: 471 us; the launch traced here: 470 us
  blocking collectives  254 us (54%)
  local copies, waits for them, and re-layouts  82.9 us (18%)
  waiting for transfers between devices  64.7 us (14%)
  matrix products  26 us (6%)
  other arithmetic  23.4 us (5%)
  starting transfers between devices  14.8 us (3%)
    psum x1, blocking collectives, per_device(): summed = lax.psum(local_sum, ('seg', 'ep'))  89.6 us
    all_to_all x1, blocking collectives, per_device(): lax.all_to_all(grad_send, 'ep', split_axis=0, concat_axis=0, tiled=True)  86.7 us
    all_to_all x1, blocking collectives, per_device(): lax.all_to_all(send_rows, 'ep', split_axis=0, concat_axis=0, tiled=True)  77.4 us
    all_to_all x1, waiting for transfers between devices, per_device(): lax.all_to_all(produced, 'ep', split_axis=0, concat_axis=0, tiled=True)  58.9 us
    mul x2, local copies, waits for them, and re-layouts, per_device(): gate_values[:, :, None] * moe_grad[:, None, :]  12.5 us
    gather x1, local copies, waits for them, and re-layouts, per_device(): picked = back_flat[position].reshape(tok_rows, top_count, model_width)  9.43 us
    gather x1, local copies, waits for them, and re-layouts, per_device(): grad_send = pair_flat[pair_of_slot].reshape(experts, capacity, model_width)  9.43 us
  transfers between devices with their start and end apart: 4, of which 3 were waited for; matrix products, arithmetic and copies ran while one was open for 1% of the time, Pallas kernels for 0%

commit v1 on v0

v1 whole, which is shorter than its diff:
```python
import jax
import jax.numpy as jnp
from jax import lax
from jax.sharding import PartitionSpec as P

epsilon = 1e-06
foot_weight = 2.0
both = ("seg", "ep")


def swap(block, distance):
    route = [(i, i ^ distance) for i in range(lax.axis_size("ep"))]
    return lax.ppermute(block, "ep", route)


def from_behind(block, axis, distance):
    devices = range(lax.axis_size(axis))
    route = [(i - distance, i) for i in devices if i - distance in devices]
    return lax.ppermute(block, axis, route)


def dot(a, b, dims):
    return lax.dot_general(a, b, (dims, ((), ())), preferred_element_type=jnp.float32)


def split_levels(ep_count):
    level = 1
    while 4 * level * level <= ep_count:
        level *= 2
    return level, ep_count // level


def member_tables(ids, gates, experts_of, capacity):
    blocks, top, frames = ids.shape
    peers = experts_of.shape[0]
    hit = ids[:, None] == experts_of[None, :, None, None]
    member = jnp.any(hit, axis=2)
    gate_of = jnp.sum(jnp.where(hit, gates[:, None], 0.0), axis=2)
    upper = (jnp.arange(frames)[:, None] < jnp.arange(frames)[None, :]).astype(jnp.bfloat16)
    rank = dot(member.astype(jnp.bfloat16).reshape(blocks * peers, frames), upper, ((1,), (0,)))
    rank = rank.astype(jnp.int32).reshape(blocks, peers, 1, frames)
    slot = jnp.arange(capacity, dtype=jnp.int32)[None, None, :, None]
    chosen = jnp.logical_and(member[:, :, None], rank == slot)
    slot_gate = jnp.sum(jnp.where(chosen, gate_of[:, :, None], 0.0), axis=3)
    pick = chosen.astype(jnp.bfloat16).reshape(blocks, peers * capacity, frames)
    return pick, slot_gate.reshape(blocks, peers * capacity, 1)


def per_device(
    frames_in,
    expert_ids,
    gate_values,
    gate_weight,
    up_weight,
    down_weight,
    norm_gain,
    pose_weight,
    target_pose,
    foot_contact,
):
    tok_rows, width = frames_in.shape
    top = expert_ids.shape[1]
    ep_count = lax.axis_size("ep")
    experts = ep_count
    capacity = tok_rows * top // experts
    layers, peers = split_levels(ep_count)
    me = lax.axis_index("ep")
    my_layer, my_peer = me // peers, me % peers
    gate_w, up_w, down_w = gate_weight[0], up_weight[0], down_weight[0]
    order = [0, 1, 3, 2] if layers == 4 else list(range(layers))

    ids_t, gates_t = expert_ids.T, gate_values.T
    routing = jnp.concatenate([ids_t.astype(jnp.float32), gates_t], 0)
    layer_experts = my_layer * peers + (my_peer ^ jnp.arange(peers, dtype=jnp.int32))
    tables = {0: member_tables(ids_t[None], gates_t[None], layer_experts, capacity)}
    others = [k for k in order if k]
    got = jnp.stack([swap(routing, k * peers) for k in others])
    other_pick, other_gate = member_tables(
        got[:, :top].astype(jnp.int32), got[:, top:], layer_experts, capacity
    )
    pick = {0: tables[0][0][0]}
    slot_gate = {0: tables[0][1][0]}
    for i, k in enumerate(others):
        pick[k], slot_gate[k] = other_pick[i], other_gate[i]

    def spread(rows):
        held = {0: rows}
        if layers == 4:
            held[3] = swap(rows, 3 * peers)
            held[1] = swap(rows, peers)
            inner = [i for i in range(ep_count) if i // peers in (1, 2)]
            over = lax.ppermute(held[1], "ep", [(i, i ^ (3 * peers)) for i in inner])
            out = lax.ppermute(held[3], "ep", [(i, i ^ peers) for i in inner])
            inside = jnp.logical_or(my_layer == 1, my_layer == 2)
            held[2] = jnp.where(inside, over, out)
        else:
            for k in range(1, layers):
                held[k] = swap(rows, k * peers)
        return held

    def to_experts(rows):
        rows = rows.reshape(peers, capacity, -1)
        parts = [rows[0]] + [swap(rows[j], j) for j in range(1, peers)]
        return jnp.concatenate(parts, 0)

    held = spread(frames_in)
    gate_pre, up_pre, mixed = {}, {}, {}
    for k in order:
        sent = dot(pick[k], held[k], ((1,), (0,))).astype(jnp.bfloat16)
        rows = to_experts(sent)
        gate_pre[k] = dot(rows, gate_w, ((1,), (0,)))
        up_pre[k] = dot(rows, up_w, ((1,), (0,)))
        hidden = (gate_pre[k] * jax.nn.sigmoid(gate_pre[k]) * up_pre[k]).astype(jnp.bfloat16)
        produced = dot(hidden, down_w, ((1,), (0,))).astype(jnp.bfloat16)
        returned = to_experts(produced)
        weight = pick[k].astype(jnp.float32) * slot_gate[k]
        high = lax.reduce_precision(weight, 8, 7)
        low = weight - high
        part = dot(high.astype(jnp.bfloat16), returned, ((0,), (0,)))
        part = part + dot(low.astype(jnp.bfloat16), returned, ((0,), (0,)))
        mixed[k] = swap(part.astype(jnp.bfloat16), k * peers).astype(jnp.float32) if k else part
    mixed_rows = sum(mixed[k] for k in reversed(order))

    state_rows = frames_in.astype(jnp.float32) + mixed_rows
    inverse_rms = lax.rsqrt(jnp.mean(state_rows * state_rows, axis=1, keepdims=True) + epsilon)
    unit_rows = state_rows * inverse_rms
    normed = (unit_rows * norm_gain).astype(jnp.bfloat16)
    pose_out = dot(normed, pose_weight, ((1,), (0,)))
    pose_cols = pose_out.shape[1]
    device = lax.axis_index("seg") * ep_count + me
    frames_all = lax.axis_size("seg") * ep_count * tok_rows
    frame_index = device * tok_rows + jnp.arange(tok_rows, dtype=jnp.int32)
    horizon = 0.5 + frame_index.astype(jnp.float32) / (frames_all - 1)
    feet = foot_contact.shape[1]
    foot_cols = 3 * feet
    foot_pos = pose_out[:, :foot_cols]
    contact = jnp.repeat(foot_contact.astype(jnp.float32), 3, axis=1)
    before = from_behind(foot_pos[tok_rows - 1 :], both, 1)
    after = from_behind(jnp.concatenate([foot_pos[:1], contact[:1]], 1), both, -1)
    earlier = jnp.concatenate([before, foot_pos[:-1]], 0)
    velocity = jnp.where((frame_index > 0)[:, None], foot_pos - earlier, 0.0)
    foot_pull = foot_weight * horizon[:, None] * contact * velocity
    next_horizon = 0.5 + (device * tok_rows + tok_rows).astype(jnp.float32) / (frames_all - 1)
    next_velocity = after[:, :foot_cols] - foot_pos[tok_rows - 1 :]
    next_pull = foot_weight * next_horizon * after[:, foot_cols:] * next_velocity
    pose_error = pose_out - target_pose
    local_sum = 0.5 * jnp.sum(horizon[:, None] * pose_error * pose_error) + 0.5 * jnp.sum(
        foot_pull * velocity
    )
    loss_value = lax.psum(local_sum, both) / (frames_all * pose_cols)
    later_pull = jnp.concatenate([foot_pull[1:], next_pull], 0)
    grad_pose = horizon[:, None] * pose_error
    grad_pose = jnp.concatenate(
        [grad_pose[:, :foot_cols] + (foot_pull - later_pull), grad_pose[:, foot_cols:]], 1
    )
    grad_normed = dot(grad_pose.astype(jnp.bfloat16), pose_weight, ((1,), (1,)))
    scaled = grad_normed * norm_gain
    grad_state = inverse_rms * (
        scaled - unit_rows * jnp.mean(scaled * unit_rows, axis=1, keepdims=True)
    )
    moe_grad = grad_state.astype(jnp.bfloat16)

    held = spread(moe_grad)
    back, slot_dots = {}, {}
    for k in order:
        sent = (dot(pick[k], held[k], ((1,), (0,))) * slot_gate[k]).astype(jnp.bfloat16)
        rows = to_experts(sent)
        grad_hidden = dot(rows, down_w, ((1,), (1,)))
        sig = jax.nn.sigmoid(gate_pre[k])
        activated = gate_pre[k] * sig
        slope = sig * (1.0 + gate_pre[k] * (1.0 - sig))
        slot_dots[k] = jnp.sum(grad_hidden * (activated * up_pre[k]), axis=1)
        grad_gate_pre = (grad_hidden * up_pre[k] * slope).astype(jnp.bfloat16)
        grad_up_pre = (grad_hidden * activated).astype(jnp.bfloat16)
        grad_rows = dot(grad_gate_pre, gate_w, ((1,), (1,)))
        grad_rows = grad_rows + dot(grad_up_pre, up_w, ((1,), (1,)))
        returned = to_experts(grad_rows.astype(jnp.bfloat16))
        part = dot(pick[k], returned, ((0,), (0,)))
        back[k] = swap(part.astype(jnp.bfloat16), k * peers).astype(jnp.float32) if k else part
    grad_input = (grad_state + sum(back[k] for k in reversed(order))).astype(jnp.bfloat16)

    dots = jnp.stack([slot_dots[k].reshape(peers, capacity) for k in range(layers)], 1)
    dots = jnp.stack([dots[0]] + [swap(dots[j], j) for j in range(1, peers)], 1)
    dots = jnp.stack([dots[0]] + [swap(dots[k], k * peers) for k in range(1, layers)], 0)
    dots = dots.reshape(experts, capacity)
    expert_of = me ^ jnp.arange(experts, dtype=jnp.int32)
    own_pick, unused = member_tables(ids_t[None], gates_t[None], expert_of, capacity)
    own_pick = own_pick.reshape(experts, capacity, tok_rows)
    spot = jnp.sum(jnp.where(own_pick > 0, dots[:, :, None], 0.0), axis=1)
    match = ids_t[:, None, :] == expert_of[None, :, None]
    grad_gates = jnp.sum(jnp.where(match, spot[None], 0.0), axis=1) / gates_t
    return (grad_input, grad_gates.T, loss_value)


def solution(mesh):
    rows = P(both, None)
    expert = P("ep", None, None)
    in_specs = (rows, rows, rows, expert, expert, expert, P(), P(), rows, rows)
    return jax.shard_map(
        per_device, mesh=mesh, in_specs=in_specs, out_specs=(rows, rows, P()), check_vma=False
    )
```

time: 471 us -> 362 us (0.77)
  blocking collectives: 254 us -> 47.1 us
  waiting for transfers between devices: 64.7 us -> 154 us
  local copies, waits for them, and re-layouts: 82.9 us -> 14.3 us
  starting transfers between devices: 14.8 us -> 75.5 us
  matrix products: 26 us -> 58.2 us
  other arithmetic: 23.4 us -> 6.85 us
    all_to_all x2 -> x0, blocking collectives: 164 us -> none  [the longest x1 86.7 us: per_device(): lax.all_to_all(grad_send, 'ep', split_axis=0, concat_axis=0, tiled=True)]
    ppermute x0 -> x71, waiting for transfers between devices: none -> 152 us  [the longest x67 152 us: swap(): return lax.ppermute(block, 'ep', route)]
    ppermute x0 -> x71, starting transfers between devices: none -> 70.6 us  [the longest x67 65.4 us: swap(): return lax.ppermute(block, 'ep', route)]
    all_to_all x2 -> x0, waiting for transfers between devices: 58.9 us -> none  [the longest x1 58.9 us: per_device(): lax.all_to_all(produced, 'ep', split_axis=0, concat_axis=0, tiled=True)]
    psum x1, blocking collectives: 89.6 us -> 47.1 us  [per_device(): loss_value = lax.psum(local_sum, both) / (frames_all * pose_cols)]
    gather x4 -> x0, local copies, waits for them, and re-layouts: 36.5 us -> none  [the longest x1 9.43 us: per_device(): picked = back_flat[position].reshape(tok_rows, top_count, model_width)]
    dot_general x9 -> x49, matrix products: 26 us -> 58.2 us  [dot(): lax.dot_general(a, b, (dims, ((), ())), preferred_element_type=jnp.float32)]
    mul x5 -> x4, local copies, waits for them, and re-layouts: 12.9 us -> 0.33 us  [per_device(): weight = pick[k].astype(jnp.float32) * slot_gate[k]]
  transfers between devices with their start and end apart: 4 -> 73, of which waited for: 3 -> 32; matrix products, arithmetic and copies ran while one was open for 1% -> 18% of each run, Pallas kernels for 0% -> 0%
where the time goes in v1:
time: 362 us; the launch traced here: 361 us
  waiting for transfers between devices  154 us (43%)
  starting transfers between devices  75.5 us (21%)
  matrix products  58.2 us (16%)
  blocking collectives  47.1 us (13%)
  local copies, waits for them, and re-layouts  14.3 us (4%)
  other arithmetic  6.85 us (2%)
  between operations  4.86 us (1%)
    ppermute x67, waiting for transfers between devices, swap(): return lax.ppermute(block, 'ep', route)  152 us
    ppermute x67, starting transfers between devices, swap(): return lax.ppermute(block, 'ep', route)  65.4 us
    dot_general x49, matrix products, dot(): lax.dot_general(a, b, (dims, ((), ())), preferred_element_type=jnp.float32)  58.2 us
    psum x1, blocking collectives, per_device(): loss_value = lax.psum(local_sum, both) / (frames_all * pose_cols)  47.1 us
    slice x16, local copies, waits for them, and re-layouts, to_experts(): parts = [rows[0]] + [swap(rows[j], j) for j in range(1, peers)]  8.26 us
  transfers between devices with their start and end apart: 73, of which 32 were waited for; matrix products, arithmetic and copies ran while one was open for 18% of the time, Pallas kernels for 0%

profile of v1, /device:TPU:0, one launch (start us, length us, event | category | flops | bytes accessed | tf_op | source)
XLA Modules:
  0.0 360.8 jit_solution(4010914792757774218)
XLA Ops:
  2.3 4.0 %collective-permute-start.2 = (f32[12,128]{1,0:T(8,128)S(1)}, f32[12,128]{1,0:T(8,128)S(1)}, u32[]{:S(2)}, u32[]{:S(2)}) collective-permute-start(f32[12,128]{1,0:T(8,128)S(1)} %pad_maximum_fusion.27), channel_id=1, source_target_pairs={{0,8},{1,9},{2,10},{3,11},{4,12},{5,13},{6,14},{7,15},{8,0},{9,1},... | collective-permute-start | bytes 18440 | tf_op jit(solution)/shard_map/ppermute | solution.py:13
  20.1 4.0 %collective-permute-done.30 = bf16[48,2048]{1,0:T(8,128)(2,1)} collective-permute-done((bf16[48,2048]{1,0:T(8,128)(2,1)}, bf16[48,2048]{1,0:T(8,128)(2,1)}, u32[]{:S(2)}, u32[]{:S(2)}) %collective-permute-start.30) | collective-permute-done | bytes 196640 | tf_op jit(solution)/shard_map/ppermute | solution.py:13
  24.1 4.3 %collective-permute-done.29 = bf16[48,2048]{1,0:T(8,128)(2,1)} collective-permute-done((bf16[48,2048]{1,0:T(8,128)(2,1)}, bf16[48,2048]{1,0:T(8,128)(2,1)}, u32[]{:S(2)}, u32[]{:S(2)}) %collective-permute-start.29) | collective-permute-done | bytes 196640 | tf_op jit(solution)/shard_map/ppermute | solution.py:13
  28.4 3.1 fusion.24
  44.3 4.4 %collective-permute-done.22 = bf16[48,2048]{1,0:T(8,128)(2,1)S(1)} collective-permute-done((bf16[48,2048]{1,0:T(8,128)(2,1)S(1)}, bf16[48,2048]{1,0:T(8,128)(2,1)S(1)}, u32[]{:S(2)}, u32[]{:S(2)}) %collective-permute-start.22) | collective-permute-done | bytes 196640 | tf_op jit(solution)/shard_map/ppermute | solution.py:13
  53.5 3.6 collective-permute-done.15
  61.9 3.6 %collective-permute-done.25 = bf16[48,2048]{1,0:T(8,128)(2,1)S(1)} collective-permute-done((bf16[48,2048]{1,0:T(8,128)(2,1)S(1)}, bf16[48,2048]{1,0:T(8,128)(2,1)S(1)}, u32[]{:S(2)}, u32[]{:S(2)}) %collective-permute-start.25) | collective-permute-done | bytes 196640 | tf_op jit(solution)/shard_map/ppermute | solution.py:13
  74.0 4.2 %collective-permute-done.18 = bf16[48,2048]{1,0:T(8,128)(2,1)S(1)} collective-permute-done((bf16[48,2048]{1,0:T(8,128)(2,1)S(1)}, bf16[48,2048]{1,0:T(8,128)(2,1)S(1)}, u32[]{:S(2)}, u32[]{:S(2)}) %collective-permute-start.18) | collective-permute-done | bytes 196640 | tf_op jit(solution)/shard_map/ppermute | solution.py:13
  78.8 3.1 collective-permute-done.9
  81.9 4.5 %collective-permute-done.8 = bf16[48,2048]{1,0:T(8,128)(2,1)S(1)} collective-permute-done((bf16[48,2048]{1,0:T(8,128)(2,1)S(1)}, bf16[48,2048]{1,0:T(8,128)(2,1)S(1)}, u32[]{:S(2)}, u32[]{:S(2)}) %collective-permute-start.8) | collective-permute-done | bytes 196640 | tf_op jit(solution)/shard_map/ppermute | solution.py:13
  92.0 4.1 %collective-permute-done.12 = bf16[48,2048]{1,0:T(8,128)(2,1)S(1)} collective-permute-done((bf16[48,2048]{1,0:T(8,128)(2,1)S(1)}, bf16[48,2048]{1,0:T(8,128)(2,1)S(1)}, u32[]{:S(2)}, u32[]{:S(2)}) %collective-permute-start.12) | collective-permute-done | bytes 196640 | tf_op jit(solution)/shard_map/ppermute | solution.py:13
  105.9 5.1 %collective-permute-done.32 = bf16[48,2048]{1,0:T(8,128)(2,1)S(1)} collective-permute-done((bf16[48,2048]{1,0:T(8,128)(2,1)}, bf16[48,2048]{1,0:T(8,128)(2,1)S(1)}, u32[]{:S(2)}, u32[]{:S(2)}) %collective-permute-start.32) | collective-permute-done | bytes 196640 | tf_op jit(solution)/shard_map/ppermute | solution.py:13
  113.1 31.9 %collective-permute-done.13 = bf16[128,2048]{1,0:T(8,128)(2,1)} collective-permute-done((bf16[128,2048]{1,0:T(8,128)(2,1)}, bf16[128,2048]{1,0:T(8,128)(2,1)}, u32[]{:S(2)}, u32[]{:S(2)}) %collective-permute-start.13) | collective-permute-done | bytes 524320 | tf_op jit(solution)/shard_map/ppermute | solution.py:13
  151.4 3.7 %collective-permute-start.34 = (f32[1,12]{1,0:T(1,128)S(1)}, f32[1,12]{1,0:T(1,128)S(1)}, u32[]{:S(2)}, u32[]{:S(2)}) collective-permute-start(f32[1,12]{1,0:T(1,128)S(1)} %get-tuple-element.75), channel_id=1, source_target_pairs={{0,1},{1,2},{2,3},{3,4},{4,5},{5,6},{6,7},{7,8},{8,9},{9,10},{10,1... | collective-permute-start | bytes 152 | tf_op jit(solution)/shard_map/ppermute | solution.py:19
  163.0 3.3 collective-permute-start.36
  168.4 47.1 %psum.7 = f32[]{:T(128)} all-reduce(f32[]{:T(128)S(6)} %add.184), channel_id=1, replica_groups=mesh['seg'=2,'ep'=16] {'seg','ep'}, use_global_device_ids=true, to_apply=%region_17.18 | all-reduce | flops 1 | bytes 8 | tf_op jit(solution)/shard_map/psum | solution.py:150
  216.3 2.9 multiply_reduce_fusion.5
  234.8 4.4 %collective-permute-done.55 = bf16[48,2048]{1,0:T(8,128)(2,1)S(1)} collective-permute-done((bf16[48,2048]{1,0:T(8,128)(2,1)S(1)}, bf16[48,2048]{1,0:T(8,128)(2,1)S(1)}, u32[]{:S(2)}, u32[]{:S(2)}) %collective-permute-start.55) | collective-permute-done | bytes 196640 | tf_op jit(solution)/shard_map/ppermute | solution.py:13
  266.1 6.2 %collective-permute-done.52 = bf16[48,2048]{1,0:T(8,128)(2,1)S(1)} collective-permute-done((bf16[48,2048]{1,0:T(8,128)(2,1)}, bf16[48,2048]{1,0:T(8,128)(2,1)S(1)}, u32[]{:S(2)}, u32[]{:S(2)}) %collective-permute-start.52) | collective-permute-done | bytes 196640 | tf_op jit(solution)/shard_map/ppermute | solution.py:13
  295.3 4.3 %collective-permute-done.45 = bf16[48,2048]{1,0:T(8,128)(2,1)S(1)} collective-permute-done((bf16[48,2048]{1,0:T(8,128)(2,1)S(1)}, bf16[48,2048]{1,0:T(8,128)(2,1)S(1)}, u32[]{:S(2)}, u32[]{:S(2)}) %collective-permute-start.45) | collective-permute-done | bytes 196640 | tf_op jit(solution)/shard_map/ppermute | solution.py:13
  304.5 3.8 %collective-permute-start.71 = (f32[4,48]{1,0:T(4,128)S(1)}, f32[4,48]{1,0:T(4,128)S(1)}, u32[]{:S(2)}, u32[]{:S(2)}) collective-permute-start(f32[4,48]{1,0:T(4,128)S(1)} %get-tuple-element.83), channel_id=1, source_target_pairs={{0,8},{1,9},{2,10},{3,11},{4,12},{5,13},{6,14},{7,15},{8,0},{9,1},... | collective-permute-start | bytes 2312 | tf_op jit(solution)/shard_map/ppermute | solution.py:13
  315.2 9.4 %collective-permute-done.60 = bf16[128,2048]{1,0:T(8,128)(2,1)S(1)} collective-permute-done((bf16[128,2048]{1,0:T(8,128)(2,1)S(1)}, bf16[128,2048]{1,0:T(8,128)(2,1)S(1)}, u32[]{:S(2)}, u32[]{:S(2)}) %collective-permute-start.60) | collective-permute-done | bytes 524320 | tf_op jit(solution)/shard_map/ppermute | solution.py:13
  324.5 11.9 %collective-permute-done.53 = bf16[128,2048]{1,0:T(8,128)(2,1)S(1)} collective-permute-done((bf16[128,2048]{1,0:T(8,128)(2,1)S(1)}, bf16[128,2048]{1,0:T(8,128)(2,1)S(1)}, u32[]{:S(2)}, u32[]{:S(2)}) %collective-permute-start.53) | collective-permute-done | bytes 524320 | tf_op jit(solution)/shard_map/ppermute | solution.py:13
  336.4 20.8 %collective-permute-done.46 = bf16[128,2048]{1,0:T(8,128)(2,1)S(1)} collective-permute-done((bf16[128,2048]{1,0:T(8,128)(2,1)S(1)}, bf16[128,2048]{1,0:T(8,128)(2,1)S(1)}, u32[]{:S(2)}, u32[]{:S(2)}) %collective-permute-start.46) | collective-permute-done | bytes 524320 | tf_op jit(solution)/shard_map/ppermute | solution.py:13
  (339 shorter events, 158.4 us)
Async XLA Ops:
  7.9 27.6 %collective-permute-start.3 = (bf16[128,2048]{1,0:T(8,128)(2,1)}, bf16[128,2048]{1,0:T(8,128)(2,1)}, u32[]{:S(2)}, u32[]{:S(2)}) collective-permute-start(bf16[128,2048]{1,0:T(8,128)(2,1)} %param.10), channel_id=1, source_target_pairs={{0,4},{1,5},{2,6},{3,7},{4,0},{5,1},{6,2},{7,3},{8,12},{9,13},{10,... | collective-permute-start | bytes 1572872 | tf_op jit(solution)/shard_map/ppermute | solution.py:13
  9.7 29.2 %collective-permute-start.5 = (bf16[128,2048]{1,0:T(8,128)(2,1)}, bf16[128,2048]{1,0:T(8,128)(2,1)}, u32[]{:S(2)}, u32[]{:S(2)}) collective-permute-start(bf16[128,2048]{1,0:T(8,128)(2,1)} %param.10), channel_id=1, source_target_pairs={{0,12},{1,13},{2,14},{3,15},{4,8},{5,9},{6,10},{7,11},{8,4},{9,5},... | collective-permute-start | bytes 1572872 | tf_op jit(solution)/shard_map/ppermute | solution.py:13
  41.0 16.1 %collective-permute-start.15 = (bf16[48,2048]{1,0:T(8,128)(2,1)S(1)}, bf16[48,2048]{1,0:T(8,128)(2,1)S(1)}, u32[]{:S(2)}, u32[]{:S(2)}) collective-permute-start(bf16[48,2048]{1,0:T(8,128)(2,1)S(1)} %get-tuple-element.59), channel_id=1, source_target_pairs={{0,2},{1,3},{2,0},{3,1},{4,6},{5,7},{6,4},{7,5},{8,10},{9,11},{10,... | collective-permute-start | bytes 589832 | tf_op jit(solution)/shard_map/ppermute | solution.py:13
  48.7 19.7 %collective-permute-start.4 = (bf16[128,2048]{1,0:T(8,128)(2,1)}, bf16[128,2048]{1,0:T(8,128)(2,1)S(1)}, u32[]{:S(2)}, u32[]{:S(2)}) collective-permute-start(bf16[128,2048]{1,0:T(8,128)(2,1)} %collective-permute-done.3), channel_id=1, source_target_pairs={{4,8},{5,9},{6,10},{7,11},{8,4},{9,5},{10,6},{11,7},{20,24},{21,25... | collective-permute-start | bytes 1572872 | tf_op jit(solution)/shard_map/ppermute | solution.py:92
  49.4 19.7 %collective-permute-start.6 = (bf16[128,2048]{1,0:T(8,128)(2,1)}, bf16[128,2048]{1,0:T(8,128)(2,1)S(1)}, u32[]{:S(2)}, u32[]{:S(2)}) collective-permute-start(bf16[128,2048]{1,0:T(8,128)(2,1)} %collective-permute-done.5), channel_id=1, source_target_pairs={{4,0},{5,1},{6,2},{7,3},{8,12},{9,13},{10,14},{11,15},{20,16},{21,... | collective-permute-start | bytes 1572872 | tf_op jit(solution)/shard_map/ppermute | solution.py:93
  60.8 45.0 %collective-permute-start.33 = (bf16[48,2048]{1,0:T(8,128)(2,1)}, bf16[48,2048]{1,0:T(8,128)(2,1)}, u32[]{:S(2)}, u32[]{:S(2)}) collective-permute-start(bf16[48,2048]{1,0:T(8,128)(2,1)} %get-tuple-element.38), channel_id=1, source_target_pairs={{0,3},{1,2},{2,1},{3,0},{4,7},{5,6},{6,5},{7,4},{8,11},{9,10},{10,... | collective-permute-start | bytes 589832 | tf_op jit(solution)/shard_map/ppermute | solution.py:13
  69.1 43.3 %collective-permute-start.27 = (bf16[128,2048]{1,0:T(8,128)(2,1)}, bf16[128,2048]{1,0:T(8,128)(2,1)}, u32[]{:S(2)}, u32[]{:S(2)}) collective-permute-start(bf16[128,2048]{1,0:T(8,128)(2,1)} %fusion.90), channel_id=1, source_target_pairs={{0,4},{1,5},{2,6},{3,7},{4,0},{5,1},{6,2},{7,3},{8,12},{9,13},{10,... | collective-permute-start | bytes 1572872 | tf_op jit(solution)/shard_map/ppermute | solution.py:13
  96.2 17.0 %collective-permute-start.20 = (bf16[128,2048]{1,0:T(8,128)(2,1)}, bf16[128,2048]{1,0:T(8,128)(2,1)}, u32[]{:S(2)}, u32[]{:S(2)}) collective-permute-start(bf16[128,2048]{1,0:T(8,128)(2,1)} %fusion.89), channel_id=1, source_target_pairs={{0,12},{1,13},{2,14},{3,15},{4,8},{5,9},{6,10},{7,11},{8,4},{9,5},... | collective-permute-start | bytes 1572872 | tf_op jit(solution)/shard_map/ppermute | solution.py:13
  102.1 42.9 %collective-permute-start.13 = (bf16[128,2048]{1,0:T(8,128)(2,1)}, bf16[128,2048]{1,0:T(8,128)(2,1)}, u32[]{:S(2)}, u32[]{:S(2)}) collective-permute-start(bf16[128,2048]{1,0:T(8,128)(2,1)} %fusion.88), channel_id=1, source_target_pairs={{0,8},{1,9},{2,10},{3,11},{4,12},{5,13},{6,14},{7,15},{8,0},{9,1},... | collective-permute-start | bytes 1572872 | tf_op jit(solution)/shard_map/ppermute | solution.py:13
  160.4 55.8 %collective-permute-start.63 = (bf16[48,2048]{1,0:T(8,128)(2,1)}, bf16[48,2048]{1,0:T(8,128)(2,1)}, u32[]{:S(2)}, u32[]{:S(2)}) collective-permute-start(bf16[48,2048]{1,0:T(8,128)(2,1)} %get-tuple-element.10), channel_id=1, source_target_pairs={{0,3},{1,2},{2,1},{3,0},{4,7},{5,6},{6,5},{7,4},{8,11},{9,10},{10,... | collective-permute-start | bytes 589832 | tf_op jit(solution)/shard_map/ppermute | solution.py:13
  162.6 53.6 %collective-permute-start.62 = (bf16[48,2048]{1,0:T(8,128)(2,1)}, bf16[48,2048]{1,0:T(8,128)(2,1)}, u32[]{:S(2)}, u32[]{:S(2)}) collective-permute-start(bf16[48,2048]{1,0:T(8,128)(2,1)} %get-tuple-element.11), channel_id=1, source_target_pairs={{0,2},{1,3},{2,0},{3,1},{4,6},{5,7},{6,4},{7,5},{8,10},{9,11},{10,... | collective-permute-start | bytes 589832 | tf_op jit(solution)/shard_map/ppermute | solution.py:13
  162.8 53.5 %collective-permute-start.61 = (bf16[48,2048]{1,0:T(8,128)(2,1)}, bf16[48,2048]{1,0:T(8,128)(2,1)}, u32[]{:S(2)}, u32[]{:S(2)}) collective-permute-start(bf16[48,2048]{1,0:T(8,128)(2,1)} %get-tuple-element.12), channel_id=1, source_target_pairs={{0,1},{1,0},{2,3},{3,2},{4,5},{5,4},{6,7},{7,6},{8,9},{9,8},{10,11... | collective-permute-start | bytes 589832 | tf_op jit(solution)/shard_map/ppermute | solution.py:13
  163.0 62.4 %collective-permute-start.36 = (bf16[128,2048]{1,0:T(8,128)(2,1)}, bf16[128,2048]{1,0:T(8,128)(2,1)}, u32[]{:S(2)}, u32[]{:S(2)}) collective-permute-start(bf16[128,2048]{1,0:T(8,128)(2,1)} %fusion.244), channel_id=1, source_target_pairs={{0,4},{1,5},{2,6},{3,7},{4,0},{5,1},{6,2},{7,3},{8,12},{9,13},{10,... | collective-permute-start | bytes 1572872 | tf_op jit(solution)/shard_map/ppermute | solution.py:13
  167.6 61.8 %collective-permute-start.38 = (bf16[128,2048]{1,0:T(8,128)(2,1)}, bf16[128,2048]{1,0:T(8,128)(2,1)}, u32[]{:S(2)}, u32[]{:S(2)}) collective-permute-start(bf16[128,2048]{1,0:T(8,128)(2,1)} %fusion.244), channel_id=1, source_target_pairs={{0,12},{1,13},{2,14},{3,15},{4,8},{5,9},{6,10},{7,11},{8,4},{9,5},... | collective-permute-start | bytes 1572872 | tf_op jit(solution)/shard_map/ppermute | solution.py:13
  230.8 17.2 %collective-permute-start.49 = (bf16[48,2048]{1,0:T(8,128)(2,1)S(1)}, bf16[48,2048]{1,0:T(8,128)(2,1)S(1)}, u32[]{:S(2)}, u32[]{:S(2)}) collective-permute-start(bf16[48,2048]{1,0:T(8,128)(2,1)S(1)} %get-tuple-element.26), channel_id=1, source_target_pairs={{0,3},{1,2},{2,1},{3,0},{4,7},{5,6},{6,5},{7,4},{8,11},{9,10},{10,... | collective-permute-start | bytes 589832 | tf_op jit(solution)/shard_map/ppermute | solution.py:13
  232.2 16.7 %collective-permute-start.48 = (bf16[48,2048]{1,0:T(8,128)(2,1)S(1)}, bf16[48,2048]{1,0:T(8,128)(2,1)S(1)}, u32[]{:S(2)}, u32[]{:S(2)}) collective-permute-start(bf16[48,2048]{1,0:T(8,128)(2,1)S(1)} %get-tuple-element.27), channel_id=1, source_target_pairs={{0,2},{1,3},{2,0},{3,1},{4,6},{5,7},{6,4},{7,5},{8,10},{9,11},{10,... | collective-permute-start | bytes 589832 | tf_op jit(solution)/shard_map/ppermute | solution.py:13
  233.3 15.6 %collective-permute-start.47 = (bf16[48,2048]{1,0:T(8,128)(2,1)S(1)}, bf16[48,2048]{1,0:T(8,128)(2,1)S(1)}, u32[]{:S(2)}, u32[]{:S(2)}) collective-permute-start(bf16[48,2048]{1,0:T(8,128)(2,1)S(1)} %get-tuple-element.28), channel_id=1, source_target_pairs={{0,1},{1,0},{2,3},{3,2},{4,5},{5,4},{6,7},{7,6},{8,9},{9,8},{10,11... | collective-permute-start | bytes 589832 | tf_op jit(solution)/shard_map/ppermute | solution.py:13
  239.2 24.1 %collective-permute-start.37 = (bf16[128,2048]{1,0:T(8,128)(2,1)}, bf16[128,2048]{1,0:T(8,128)(2,1)}, u32[]{:S(2)}, u32[]{:S(2)}) collective-permute-start(bf16[128,2048]{1,0:T(8,128)(2,1)} %collective-permute-done.36), channel_id=1, source_target_pairs={{4,8},{5,9},{6,10},{7,11},{8,4},{9,5},{10,6},{11,7},{20,24},{21,25... | collective-permute-start | bytes 1572872 | tf_op jit(solution)/shard_map/ppermute | solution.py:92
  240.7 22.9 %collective-permute-start.39 = (bf16[128,2048]{1,0:T(8,128)(2,1)}, bf16[128,2048]{1,0:T(8,128)(2,1)}, u32[]{:S(2)}, u32[]{:S(2)}) collective-permute-start(bf16[128,2048]{1,0:T(8,128)(2,1)} %collective-permute-done.38), channel_id=1, source_target_pairs={{4,0},{5,1},{6,2},{7,3},{8,12},{9,13},{10,14},{11,15},{20,16},{21,... | collective-permute-start | bytes 1572872 | tf_op jit(solution)/shard_map/ppermute | solution.py:93
  255.5 58.1 %collective-permute-start.66 = (bf16[48,2048]{1,0:T(8,128)(2,1)}, bf16[48,2048]{1,0:T(8,128)(2,1)}, u32[]{:S(2)}, u32[]{:S(2)}) collective-permute-start(bf16[48,2048]{1,0:T(8,128)(2,1)} %get-tuple-element.6), channel_id=1, source_target_pairs={{0,3},{1,2},{2,1},{3,0},{4,7},{5,6},{6,5},{7,4},{8,11},{9,10},{10,... | collective-permute-start | bytes 589832 | tf_op jit(solution)/shard_map/ppermute | solution.py:13
  258.3 56.0 %collective-permute-start.65 = (bf16[48,2048]{1,0:T(8,128)(2,1)}, bf16[48,2048]{1,0:T(8,128)(2,1)}, u32[]{:S(2)}, u32[]{:S(2)}) collective-permute-start(bf16[48,2048]{1,0:T(8,128)(2,1)} %get-tuple-element.7), channel_id=1, source_target_pairs={{0,2},{1,3},{2,0},{3,1},{4,6},{5,7},{6,4},{7,5},{8,10},{9,11},{10,... | collective-permute-start | bytes 589832 | tf_op jit(solution)/shard_map/ppermute | solution.py:13
  308.6 15.9 %collective-permute-start.60 = (bf16[128,2048]{1,0:T(8,128)(2,1)S(1)}, bf16[128,2048]{1,0:T(8,128)(2,1)S(1)}, u32[]{:S(2)}, u32[]{:S(2)}) collective-permute-start(bf16[128,2048]{1,0:T(8,128)(2,1)S(1)} %copy-done.44), channel_id=1, source_target_pairs={{0,4},{1,5},{2,6},{3,7},{4,0},{5,1},{6,2},{7,3},{8,12},{9,13},{10,... | collective-permute-start | bytes 1572872 | tf_op jit(solution)/shard_map/ppermute | solution.py:13
  310.7 25.7 %collective-permute-start.53 = (bf16[128,2048]{1,0:T(8,128)(2,1)S(1)}, bf16[128,2048]{1,0:T(8,128)(2,1)S(1)}, u32[]{:S(2)}, u32[]{:S(2)}) collective-permute-start(bf16[128,2048]{1,0:T(8,128)(2,1)S(1)} %copy-done.45), channel_id=1, source_target_pairs={{0,12},{1,13},{2,14},{3,15},{4,8},{5,9},{6,10},{7,11},{8,4},{9,5},... | collective-permute-start | bytes 1572872 | tf_op jit(solution)/shard_map/ppermute | solution.py:13
  312.2 45.0 %collective-permute-start.46 = (bf16[128,2048]{1,0:T(8,128)(2,1)S(1)}, bf16[128,2048]{1,0:T(8,128)(2,1)S(1)}, u32[]{:S(2)}, u32[]{:S(2)}) collective-permute-start(bf16[128,2048]{1,0:T(8,128)(2,1)S(1)} %convolution_convert_fusion.6), channel_id=1, source_target_pairs={{0,8},{1,9},{2,10},{3,11},{4,12},{5,13},{6,14},{7,15},{8,0},{9,1},... | collective-permute-start | bytes 1572872 | tf_op jit(solution)/shard_map/ppermute | solution.py:13
  (95 other events, 1006.7 us)

commit v2 on v1

v2 whole, which is shorter than its diff:
```python
import functools

import jax
import jax.numpy as jnp
from jax import lax
from jax.experimental import pallas as pl
from jax.experimental.pallas import tpu as pltpu
from jax.sharding import PartitionSpec as P

forward_plan = (
    "G", "c0", "t0", "c1", "r3", "c2", "t1", "e0", "e1", "t2", "e2", "b2",
    "c3", "t3", "e3", "b3", "g2", "l2", "b1", "g3", "s3", "b0", "g1", "s1",
    "g0",
)
backward_plan = (
    "G", "c0", "t0", "c1", "r3", "c2", "t1", "e0", "t2", "e2", "b2", "c3",
    "e1", "t3", "e3", "b3", "g2", "l2", "b1", "g3", "s3", "b0", "g1", "s1",
    "g0",
)
epsilon = 1e-06
foot_weight = 2.0
both = ("seg", "ep")


def swap(block, distance):
    route = [(i, i ^ distance) for i in range(lax.axis_size("ep"))]
    return lax.ppermute(block, "ep", route)


def from_behind(block, axis, distance):
    devices = range(lax.axis_size(axis))
    route = [(i - distance, i) for i in devices if i - distance in devices]
    return lax.ppermute(block, axis, route)


def after(value, *earlier):
    return lax.optimization_barrier((value,) + earlier)[0]


def dot(a, b, dims):
    return lax.dot_general(a, b, (dims, ((), ())), preferred_element_type=jnp.float32)


def split_levels(ep_count):
    level = 1
    while 4 * level * level <= ep_count:
        level *= 2
    return level, ep_count // level


def no_cost():
    return pl.CostEstimate(flops=0, bytes_accessed=0, transcendentals=0)


def kernel_call(body, out_shape, *operands, scalars=()):
    return pl.pallas_call(
        body,
        out_shape=out_shape,
        in_specs=[pl.BlockSpec(memory_space=pltpu.SMEM)] * len(scalars)
        + [pl.BlockSpec(memory_space=pltpu.VMEM)] * len(operands),
        out_specs=jax.tree.map(lambda _: pl.BlockSpec(memory_space=pltpu.VMEM), out_shape),
        cost_estimate=no_cost(),
        compiler_params=pltpu.CompilerParams(vmem_limit_bytes=8 * 1024 * 1024),
    )(*scalars, *operands)


def shape(dims, dtype):
    return jax.ShapeDtypeStruct(dims, dtype)


def payload_body(ids_ref, gates_ref, rows_ref, out_ref):
    top, frames = ids_ref.shape
    width = rows_ref.shape[1]
    line = lax.broadcasted_iota(jnp.int32, (128, frames), 0)
    values, rest = [ids_ref[...].astype(jnp.float32)], gates_ref[...]
    for _ in range(3):
        values.append(rest.astype(jnp.bfloat16).astype(jnp.float32))
        rest = rest - values[-1]
    routing = jnp.zeros((128, frames), jnp.float32)
    for i, value in enumerate(values):
        for t in range(top):
            routing = jnp.where(line == 8 * i + t, value[t : t + 1], routing)
    out_ref[:, width:] = routing.T.astype(jnp.bfloat16)
    out_ref[:, :width] = rows_ref[...]


def exact_dot(a, b):
    return jnp.dot(a, b, preferred_element_type=jnp.float32)


def joined(refs):
    return refs[0][...] if len(refs) == 1 else refs[0][...] + refs[1][...]


def table_body(top, pieces, first_ref, mine_ref, *refs):
    block = joined(refs[:pieces])
    table_ref, *parts = refs[pieces:]
    peers, capacity, frames = table_ref.shape
    width = parts[0].shape[1]
    routing = block[:, width:].astype(jnp.float32).T
    top_rows = lax.broadcasted_iota(jnp.int32, (8, frames), 0)
    ids = routing[:8]
    gates = routing[8:16] + routing[16:24] + routing[24:32]
    line = lax.broadcasted_iota(jnp.int32, (128, frames), 0)
    lane = lax.broadcasted_iota(jnp.int32, (128, frames), 1)
    member = jnp.zeros((128, frames), jnp.float32)
    gate_of = []
    for j in range(peers):
        expert = first_ref[0] + (mine_ref[0] ^ j)
        hit = jnp.logical_and(ids == expert.astype(jnp.float32), top_rows < top)
        member = jnp.where(line == j, jnp.sum(hit.astype(jnp.float32), 0, keepdims=True), member)
        gate_of.append(jnp.sum(jnp.where(hit, gates, 0.0), 0, keepdims=True))
    before = (line < lane).astype(jnp.bfloat16)
    rank = exact_dot(member.astype(jnp.bfloat16), before)
    rank = jnp.where(member > 0.0, rank, -1.0)
    slot = lax.broadcasted_iota(jnp.int32, (capacity, frames), 0).astype(jnp.float32)
    picks = []
    for j in range(peers):
        chosen = rank[j : j + 1] == slot
        table_ref[j] = jnp.where(chosen, gate_of[j], 0.0)
        picks.append(chosen.astype(jnp.float32).astype(jnp.bfloat16))
    choose_parts(picks, block[:, :width], None, parts)


def choose_parts(picks, rows, gates, parts):
    capacity = picks[0].shape[0]
    if capacity % 16 == 0:
        chosen = exact_dot(jnp.concatenate(picks, 0), rows)
        chosen = [chosen[j * capacity : (j + 1) * capacity] for j in range(len(parts))]
    else:
        chosen = [exact_dot(pick, rows) for pick in picks]
    for j, part in enumerate(parts):
        value = chosen[j] if gates is None else chosen[j] * gates[j]
        part[...] = value.astype(part.dtype)


def as_pick(weight):
    return jnp.where(weight != 0.0, 1.0, 0.0)


def choose_body(pieces, table_ref, *refs):
    block, parts = joined(refs[:pieces]), refs[pieces:]
    tables = [table_ref[j] for j in range(len(parts))]
    picks = [as_pick(table).astype(jnp.bfloat16) for table in tables]
    gates = [jnp.sum(table, 1, keepdims=True) for table in tables]
    choose_parts(picks, block[:, : parts[0].shape[1]], gates, parts)


def put_pieces(block, value, place):
    lane = lax.broadcasted_iota(jnp.int32, block.shape, 1)
    for i in range(3):
        piece = value.astype(jnp.bfloat16).astype(jnp.float32)
        block = jnp.where(lane == place + i, piece, block)
        value = value - piece
    return block


def tree_sum(values):
    while len(values) > 1:
        values = [values[i] + values[i + 1] for i in range(0, len(values), 2)]
    return values[0]


def collect_parts(gated, table_ref, parts):
    total = None
    for j, part in enumerate(parts):
        table = table_ref[j]
        if gated:
            high = table.astype(jnp.bfloat16).astype(jnp.float32)
            sides = [high, table - high]
        else:
            sides = [as_pick(table)]
        for side in sides:
            term = exact_dot(side.T.astype(jnp.bfloat16), part[...])
            total = term if total is None else total + term
    return total


def collect_body(peers, lent, table_ref, *refs):
    out_ref = refs[-1]
    total = collect_parts(True, table_ref, refs[:peers])
    if lent:
        total = total + refs[peers][...].astype(jnp.float32)
    out_ref[...] = total.astype(out_ref.dtype)


def collect_back_body(width, place, peers, lent, first, layer_ref, table_ref, *refs):
    parts = refs[:peers]
    out_ref = refs[-2] if first else refs[-1]
    total = collect_parts(False, table_ref, parts)
    extra = out_ref.shape[1] - width
    if first:
        lane = lax.broadcasted_iota(jnp.int32, (8, extra), 1)
        inside = jnp.logical_and(lane >= place, lane < place + 3)
        losses = [
            jnp.sum(jnp.where(inside, part[0:8, width:].astype(jnp.float32), 0.0), 1, keepdims=True)
            for part in parts
        ]
        loss = tree_sum(losses)
        refs[-1][...] = jnp.broadcast_to(loss, refs[-1].shape)
        loss = loss[0:1]
    else:
        loss = refs[peers][0:1, 0:1]
    behind = put_pieces(total[:, width:], loss, place + 4 + 3 * layer_ref[0])
    total = total[:, :width]
    if lent:
        total = total + refs[peers + 1][:, :width].astype(jnp.float32)
        behind = behind + refs[peers + 1][:, width:].astype(jnp.float32)
    out_ref[:, :width] = total.astype(out_ref.dtype)
    out_ref[:, width:] = behind.astype(out_ref.dtype)


def per_device(
    frames_in,
    expert_ids,
    gate_values,
    gate_weight,
    up_weight,
    down_weight,
    norm_gain,
    pose_weight,
    target_pose,
    foot_contact,
):
    tok_rows, width = frames_in.shape
    top = expert_ids.shape[1]
    ep_count = lax.axis_size("ep")
    experts = ep_count
    capacity = tok_rows * top // experts
    layers, peers = split_levels(ep_count)
    me = lax.axis_index("ep")
    my_layer, my_peer = me // peers, me % peers
    gate_w, up_w, down_w = gate_weight[0], up_weight[0], down_weight[0]

    frames_out = kernel_call(
        payload_body,
        shape((tok_rows, width + 128), jnp.bfloat16),
        expert_ids.T,
        gate_values.T,
        frames_in,
    )
    first_expert = (my_layer * peers).astype(jnp.int32).reshape(1)
    mine = my_peer.astype(jnp.int32).reshape(1)
    table_shape = (shape((peers, capacity, tok_rows), jnp.float32),)
    part_shape = tuple([shape((capacity, width), jnp.bfloat16)] * peers)
    tables = {}

    inner = [i for i in range(ep_count) if i // peers in (1, 2)]

    def across(block):
        return lax.ppermute(block, "ep", [(i, i ^ (3 * peers)) for i in inner])

    def outward(block):
        return lax.ppermute(block, "ep", [(i, i ^ peers) for i in inner])

    def exchange(parts):
        return [parts[0]] + [swap(parts[j], j) for j in range(1, peers)]

    def rounds(plan, rows, choose, expert, collect):
        scheme, plan = plan
        held = {0: [rows]}
        for k in {"I": [1], "F": [1, 3], "G": [1, 2]}.get(scheme, range(1, layers)):
            held[k] = [swap(rows, k * peers)]
        if scheme == "I":
            held[3] = [across(rows)]
        arrived, results, parts, lent = {}, {}, {}, {}

        def do_choose(k, last):
            sent = choose(k, [after(held[k][0], *last)] + held[k][1:])
            arrived[k] = exchange(sent)
            return (sent[0],)

        def do_expert(k, last):
            rows = arrived[k]
            results[k] = expert(k, [after(rows[0], *last)] + rows[1:])
            return (results[k][0],)

        def do_back(k, last):
            rows = lax.optimization_barrier(tuple(results[k]) + last)
            results[k] = exchange(list(rows[:peers]))
            return last

        def do_relay(k, last):
            if scheme in "FG":
                held[k ^ 1] = [after(held[k ^ 1][0], *last)]
                held[k] = [swap(held[k ^ 1][0], peers)]
                return last
            if k == 2:
                first, cross = after(held[1][0], *last), after(held[3][0], *last)
                held[1], held[3] = [first], [cross]
                held[2] = [outward(cross), across(first)]
                return (first, cross)
            held[2][1] = after(held[2][1], *last)
            held[3].append(outward(held[2][1]))
            return (held[2][1],)

        def do_touch(k, last):
            return last + tuple(arrived[k])

        def do_collect(k, last):
            extra_part = [lent[k]] if k in lent else []
            rows = [after(results[k][0], *last)] + results[k][1:]
            parts[k] = collect(k, rows, extra_part)
            return (parts[k],)

        def do_lend(k, last):
            lent[k ^ 1] = swap(after(parts[k], *last), peers)
            parts[k] = None
            return last

        def do_send(k, last):
            part = after(parts[k], *last)
            parts[k] = swap(part, k * peers)
            return (part,)

        steps = {
            "c": do_choose,
            "e": do_expert,
            "b": do_back,
            "g": do_collect,
            "l": do_lend,
            "r": do_relay,
            "t": do_touch,
            "s": do_send,
        }
        last = ()
        for step, k in plan:
            last = steps[step](k, last)
        return [parts[k] for k in range(layers) if parts[k] is not None]

    def read_plan(written):
        if layers == 4:
            scheme, *words = written
            return scheme, [(word[0], int(word[1])) for word in words]
        steps = []
        for k in range(layers):
            steps += [("c", k)] + ([("e", k - 1), ("b", k - 1)] if k else [])
        steps += [("e", layers - 1), ("b", layers - 1), ("g", 0)]
        for k in range(1, layers):
            steps += [("g", k), ("s", k)]
        return "D", steps

    kept = {}

    def split(rows):
        return [rows[i : i + capacity] for i in range(0, rows.shape[0], capacity)]

    def choose_in(k, blocks):
        tables[k], *sent = kernel_call(
            functools.partial(table_body, top, len(blocks)),
            table_shape + part_shape,
            *blocks,
            scalars=(first_expert, mine),
        )
        return sent

    def expert_in(k, parts):
        rows = jnp.concatenate(parts, 0)
        kept[k] = (dot(rows, gate_w, ((1,), (0,))), dot(rows, up_w, ((1,), (0,))))
        gate_pre, up_pre = kept[k]
        hidden = (gate_pre * jax.nn.sigmoid(gate_pre) * up_pre).astype(jnp.bfloat16)
        return split(dot(hidden, down_w, ((1,), (0,))).astype(jnp.bfloat16))

    def sum_type(k):
        return jnp.bfloat16 if k else jnp.float32

    def collect_in(k, returned, lent):
        return kernel_call(
            functools.partial(collect_body, peers, len(lent)),
            shape((tok_rows, width), sum_type(k)),
            tables[k],
            *returned,
            *lent,
        )

    mixed_parts = rounds(read_plan(forward_plan), frames_out, choose_in, expert_in, collect_in)

    mixed_rows = sum(part.astype(jnp.float32) for part in mixed_parts)
    state_rows = frames_in.astype(jnp.float32) + mixed_rows
    inverse_rms = lax.rsqrt(jnp.mean(state_rows * state_rows, axis=1, keepdims=True) + epsilon)
    unit_rows = state_rows * inverse_rms
    normed = (unit_rows * norm_gain).astype(jnp.bfloat16)
    pose_out = dot(normed, pose_weight, ((1,), (0,)))
    pose_cols = pose_out.shape[1]
    device = lax.axis_index("seg") * ep_count + me
    frames_all = lax.axis_size("seg") * ep_count * tok_rows
    frame_index = device * tok_rows + jnp.arange(tok_rows, dtype=jnp.int32)
    horizon = 0.5 + frame_index.astype(jnp.float32) / (frames_all - 1)
    feet = foot_contact.shape[1]
    foot_cols = 3 * feet
    foot_pos = pose_out[:, :foot_cols]
    contact = jnp.repeat(foot_contact.astype(jnp.float32), 3, axis=1)
    with jax.named_scope("feet"):
        before = from_behind(foot_pos[tok_rows - 1 :], both, 1)
        after_row = from_behind(jnp.concatenate([foot_pos[:1], contact[:1]], 1), both, -1)
    before, after_row = lax.optimization_barrier((before, after_row))
    earlier = jnp.concatenate([before, foot_pos[:-1]], 0)
    velocity = jnp.where((frame_index > 0)[:, None], foot_pos - earlier, 0.0)
    foot_pull = foot_weight * horizon[:, None] * contact * velocity
    next_horizon = 0.5 + (device * tok_rows + tok_rows).astype(jnp.float32) / (frames_all - 1)
    next_velocity = after_row[:, :foot_cols] - foot_pos[tok_rows - 1 :]
    next_pull = foot_weight * next_horizon * after_row[:, foot_cols:] * next_velocity
    pose_error = pose_out - target_pose
    local_sum = 0.5 * jnp.sum(horizon[:, None] * pose_error * pose_error) + 0.5 * jnp.sum(
        foot_pull * velocity
    )
    later_pull = jnp.concatenate([foot_pull[1:], next_pull], 0)
    grad_pose = horizon[:, None] * pose_error
    grad_pose = jnp.concatenate(
        [grad_pose[:, :foot_cols] + (foot_pull - later_pull), grad_pose[:, foot_cols:]], 1
    )
    grad_normed = dot(grad_pose.astype(jnp.bfloat16), pose_weight, ((1,), (1,)))
    scaled = grad_normed * norm_gain
    grad_state = inverse_rms * (
        scaled - unit_rows * jnp.mean(scaled * unit_rows, axis=1, keepdims=True)
    )
    moe_grad = grad_state.astype(jnp.bfloat16)

    place = 3 * experts
    extra = -(-(place + 4 + 3 * layers) // 128) * 128
    loss_stage = [k for step, k in read_plan(backward_plan)[1] if step == "g"][0]
    seg_count = lax.axis_size("seg")
    layer_loss = []
    routes = [[(i, i ^ n) for i in range(seg_count)] for n in range(1, seg_count)]
    seg_loss = tree_sum([local_sum] + [lax.ppermute(local_sum, "seg", way) for way in routes])

    def choose_back(k, blocks):
        if k == 1:
            blocks = [after(blocks[0], seg_loss)] + blocks[1:]
        body = functools.partial(choose_body, len(blocks))
        return kernel_call(body, part_shape, tables[k], *blocks)

    def expert_back(k, parts):
        loss = seg_loss if k == loss_stage else jnp.zeros((), jnp.float32)
        gate_pre, up_pre = kept[k]
        grad_hidden = dot(jnp.concatenate(parts, 0), down_w, ((1,), (1,)))
        sig = jax.nn.sigmoid(gate_pre)
        activated = gate_pre * sig
        slope = sig * (1.0 + gate_pre * (1.0 - sig))
        dots = jnp.sum(grad_hidden * (activated * up_pre), axis=1, keepdims=True)
        grad_gate_pre = (grad_hidden * up_pre * slope).astype(jnp.bfloat16)
        grad_up_pre = (grad_hidden * activated).astype(jnp.bfloat16)
        grad_rows = dot(grad_gate_pre, gate_w, ((1,), (1,)))
        grad_rows = grad_rows + dot(grad_up_pre, up_w, ((1,), (1,)))
        behind = jnp.zeros((grad_rows.shape[0], extra), jnp.float32)
        column = jnp.arange(extra, dtype=jnp.int32)[None]
        for start, rest in ((3 * me, dots), (place, jnp.broadcast_to(loss, dots.shape))):
            for i in range(3):
                piece = lax.reduce_precision(rest, 8, 7)
                behind = jnp.where(column == start + i, piece, behind)
                rest = rest - piece
        return split(jnp.concatenate([grad_rows, behind], 1).astype(jnp.bfloat16))

    def collect_back(k, returned, lent):
        first = k == loss_stage
        body = functools.partial(collect_back_body, width, place, peers, len(lent), first)
        total = shape((tok_rows, width + extra), sum_type(k))
        scalars = (my_layer.astype(jnp.int32).reshape(1),)
        if first:
            outs = (total, shape((8, 128), jnp.float32))
            total, loss = kernel_call(body, outs, tables[k], *returned, scalars=scalars)
            layer_loss.append(loss)
            return total
        operands = (tables[k], *returned, layer_loss[0], *lent)
        return kernel_call(body, total, *operands, scalars=scalars)

    returned_parts = rounds(read_plan(backward_plan), moe_grad, choose_back, expert_back, collect_back)
    summed_back = sum(part.astype(jnp.float32) for part in returned_parts)
    grad_input = (grad_state + summed_back[:, :width]).astype(jnp.bfloat16)
    dots = summed_back[:, width : width + 3 * experts].reshape(tok_rows, experts, 3)
    dots = dots[:, :, 0] + dots[:, :, 1] + dots[:, :, 2]
    chosen = expert_ids[:, :, None] == jnp.arange(experts, dtype=jnp.int32)
    grad_gates = jnp.sum(jnp.where(chosen, dots[:, None], 0.0), axis=2) / gate_values
    losses = summed_back[0, width + place + 4 : width + place + 4 + 3 * layers]
    loss_sum = tree_sum([losses[3 * i] + losses[3 * i + 1] + losses[3 * i + 2] for i in range(layers)])
    loss_value = loss_sum / (frames_all * pose_cols)
    return (grad_input, grad_gates, loss_value)


def solution(mesh):
    rows = P(both, None)
    expert = P("ep", None, None)
    in_specs = (rows, rows, rows, expert, expert, expert, P(), P(), rows, rows)
    return jax.shard_map(
        per_device, mesh=mesh, in_specs=in_specs, out_specs=(rows, rows, P()), check_vma=False
    )
```

time: 362 us -> 279 us (0.77)
  blocking collectives: 47.1 us -> 0 us
  matrix products: 58.2 us -> 29.1 us
  waiting for transfers between devices: 154 us -> 127 us
  Pallas kernels: 0 us -> 22.6 us
  starting transfers between devices: 75.5 us -> 63.2 us
  between operations: 4.86 us -> 15.4 us
    psum x1 -> x0, blocking collectives: 47.1 us -> none  [per_device(): loss_value = lax.psum(local_sum, both) / (frames_all * pose_cols)]
    dot_general x49 -> x26, matrix products: 58.2 us -> 29.1 us  [dot(): lax.dot_general(a, b, (dims, ((), ())), preferred_element_type=jnp.float32)]
    ppermute x67 -> x60, waiting for transfers between devices: 152 us -> 126 us  [swap(): return lax.ppermute(block, 'ep', route)]
    pallas_call x0 -> x17, Pallas kernels: none -> 22.6 us  [kernel_call(): pl.pallas_call(body, out_shape=out_shape, in_specs=[pl.BlockSpec(memory_s...]
    ppermute x67 -> x60, starting transfers between devices: 65.4 us -> 53.9 us  [swap(): return lax.ppermute(block, 'ep', route)]
    slice x21 -> x7, local copies, waits for them, and re-layouts: 8.98 us -> 1.91 us  [the longest x4 1.15 us: split(): return [rows[i:i + capacity] for i in range(0, rows.shape[0], capacity)]]
  transfers between devices with their start and end apart: 73 -> 63, of which waited for: 32 -> 34; matrix products, arithmetic and copies ran while one was open for 18% -> 13% of each run, Pallas kernels for 0% -> 6%
where the time goes in v2:
time: 279 us; the launch traced here: 278 us
  waiting for transfers between devices  127 us (46%)
  starting transfers between devices  63.2 us (23%)
  matrix products  29.1 us (10%)
  Pallas kernels  22.6 us (8%)
  between operations  15.4 us (6%)
  local copies, waits for them, and re-layouts  10.9 us (4%)
  other arithmetic  9.66 us (3%)
    ppermute x60, waiting for transfers between devices, swap(): return lax.ppermute(block, 'ep', route)  126 us
    ppermute x60, starting transfers between devices, swap(): return lax.ppermute(block, 'ep', route)  53.9 us
    dot_general x26, matrix products, dot(): lax.dot_general(a, b, (dims, ((), ())), preferred_element_type=jnp.float32)  29.1 us
    pallas_call x17, Pallas kernels, kernel_call(): pl.pallas_call(body, out_shape=out_shape, in_specs=[pl.BlockSpec(memory_s...  22.6 us
    unnamed x102, local copies, waits for them, and re-layouts  6 us
  transfers between devices with their start and end apart: 63, of which 34 were waited for; matrix products, arithmetic and copies ran while one was open for 13% of the time, Pallas kernels for 6%

profile of v2, /device:TPU:0, one launch (start us, length us, event | category | flops | bytes accessed | tf_op | source)
XLA Modules:
  0.0 278.0 jit_solution(4725168813828314296)
XLA Ops:
  13.4 5.9 %collective-permute-done.3 = bf16[48,2048]{1,0:T(8,128)(2,1)S(1)} collective-permute-done((bf16[48,2048]{1,0:T(8,128)(2,1)S(1)}, bf16[48,2048]{1,0:T(8,128)(2,1)S(1)}, u32[]{:S(2)}, u32[]{:S(2)}) %collective-permute-start.3) | collective-permute-done | bytes 196640 | tf_op jit(solution)/shard_map/ppermute | solution.py:27
  19.3 3.3 %collective-permute-done.4 = bf16[48,2048]{1,0:T(8,128)(2,1)S(1)} collective-permute-done((bf16[48,2048]{1,0:T(8,128)(2,1)S(1)}, bf16[48,2048]{1,0:T(8,128)(2,1)S(1)}, u32[]{:S(2)}, u32[]{:S(2)}) %collective-permute-start.4) | collective-permute-done | bytes 196640 | tf_op jit(solution)/shard_map/ppermute | solution.py:27
  22.6 9.3 %collective-permute-done.1.refs_0_ = bf16[128,2176]{1,0:T(8,128)(2,1)} collective-permute-done((bf16[128,2176]{1,0:T(8,128)(2,1)}, bf16[128,2176]{1,0:T(8,128)(2,1)}, u32[]{:S(2)}, u32[]{:S(2)}) %collective-permute-start.1) | collective-permute-done | bytes 557088 | tf_op jit(solution)/shard_map/ppermute | solution.py:27
  41.3 3.4 %collective-permute-done.7 = bf16[48,2048]{1,0:T(8,128)(2,1)S(1)} collective-permute-done((bf16[48,2048]{1,0:T(8,128)(2,1)S(1)}, bf16[48,2048]{1,0:T(8,128)(2,1)S(1)}, u32[]{:S(2)}, u32[]{:S(2)}) %collective-permute-start.7) | collective-permute-done | bytes 196640 | tf_op jit(solution)/shard_map/ppermute | solution.py:27
  60.5 3.9 %collective-permute-done.13 = bf16[48,2048]{1,0:T(8,128)(2,1)S(1)} collective-permute-done((bf16[48,2048]{1,0:T(8,128)(2,1)S(1)}, bf16[48,2048]{1,0:T(8,128)(2,1)S(1)}, u32[]{:S(2)}, u32[]{:S(2)}) %collective-permute-start.13) | collective-permute-done | bytes 196640 | tf_op jit(solution)/shard_map/ppermute | solution.py:27
  64.4 3.4 %collective-permute-done.14 = bf16[48,2048]{1,0:T(8,128)(2,1)S(1)} collective-permute-done((bf16[48,2048]{1,0:T(8,128)(2,1)S(1)}, bf16[48,2048]{1,0:T(8,128)(2,1)S(1)}, u32[]{:S(2)}, u32[]{:S(2)}) %collective-permute-start.14) | collective-permute-done | bytes 196640 | tf_op jit(solution)/shard_map/ppermute | solution.py:27
  81.4 4.0 %collective-permute-done.19.refs_2_ = bf16[48,2048]{1,0:T(8,128)(2,1)S(1)} collective-permute-done((bf16[48,2048]{1,0:T(8,128)(2,1)S(1)}, bf16[48,2048]{1,0:T(8,128)(2,1)S(1)}, u32[]{:S(2)}, u32[]{:S(2)}) %collective-permute-start.19) | collective-permute-done | bytes 196640 | tf_op jit(solution)/shard_map/ppermute | solution.py:27
  85.3 3.4 %collective-permute-done.20.refs_3_ = bf16[48,2048]{1,0:T(8,128)(2,1)S(1)} collective-permute-done((bf16[48,2048]{1,0:T(8,128)(2,1)S(1)}, bf16[48,2048]{1,0:T(8,128)(2,1)S(1)}, u32[]{:S(2)}, u32[]{:S(2)}) %collective-permute-start.20) | collective-permute-done | bytes 196640 | tf_op jit(solution)/shard_map/ppermute | solution.py:27
  107.8 6.1 %collective-permute-done.26.refs_2_ = bf16[48,2048]{1,0:T(8,128)(2,1)S(1)} collective-permute-done((bf16[48,2048]{1,0:T(8,128)(2,1)}, bf16[48,2048]{1,0:T(8,128)(2,1)S(1)}, u32[]{:S(2)}, u32[]{:S(2)}) %collective-permute-start.26) | collective-permute-done | bytes 196640 | tf_op jit(solution)/shard_map/ppermute | solution.py:27
  113.9 3.3 %collective-permute-done.27.refs_3_ = bf16[48,2048]{1,0:T(8,128)(2,1)S(1)} collective-permute-done((bf16[48,2048]{1,0:T(8,128)(2,1)}, bf16[48,2048]{1,0:T(8,128)(2,1)S(1)}, u32[]{:S(2)}, u32[]{:S(2)}) %collective-permute-start.27) | collective-permute-done | bytes 196640 | tf_op jit(solution)/shard_map/ppermute | solution.py:27
  119.4 7.5 %collective-permute-done.29 = bf16[128,2048]{1,0:T(8,128)(2,1)} collective-permute-done((bf16[128,2048]{1,0:T(8,128)(2,1)}, bf16[128,2048]{1,0:T(8,128)(2,1)}, u32[]{:S(2)}, u32[]{:S(2)}) %collective-permute-start.29) | collective-permute-done | bytes 524320 | tf_op jit(solution)/shard_map/ppermute | solution.py:27
  131.1 3.0 %collective-permute-start.30 = (f32[1,12]{1,0:T(1,128)S(1)}, f32[1,12]{1,0:T(1,128)S(1)}, u32[]{:S(2)}, u32[]{:S(2)}) collective-permute-start(f32[1,12]{1,0:T(1,128)S(1)} %get-tuple-element.252), channel_id=1, source_target_pairs={{0,1},{1,2},{2,3},{3,4},{4,5},{5,6},{6,7},{7,8},{8,9},{9,10},{10,1... | collective-permute-start | bytes 152 | tf_op jit(solution)/shard_map/feet/ppermute | solution.py:33
  137.5 4.8 %collective-permute-start.33 = (bf16[128,2048]{1,0:T(8,128)(2,1)}, bf16[128,2048]{1,0:T(8,128)(2,1)}, u32[]{:S(2)}, u32[]{:S(2)}) collective-permute-start(bf16[128,2048]{1,0:T(8,128)(2,1)} %fusion.167.refs_0_), channel_id=1, source_target_pairs={{0,4},{1,5},{2,6},{3,7},{4,0},{5,1},{6,2},{7,3},{8,12},{9,13},{10,... | collective-permute-start | bytes 1572872 | tf_op jit(solution)/shard_map/ppermute | solution.py:27
  143.6 4.9 %collective-permute-start.37 = (f32[]{:T(128)}, f32[]{:T(128)}, u32[]{:S(2)}, u32[]{:S(2)}) collective-permute-start(f32[]{:T(128)} %add.216), channel_id=1, source_target_pairs={{0,16},{16,0},{1,17},{17,1},{2,18},{18,2},{3,19},{19,3},{4,20},{20... | collective-permute-start | bytes 20 | tf_op jit(solution)/shard_map/ppermute | solution.py:425
  154.6 4.9 %collective-permute-done.35 = bf16[48,2048]{1,0:T(8,128)(2,1)} collective-permute-done((bf16[48,2048]{1,0:T(8,128)(2,1)}, bf16[48,2048]{1,0:T(8,128)(2,1)}, u32[]{:S(2)}, u32[]{:S(2)}) %collective-permute-start.35) | collective-permute-done | bytes 196640 | tf_op jit(solution)/shard_map/ppermute | solution.py:27
  159.5 3.5 %collective-permute-done.36 = bf16[48,2048]{1,0:T(8,128)(2,1)} collective-permute-done((bf16[48,2048]{1,0:T(8,128)(2,1)}, bf16[48,2048]{1,0:T(8,128)(2,1)}, u32[]{:S(2)}, u32[]{:S(2)}) %collective-permute-start.36) | collective-permute-done | bytes 196640 | tf_op jit(solution)/shard_map/ppermute | solution.py:27
  177.9 3.0 %multiply_reduce_fusion.5 = (f32[192]{0:T(256)S(1)}, f32[192,768]{1,0:T(8,128)S(1)}) fusion(f32[192,768]{1,0:T(8,128)} %copy-done.27, f32[192,768]{1,0:T(8,128)} %copy-done.29, bf16[1,768,2048]{2,1,0:T(8,128)(2,1)S(1)} %copy-done, bf16[48,2048]{1,0:T(8,128)(2,1)} %collective-permute-done.36, bf16[48,2048]{1,0:T(8,128)(2,1)} %collective-permute-done.35, ...), kind=kOutput, calls=%fused_computation.130 | convolution fusion | flops 608157504 | bytes 5702400 | tf_op jit(solution)/shard_map/dot_general | solution.py:41
  201.8 5.4 %collective-permute-done.46 = bf16[48,2048]{1,0:T(8,128)(2,1)S(1)} collective-permute-done((bf16[48,2048]{1,0:T(8,128)(2,1)S(1)}, bf16[48,2048]{1,0:T(8,128)(2,1)S(1)}, u32[]{:S(2)}, u32[]{:S(2)}) %collective-permute-start.46) | collective-permute-done | bytes 196640 | tf_op jit(solution)/shard_map/ppermute | solution.py:27
  207.2 3.3 %collective-permute-done.47 = bf16[48,2048]{1,0:T(8,128)(2,1)S(1)} collective-permute-done((bf16[48,2048]{1,0:T(8,128)(2,1)S(1)}, bf16[48,2048]{1,0:T(8,128)(2,1)S(1)}, u32[]{:S(2)}, u32[]{:S(2)}) %collective-permute-start.47) | collective-permute-done | bytes 196640 | tf_op jit(solution)/shard_map/ppermute | solution.py:27
  220.3 4.4 %collective-permute-done.52.refs_2_ = bf16[48,2176]{1,0:T(8,128)(2,1)S(1)} collective-permute-done((bf16[48,2176]{1,0:T(8,128)(2,1)S(1)}, bf16[48,2176]{1,0:T(8,128)(2,1)S(1)}, u32[]{:S(2)}, u32[]{:S(2)}) %collective-permute-start.52) | collective-permute-done | bytes 208928 | tf_op jit(solution)/shard_map/ppermute | solution.py:27
  224.7 3.5 %collective-permute-done.53.refs_3_ = bf16[48,2176]{1,0:T(8,128)(2,1)S(1)} collective-permute-done((bf16[48,2176]{1,0:T(8,128)(2,1)S(1)}, bf16[48,2176]{1,0:T(8,128)(2,1)S(1)}, u32[]{:S(2)}, u32[]{:S(2)}) %collective-permute-start.53) | collective-permute-done | bytes 208928 | tf_op jit(solution)/shard_map/ppermute | solution.py:27
  243.4 6.3 %collective-permute-done.59.refs_2_ = bf16[48,2176]{1,0:T(8,128)(2,1)S(1)} collective-permute-done((bf16[48,2176]{1,0:T(8,128)(2,1)S(1)}, bf16[48,2176]{1,0:T(8,128)(2,1)S(1)}, u32[]{:S(2)}, u32[]{:S(2)}) %collective-permute-start.59) | collective-permute-done | bytes 208928 | tf_op jit(solution)/shard_map/ppermute | solution.py:27
  249.7 3.3 %collective-permute-done.60.refs_3_ = bf16[48,2176]{1,0:T(8,128)(2,1)S(1)} collective-permute-done((bf16[48,2176]{1,0:T(8,128)(2,1)S(1)}, bf16[48,2176]{1,0:T(8,128)(2,1)S(1)}, u32[]{:S(2)}, u32[]{:S(2)}) %collective-permute-start.60) | collective-permute-done | bytes 208928 | tf_op jit(solution)/shard_map/ppermute | solution.py:27
  253.9 12.9 %collective-permute-done.62 = bf16[128,2176]{1,0:T(8,128)(2,1)S(1)} collective-permute-done((bf16[128,2176]{1,0:T(8,128)(2,1)S(1)}, bf16[128,2176]{1,0:T(8,128)(2,1)S(1)}, u32[]{:S(2)}, u32[]{:S(2)}) %collective-permute-start.62) | collective-permute-done | bytes 557088 | tf_op jit(solution)/shard_map/ppermute | solution.py:27
  (301 shorter events, 146.0 us)
Async XLA Ops:
  4.1 27.8 %collective-permute-start.1 = (bf16[128,2176]{1,0:T(8,128)(2,1)}, bf16[128,2176]{1,0:T(8,128)(2,1)}, u32[]{:S(2)}, u32[]{:S(2)}) collective-permute-start(bf16[128,2176]{1,0:T(8,128)(2,1)} %shard_map.121.refs_0_), channel_id=1, source_target_pairs={{0,4},{1,5},{2,6},{3,7},{4,0},{5,1},{6,2},{7,3},{8,12},{9,13},{10,... | collective-permute-start | bytes 1671176 | tf_op jit(solution)/shard_map/ppermute | solution.py:27
  7.2 28.3 %collective-permute-start = (bf16[128,2176]{1,0:T(8,128)(2,1)}, bf16[128,2176]{1,0:T(8,128)(2,1)}, u32[]{:S(2)}, u32[]{:S(2)}) collective-permute-start(bf16[128,2176]{1,0:T(8,128)(2,1)} %shard_map.121.refs_0_), channel_id=1, source_target_pairs={{0,8},{1,9},{2,10},{3,11},{4,12},{5,13},{6,14},{7,15},{8,0},{9,1},... | collective-permute-start | bytes 1671176 | tf_op jit(solution)/shard_map/ppermute | solution.py:27
  35.4 20.3 %collective-permute-start.8 = (bf16[128,2176]{1,0:T(8,128)(2,1)}, bf16[128,2176]{1,0:T(8,128)(2,1)S(1)}, u32[]{:S(2)}, u32[]{:S(2)}) collective-permute-start(bf16[128,2176]{1,0:T(8,128)(2,1)} %collective-permute-done.refs_0_), channel_id=1, source_target_pairs={{0,4},{1,5},{2,6},{3,7},{4,0},{5,1},{6,2},{7,3},{8,12},{9,13},{10,... | collective-permute-start | bytes 1671176 | tf_op jit(solution)/shard_map/ppermute | solution.py:27
  37.1 13.9 %collective-permute-start.10 = (bf16[48,2048]{1,0:T(8,128)(2,1)S(1)}, bf16[48,2048]{1,0:T(8,128)(2,1)S(1)}, u32[]{:S(2)}, u32[]{:S(2)}) collective-permute-start(bf16[48,2048]{1,0:T(8,128)(2,1)S(1)} %get-tuple-element.118), channel_id=1, source_target_pairs={{0,2},{1,3},{2,0},{3,1},{4,6},{5,7},{6,4},{7,5},{8,10},{9,11},{10,... | collective-permute-start | bytes 589832 | tf_op jit(solution)/shard_map/ppermute | solution.py:27
  38.8 14.3 %collective-permute-start.11 = (bf16[48,2048]{1,0:T(8,128)(2,1)S(1)}, bf16[48,2048]{1,0:T(8,128)(2,1)S(1)}, u32[]{:S(2)}, u32[]{:S(2)}) collective-permute-start(bf16[48,2048]{1,0:T(8,128)(2,1)S(1)} %get-tuple-element.119), channel_id=1, source_target_pairs={{0,3},{1,2},{2,1},{3,0},{4,7},{5,6},{6,5},{7,4},{8,11},{9,10},{10,... | collective-permute-start | bytes 589832 | tf_op jit(solution)/shard_map/ppermute | solution.py:27
  58.3 12.2 %collective-permute-start.15 = (bf16[48,2048]{1,0:T(8,128)(2,1)S(1)}, bf16[48,2048]{1,0:T(8,128)(2,1)S(1)}, u32[]{:S(2)}, u32[]{:S(2)}) collective-permute-start(bf16[48,2048]{1,0:T(8,128)(2,1)S(1)} %get-tuple-element.132), channel_id=1, source_target_pairs={{0,1},{1,0},{2,3},{3,2},{4,5},{5,4},{6,7},{7,6},{8,9},{9,8},{10,11... | collective-permute-start | bytes 589832 | tf_op jit(solution)/shard_map/ppermute | solution.py:27
  58.8 14.0 %collective-permute-start.16 = (bf16[48,2048]{1,0:T(8,128)(2,1)S(1)}, bf16[48,2048]{1,0:T(8,128)(2,1)S(1)}, u32[]{:S(2)}, u32[]{:S(2)}) collective-permute-start(bf16[48,2048]{1,0:T(8,128)(2,1)S(1)} %get-tuple-element.133), channel_id=1, source_target_pairs={{0,2},{1,3},{2,0},{3,1},{4,6},{5,7},{6,4},{7,5},{8,10},{9,11},{10,... | collective-permute-start | bytes 589832 | tf_op jit(solution)/shard_map/ppermute | solution.py:27
  60.5 15.2 %collective-permute-start.17 = (bf16[48,2048]{1,0:T(8,128)(2,1)S(1)}, bf16[48,2048]{1,0:T(8,128)(2,1)S(1)}, u32[]{:S(2)}, u32[]{:S(2)}) collective-permute-start(bf16[48,2048]{1,0:T(8,128)(2,1)S(1)} %get-tuple-element.134), channel_id=1, source_target_pairs={{0,3},{1,2},{2,1},{3,0},{4,7},{5,6},{6,5},{7,4},{8,11},{9,10},{10,... | collective-permute-start | bytes 589832 | tf_op jit(solution)/shard_map/ppermute | solution.py:27
  76.9 14.4 %collective-permute-start.21 = (bf16[128,2048]{1,0:T(8,128)(2,1)S(1)}, bf16[128,2048]{1,0:T(8,128)(2,1)S(1)}, u32[]{:S(2)}, u32[]{:S(2)}) collective-permute-start(bf16[128,2048]{1,0:T(8,128)(2,1)S(1)} %shard_map.126), channel_id=1, source_target_pairs={{0,4},{1,5},{2,6},{3,7},{4,0},{5,1},{6,2},{7,3},{8,12},{9,13},{10,... | collective-permute-start | bytes 1572872 | tf_op jit(solution)/shard_map/ppermute | solution.py:27
  79.2 14.4 %collective-permute-start.22 = (bf16[48,2048]{1,0:T(8,128)(2,1)S(1)}, bf16[48,2048]{1,0:T(8,128)(2,1)S(1)}, u32[]{:S(2)}, u32[]{:S(2)}) collective-permute-start(bf16[48,2048]{1,0:T(8,128)(2,1)S(1)} %get-tuple-element.144), channel_id=1, source_target_pairs={{0,1},{1,0},{2,3},{3,2},{4,5},{5,4},{6,7},{7,6},{8,9},{9,8},{10,11... | collective-permute-start | bytes 589832 | tf_op jit(solution)/shard_map/ppermute | solution.py:27
  79.7 14.0 %collective-permute-start.23 = (bf16[48,2048]{1,0:T(8,128)(2,1)S(1)}, bf16[48,2048]{1,0:T(8,128)(2,1)S(1)}, u32[]{:S(2)}, u32[]{:S(2)}) collective-permute-start(bf16[48,2048]{1,0:T(8,128)(2,1)S(1)} %get-tuple-element.145), channel_id=1, source_target_pairs={{0,2},{1,3},{2,0},{3,1},{4,6},{5,7},{6,4},{7,5},{8,10},{9,11},{10,... | collective-permute-start | bytes 589832 | tf_op jit(solution)/shard_map/ppermute | solution.py:27
  98.4 21.0 %collective-permute-start.28 = (bf16[128,2048]{1,0:T(8,128)(2,1)}, bf16[128,2048]{1,0:T(8,128)(2,1)}, u32[]{:S(2)}, u32[]{:S(2)}) collective-permute-start(bf16[128,2048]{1,0:T(8,128)(2,1)} %shard_map.128), channel_id=1, source_target_pairs={{0,4},{1,5},{2,6},{3,7},{4,0},{5,1},{6,2},{7,3},{8,12},{9,13},{10,... | collective-permute-start | bytes 1572872 | tf_op jit(solution)/shard_map/ppermute | solution.py:27
  100.4 26.5 %collective-permute-start.29 = (bf16[128,2048]{1,0:T(8,128)(2,1)}, bf16[128,2048]{1,0:T(8,128)(2,1)}, u32[]{:S(2)}, u32[]{:S(2)}) collective-permute-start(bf16[128,2048]{1,0:T(8,128)(2,1)} %shard_map.127), channel_id=1, source_target_pairs={{0,12},{1,13},{2,14},{3,15},{4,8},{5,9},{6,10},{7,11},{8,4},{9,5},... | collective-permute-start | bytes 1572872 | tf_op jit(solution)/shard_map/ppermute | solution.py:27
  137.5 25.4 %collective-permute-start.33 = (bf16[128,2048]{1,0:T(8,128)(2,1)}, bf16[128,2048]{1,0:T(8,128)(2,1)}, u32[]{:S(2)}, u32[]{:S(2)}) collective-permute-start(bf16[128,2048]{1,0:T(8,128)(2,1)} %fusion.167.refs_0_), channel_id=1, source_target_pairs={{0,4},{1,5},{2,6},{3,7},{4,0},{5,1},{6,2},{7,3},{8,12},{9,13},{10,... | collective-permute-start | bytes 1572872 | tf_op jit(solution)/shard_map/ppermute | solution.py:27
  142.3 29.6 %collective-permute-start.32 = (bf16[128,2048]{1,0:T(8,128)(2,1)}, bf16[128,2048]{1,0:T(8,128)(2,1)}, u32[]{:S(2)}, u32[]{:S(2)}) collective-permute-start(bf16[128,2048]{1,0:T(8,128)(2,1)} %fusion.167.refs_0_), channel_id=1, source_target_pairs={{0,8},{1,9},{2,10},{3,11},{4,12},{5,13},{6,14},{7,15},{8,0},{9,1},... | collective-permute-start | bytes 1572872 | tf_op jit(solution)/shard_map/ppermute | solution.py:27
  171.9 22.2 %collective-permute-start.41 = (bf16[128,2048]{1,0:T(8,128)(2,1)}, bf16[128,2048]{1,0:T(8,128)(2,1)S(1)}, u32[]{:S(2)}, u32[]{:S(2)}) collective-permute-start(bf16[128,2048]{1,0:T(8,128)(2,1)} %collective-permute-done.32.refs_0_), channel_id=1, source_target_pairs={{0,4},{1,5},{2,6},{3,7},{4,0},{5,1},{6,2},{7,3},{8,12},{9,13},{10,... | collective-permute-start | bytes 1572872 | tf_op jit(solution)/shard_map/ppermute | solution.py:27
  192.0 22.6 %collective-permute-start.48 = (bf16[48,2176]{1,0:T(8,128)(2,1)S(1)}, bf16[48,2176]{1,0:T(8,128)(2,1)S(1)}, u32[]{:S(2)}, u32[]{:S(2)}) collective-permute-start(bf16[48,2176]{1,0:T(8,128)(2,1)S(1)} %get-tuple-element.181), channel_id=1, source_target_pairs={{0,1},{1,0},{2,3},{3,2},{4,5},{5,4},{6,7},{7,6},{8,9},{9,8},{10,11... | collective-permute-start | bytes 626696 | tf_op jit(solution)/shard_map/ppermute | solution.py:27
  192.3 22.3 %collective-permute-start.49 = (bf16[48,2176]{1,0:T(8,128)(2,1)S(1)}, bf16[48,2176]{1,0:T(8,128)(2,1)S(1)}, u32[]{:S(2)}, u32[]{:S(2)}) collective-permute-start(bf16[48,2176]{1,0:T(8,128)(2,1)S(1)} %get-tuple-element.182), channel_id=1, source_target_pairs={{0,2},{1,3},{2,0},{3,1},{4,6},{5,7},{6,4},{7,5},{8,10},{9,11},{10,... | collective-permute-start | bytes 626696 | tf_op jit(solution)/shard_map/ppermute | solution.py:27
  201.5 13.5 %collective-permute-start.50 = (bf16[48,2176]{1,0:T(8,128)(2,1)S(1)}, bf16[48,2176]{1,0:T(8,128)(2,1)S(1)}, u32[]{:S(2)}, u32[]{:S(2)}) collective-permute-start(bf16[48,2176]{1,0:T(8,128)(2,1)S(1)} %get-tuple-element.183), channel_id=1, source_target_pairs={{0,3},{1,2},{2,1},{3,0},{4,7},{5,6},{6,5},{7,4},{8,11},{9,10},{10,... | collective-permute-start | bytes 626696 | tf_op jit(solution)/shard_map/ppermute | solution.py:27
  215.7 15.3 %collective-permute-start.54 = (bf16[128,2176]{1,0:T(8,128)(2,1)S(1)}, bf16[128,2176]{1,0:T(8,128)(2,1)S(1)}, u32[]{:S(2)}, u32[]{:S(2)}) collective-permute-start(bf16[128,2176]{1,0:T(8,128)(2,1)S(1)} %get-tuple-element.190), channel_id=1, source_target_pairs={{0,4},{1,5},{2,6},{3,7},{4,0},{5,1},{6,2},{7,3},{8,12},{9,13},{10,... | collective-permute-start | bytes 1671176 | tf_op jit(solution)/shard_map/ppermute | solution.py:27
  218.1 13.8 %collective-permute-start.55 = (bf16[48,2176]{1,0:T(8,128)(2,1)S(1)}, bf16[48,2176]{1,0:T(8,128)(2,1)S(1)}, u32[]{:S(2)}, u32[]{:S(2)}) collective-permute-start(bf16[48,2176]{1,0:T(8,128)(2,1)S(1)} %get-tuple-element.194), channel_id=1, source_target_pairs={{0,1},{1,0},{2,3},{3,2},{4,5},{5,4},{6,7},{7,6},{8,9},{9,8},{10,11... | collective-permute-start | bytes 626696 | tf_op jit(solution)/shard_map/ppermute | solution.py:27
  218.8 14.8 %collective-permute-start.56 = (bf16[48,2176]{1,0:T(8,128)(2,1)S(1)}, bf16[48,2176]{1,0:T(8,128)(2,1)S(1)}, u32[]{:S(2)}, u32[]{:S(2)}) collective-permute-start(bf16[48,2176]{1,0:T(8,128)(2,1)S(1)} %get-tuple-element.195), channel_id=1, source_target_pairs={{0,2},{1,3},{2,0},{3,1},{4,6},{5,7},{6,4},{7,5},{8,10},{9,11},{10,... | collective-permute-start | bytes 626696 | tf_op jit(solution)/shard_map/ppermute | solution.py:27
  237.1 16.7 %collective-permute-start.61 = (bf16[128,2176]{1,0:T(8,128)(2,1)S(1)}, bf16[128,2176]{1,0:T(8,128)(2,1)S(1)}, u32[]{:S(2)}, u32[]{:S(2)}) collective-permute-start(bf16[128,2176]{1,0:T(8,128)(2,1)S(1)} %shard_map.136), channel_id=1, source_target_pairs={{0,4},{1,5},{2,6},{3,7},{4,0},{5,1},{6,2},{7,3},{8,12},{9,13},{10,... | collective-permute-start | bytes 1671176 | tf_op jit(solution)/shard_map/ppermute | solution.py:27
  238.8 27.9 %collective-permute-start.62 = (bf16[128,2176]{1,0:T(8,128)(2,1)S(1)}, bf16[128,2176]{1,0:T(8,128)(2,1)S(1)}, u32[]{:S(2)}, u32[]{:S(2)}) collective-permute-start(bf16[128,2176]{1,0:T(8,128)(2,1)S(1)} %shard_map.135), channel_id=1, source_target_pairs={{0,12},{1,13},{2,14},{3,15},{4,8},{5,9},{6,10},{7,11},{8,4},{9,5},... | collective-permute-start | bytes 1671176 | tf_op jit(solution)/shard_map/ppermute | solution.py:27
  (84 other events, 724.3 us)

commit v3 on v2

--- a/solution.py
+++ b/solution.py
@@ -9,12 +9,12 @@
 
 forward_plan = (
     "G", "c0", "t0", "c1", "r3", "c2", "t1", "e0", "e1", "t2", "e2", "b2",
-    "c3", "t3", "e3", "b3", "g2", "l2", "b1", "g3", "s3", "b0", "g1", "s1",
+    "c3", "t3", "e3", "b3", "g2", "l2", "g3", "s3", "b1", "b0", "g1", "s1",
     "g0",
 )
 backward_plan = (
-    "G", "c0", "t0", "c1", "r3", "c2", "t1", "e0", "t2", "e2", "b2", "c3",
-    "e1", "t3", "e3", "b3", "g2", "l2", "b1", "g3", "s3", "b0", "g1", "s1",
+    "G", "c0", "t0", "c1", "r3", "c2", "t1", "e0", "t2", "c3", "e2", "b2",
+    "t3", "e3", "b3", "e1", "g2", "l2", "g3", "s3", "b1", "b0", "g1", "s1",
     "g0",
 )
 epsilon = 1e-06
@@ -472,7 +472,7 @@
     chosen = expert_ids[:, :, None] == jnp.arange(experts, dtype=jnp.int32)
     grad_gates = jnp.sum(jnp.where(chosen, dots[:, None], 0.0), axis=2) / gate_values
     losses = summed_back[0, width + place + 4 : width + place + 4 + 3 * layers]
-    loss_sum = tree_sum([losses[3 * i] + losses[3 * i + 1] + losses[3 * i + 2] for i in range(layers)])
+    loss_sum = jnp.sum(losses)
     loss_value = loss_sum / (frames_all * pose_cols)
     return (grad_input, grad_gates, loss_value)
 

time: 279 us -> 262 us (0.939)
  waiting for transfers between devices: 127 us -> 116 us
  between operations: 15.4 us -> 8.39 us
    ppermute x60, waiting for transfers between devices: 126 us -> 115 us  [swap(): return lax.ppermute(block, 'ep', route)]
    ppermute x60, starting transfers between devices: 53.9 us -> 57.3 us  [swap(): return lax.ppermute(block, 'ep', route)]
  transfers between devices with their start and end apart: 63 -> 63, of which waited for: 34 -> 33; matrix products, arithmetic and copies ran while one was open for 13% -> 12% of each run, Pallas kernels for 6% -> 6%
where the time goes in v3:
time: 262 us
  waiting for transfers between devices  116 us (44%)
  starting transfers between devices  65.7 us (25%)
  matrix products  29.1 us (11%)
  Pallas kernels  22.6 us (9%)
  local copies, waits for them, and re-layouts  10.2 us (4%)
  other arithmetic  10.2 us (4%)
  between operations  8.39 us (3%)
    ppermute x60, waiting for transfers between devices, swap(): return lax.ppermute(block, 'ep', route)  115 us
    ppermute x60, starting transfers between devices, swap(): return lax.ppermute(block, 'ep', route)  57.3 us
    dot_general x26, matrix products, dot(): lax.dot_general(a, b, (dims, ((), ())), preferred_element_type=jnp.float32)  29.1 us
    pallas_call x17, Pallas kernels, kernel_call(): pl.pallas_call(body, out_shape=out_shape, in_specs=[pl.BlockSpec(memory_s...  22.6 us
    unnamed x102, local copies, waits for them, and re-layouts  6 us
  transfers between devices with their start and end apart: 63, of which 33 were waited for; matrix products, arithmetic and copies ran while one was open for 12% of the time, Pallas kernels for 6%

profile of v3, /device:TPU:0, one launch (start us, length us, event | category | flops | bytes accessed | tf_op | source)
XLA Modules:
  0.0 261.8 jit_solution(3330928453153334701)
XLA Ops:
  4.1 3.0 %collective-permute-start.1 = (bf16[128,2176]{1,0:T(8,128)(2,1)}, bf16[128,2176]{1,0:T(8,128)(2,1)}, u32[]{:S(2)}, u32[]{:S(2)}) collective-permute-start(bf16[128,2176]{1,0:T(8,128)(2,1)} %shard_map.121.refs_0_), channel_id=1, source_target_pairs={{0,4},{1,5},{2,6},{3,7},{4,0},{5,1},{6,2},{7,3},{8,12},{9,13},{10,... | collective-permute-start | bytes 1671176 | tf_op jit(solution)/shard_map/ppermute | solution.py:27
  13.4 5.9 %collective-permute-done.3 = bf16[48,2048]{1,0:T(8,128)(2,1)S(1)} collective-permute-done((bf16[48,2048]{1,0:T(8,128)(2,1)S(1)}, bf16[48,2048]{1,0:T(8,128)(2,1)S(1)}, u32[]{:S(2)}, u32[]{:S(2)}) %collective-permute-start.3) | collective-permute-done | bytes 196640 | tf_op jit(solution)/shard_map/ppermute | solution.py:27
  19.3 3.3 %collective-permute-done.4 = bf16[48,2048]{1,0:T(8,128)(2,1)S(1)} collective-permute-done((bf16[48,2048]{1,0:T(8,128)(2,1)S(1)}, bf16[48,2048]{1,0:T(8,128)(2,1)S(1)}, u32[]{:S(2)}, u32[]{:S(2)}) %collective-permute-start.4) | collective-permute-done | bytes 196640 | tf_op jit(solution)/shard_map/ppermute | solution.py:27
  22.7 9.2 %collective-permute-done.1.refs_0_ = bf16[128,2176]{1,0:T(8,128)(2,1)} collective-permute-done((bf16[128,2176]{1,0:T(8,128)(2,1)}, bf16[128,2176]{1,0:T(8,128)(2,1)}, u32[]{:S(2)}, u32[]{:S(2)}) %collective-permute-start.1) | collective-permute-done | bytes 557088 | tf_op jit(solution)/shard_map/ppermute | solution.py:27
  41.4 3.4 %collective-permute-done.7 = bf16[48,2048]{1,0:T(8,128)(2,1)S(1)} collective-permute-done((bf16[48,2048]{1,0:T(8,128)(2,1)S(1)}, bf16[48,2048]{1,0:T(8,128)(2,1)S(1)}, u32[]{:S(2)}, u32[]{:S(2)}) %collective-permute-start.7) | collective-permute-done | bytes 196640 | tf_op jit(solution)/shard_map/ppermute | solution.py:27
  60.5 3.9 %collective-permute-done.13 = bf16[48,2048]{1,0:T(8,128)(2,1)S(1)} collective-permute-done((bf16[48,2048]{1,0:T(8,128)(2,1)S(1)}, bf16[48,2048]{1,0:T(8,128)(2,1)S(1)}, u32[]{:S(2)}, u32[]{:S(2)}) %collective-permute-start.13) | collective-permute-done | bytes 196640 | tf_op jit(solution)/shard_map/ppermute | solution.py:27
  64.4 3.4 %collective-permute-done.14 = bf16[48,2048]{1,0:T(8,128)(2,1)S(1)} collective-permute-done((bf16[48,2048]{1,0:T(8,128)(2,1)S(1)}, bf16[48,2048]{1,0:T(8,128)(2,1)S(1)}, u32[]{:S(2)}, u32[]{:S(2)}) %collective-permute-start.14) | collective-permute-done | bytes 196640 | tf_op jit(solution)/shard_map/ppermute | solution.py:27
  79.3 6.1 %collective-permute-done.19.refs_2_ = bf16[48,2048]{1,0:T(8,128)(2,1)S(1)} collective-permute-done((bf16[48,2048]{1,0:T(8,128)(2,1)S(1)}, bf16[48,2048]{1,0:T(8,128)(2,1)S(1)}, u32[]{:S(2)}, u32[]{:S(2)}) %collective-permute-start.19) | collective-permute-done | bytes 196640 | tf_op jit(solution)/shard_map/ppermute | solution.py:27
  87.9 3.5 %collective-permute-done.21.refs_4_ = bf16[128,2048]{1,0:T(8,128)(2,1)S(1)} collective-permute-done((bf16[128,2048]{1,0:T(8,128)(2,1)S(1)}, bf16[128,2048]{1,0:T(8,128)(2,1)S(1)}, u32[]{:S(2)}, u32[]{:S(2)}) %collective-permute-start.21) | collective-permute-done | bytes 524320 | tf_op jit(solution)/shard_map/ppermute | solution.py:27
  98.1 3.2 %collective-permute-done.23.refs_2_ = bf16[48,2048]{1,0:T(8,128)(2,1)S(1)} collective-permute-done((bf16[48,2048]{1,0:T(8,128)(2,1)S(1)}, bf16[48,2048]{1,0:T(8,128)(2,1)S(1)}, u32[]{:S(2)}, u32[]{:S(2)}) %collective-permute-start.23) | collective-permute-done | bytes 196640 | tf_op jit(solution)/shard_map/ppermute | solution.py:27
  101.3 3.4 %collective-permute-done.24.refs_3_ = bf16[48,2048]{1,0:T(8,128)(2,1)S(1)} collective-permute-done((bf16[48,2048]{1,0:T(8,128)(2,1)S(1)}, bf16[48,2048]{1,0:T(8,128)(2,1)S(1)}, u32[]{:S(2)}, u32[]{:S(2)}) %collective-permute-start.24) | collective-permute-done | bytes 196640 | tf_op jit(solution)/shard_map/ppermute | solution.py:27
  112.0 6.3 %collective-permute-done.26.refs_2_ = bf16[48,2048]{1,0:T(8,128)(2,1)S(1)} collective-permute-done((bf16[48,2048]{1,0:T(8,128)(2,1)}, bf16[48,2048]{1,0:T(8,128)(2,1)S(1)}, u32[]{:S(2)}, u32[]{:S(2)}) %collective-permute-start.26) | collective-permute-done | bytes 196640 | tf_op jit(solution)/shard_map/ppermute | solution.py:27
  127.5 3.5 %collective-permute-start.30 = (f32[1,12]{1,0:T(1,128)S(1)}, f32[1,12]{1,0:T(1,128)S(1)}, u32[]{:S(2)}, u32[]{:S(2)}) collective-permute-start(f32[1,12]{1,0:T(1,128)S(1)} %get-tuple-element.240), channel_id=1, source_target_pairs={{0,1},{1,2},{2,3},{3,4},{4,5},{5,6},{6,7},{7,8},{8,9},{9,10},{10,1... | collective-permute-start | bytes 152 | tf_op jit(solution)/shard_map/feet/ppermute | solution.py:33
  134.3 5.8 %collective-permute-start.33 = (bf16[128,2048]{1,0:T(8,128)(2,1)}, bf16[128,2048]{1,0:T(8,128)(2,1)}, u32[]{:S(2)}, u32[]{:S(2)}) collective-permute-start(bf16[128,2048]{1,0:T(8,128)(2,1)} %fusion.167.refs_0_), channel_id=1, source_target_pairs={{0,4},{1,5},{2,6},{3,7},{4,0},{5,1},{6,2},{7,3},{8,12},{9,13},{10,... | collective-permute-start | bytes 1572872 | tf_op jit(solution)/shard_map/ppermute | solution.py:27
  143.7 3.7 %collective-permute-start.37 = (f32[]{:T(128)}, f32[]{:T(128)}, u32[]{:S(2)}, u32[]{:S(2)}) collective-permute-start(f32[]{:T(128)} %add.170), channel_id=1, source_target_pairs={{0,16},{16,0},{1,17},{17,1},{2,18},{18,2},{3,19},{19,3},{4,20},{20... | collective-permute-start | bytes 20 | tf_op jit(solution)/shard_map/ppermute | solution.py:425
  153.4 5.0 %collective-permute-done.35 = bf16[48,2048]{1,0:T(8,128)(2,1)} collective-permute-done((bf16[48,2048]{1,0:T(8,128)(2,1)}, bf16[48,2048]{1,0:T(8,128)(2,1)}, u32[]{:S(2)}, u32[]{:S(2)}) %collective-permute-start.35) | collective-permute-done | bytes 196640 | tf_op jit(solution)/shard_map/ppermute | solution.py:27
  158.3 3.5 %collective-permute-done.36 = bf16[48,2048]{1,0:T(8,128)(2,1)} collective-permute-done((bf16[48,2048]{1,0:T(8,128)(2,1)}, bf16[48,2048]{1,0:T(8,128)(2,1)}, u32[]{:S(2)}, u32[]{:S(2)}) %collective-permute-start.36) | collective-permute-done | bytes 196640 | tf_op jit(solution)/shard_map/ppermute | solution.py:27
  175.9 3.0 %multiply_reduce_fusion.5 = (f32[192]{0:T(256)S(1)}, f32[192,768]{1,0:T(8,128)S(1)}) fusion(f32[192,768]{1,0:T(8,128)} %copy-done.31, f32[192,768]{1,0:T(8,128)} %copy-done.33, bf16[1,768,2048]{2,1,0:T(8,128)(2,1)S(1)} %copy-done, bf16[48,2048]{1,0:T(8,128)(2,1)} %collective-permute-done.36, bf16[48,2048]{1,0:T(8,128)(2,1)} %collective-permute-done.35, ...), kind=kOutput, calls=%fused_computation.130 | convolution fusion | flops 608157504 | bytes 5702400 | tf_op jit(solution)/shard_map/dot_general | solution.py:41
  196.8 3.3 %collective-permute-done.47 = bf16[48,2048]{1,0:T(8,128)(2,1)S(1)} collective-permute-done((bf16[48,2048]{1,0:T(8,128)(2,1)S(1)}, bf16[48,2048]{1,0:T(8,128)(2,1)S(1)}, u32[]{:S(2)}, u32[]{:S(2)}) %collective-permute-start.47) | collective-permute-done | bytes 196640 | tf_op jit(solution)/shard_map/ppermute | solution.py:27
  213.8 6.7 %collective-permute-done.52.refs_2_ = bf16[48,2176]{1,0:T(8,128)(2,1)S(1)} collective-permute-done((bf16[48,2176]{1,0:T(8,128)(2,1)S(1)}, bf16[48,2176]{1,0:T(8,128)(2,1)S(1)}, u32[]{:S(2)}, u32[]{:S(2)}) %collective-permute-start.52) | collective-permute-done | bytes 208928 | tf_op jit(solution)/shard_map/ppermute | solution.py:27
  228.3 3.9 %collective-permute-start.62 = (bf16[128,2176]{1,0:T(8,128)(2,1)S(1)}, bf16[128,2176]{1,0:T(8,128)(2,1)S(1)}, u32[]{:S(2)}, u32[]{:S(2)}) collective-permute-start(bf16[128,2176]{1,0:T(8,128)(2,1)S(1)} %shard_map.135), channel_id=1, source_target_pairs={{0,12},{1,13},{2,14},{3,15},{4,8},{5,9},{6,10},{7,11},{8,4},{9,5},... | collective-permute-start | bytes 1671176 | tf_op jit(solution)/shard_map/ppermute | solution.py:27
  234.5 3.6 %collective-permute-done.57.refs_3_ = bf16[48,2176]{1,0:T(8,128)(2,1)S(1)} collective-permute-done((bf16[48,2176]{1,0:T(8,128)(2,1)S(1)}, bf16[48,2176]{1,0:T(8,128)(2,1)S(1)}, u32[]{:S(2)}, u32[]{:S(2)}) %collective-permute-start.57) | collective-permute-done | bytes 208928 | tf_op jit(solution)/shard_map/ppermute | solution.py:27
  242.5 6.4 %collective-permute-done.59.refs_2_ = bf16[48,2176]{1,0:T(8,128)(2,1)S(1)} collective-permute-done((bf16[48,2176]{1,0:T(8,128)(2,1)S(1)}, bf16[48,2176]{1,0:T(8,128)(2,1)S(1)}, u32[]{:S(2)}, u32[]{:S(2)}) %collective-permute-start.59) | collective-permute-done | bytes 208928 | tf_op jit(solution)/shard_map/ppermute | solution.py:27
  252.8 4.6 %collective-permute-done.61 = bf16[128,2176]{1,0:T(8,128)(2,1)S(1)} collective-permute-done((bf16[128,2176]{1,0:T(8,128)(2,1)S(1)}, bf16[128,2176]{1,0:T(8,128)(2,1)S(1)}, u32[]{:S(2)}, u32[]{:S(2)}) %collective-permute-start.61) | collective-permute-done | bytes 557088 | tf_op jit(solution)/shard_map/ppermute | solution.py:27
  (301 shorter events, 146.1 us)
Async XLA Ops:
  4.1 27.8 %collective-permute-start.1 = (bf16[128,2176]{1,0:T(8,128)(2,1)}, bf16[128,2176]{1,0:T(8,128)(2,1)}, u32[]{:S(2)}, u32[]{:S(2)}) collective-permute-start(bf16[128,2176]{1,0:T(8,128)(2,1)} %shard_map.121.refs_0_), channel_id=1, source_target_pairs={{0,4},{1,5},{2,6},{3,7},{4,0},{5,1},{6,2},{7,3},{8,12},{9,13},{10,... | collective-permute-start | bytes 1671176 | tf_op jit(solution)/shard_map/ppermute | solution.py:27
  7.2 28.3 %collective-permute-start = (bf16[128,2176]{1,0:T(8,128)(2,1)}, bf16[128,2176]{1,0:T(8,128)(2,1)}, u32[]{:S(2)}, u32[]{:S(2)}) collective-permute-start(bf16[128,2176]{1,0:T(8,128)(2,1)} %shard_map.121.refs_0_), channel_id=1, source_target_pairs={{0,8},{1,9},{2,10},{3,11},{4,12},{5,13},{6,14},{7,15},{8,0},{9,1},... | collective-permute-start | bytes 1671176 | tf_op jit(solution)/shard_map/ppermute | solution.py:27
  35.4 20.3 %collective-permute-start.8 = (bf16[128,2176]{1,0:T(8,128)(2,1)}, bf16[128,2176]{1,0:T(8,128)(2,1)S(1)}, u32[]{:S(2)}, u32[]{:S(2)}) collective-permute-start(bf16[128,2176]{1,0:T(8,128)(2,1)} %collective-permute-done.refs_0_), channel_id=1, source_target_pairs={{0,4},{1,5},{2,6},{3,7},{4,0},{5,1},{6,2},{7,3},{8,12},{9,13},{10,... | collective-permute-start | bytes 1671176 | tf_op jit(solution)/shard_map/ppermute | solution.py:27
  37.1 13.9 %collective-permute-start.10 = (bf16[48,2048]{1,0:T(8,128)(2,1)S(1)}, bf16[48,2048]{1,0:T(8,128)(2,1)S(1)}, u32[]{:S(2)}, u32[]{:S(2)}) collective-permute-start(bf16[48,2048]{1,0:T(8,128)(2,1)S(1)} %get-tuple-element.118), channel_id=1, source_target_pairs={{0,2},{1,3},{2,0},{3,1},{4,6},{5,7},{6,4},{7,5},{8,10},{9,11},{10,... | collective-permute-start | bytes 589832 | tf_op jit(solution)/shard_map/ppermute | solution.py:27
  38.8 14.3 %collective-permute-start.11 = (bf16[48,2048]{1,0:T(8,128)(2,1)S(1)}, bf16[48,2048]{1,0:T(8,128)(2,1)S(1)}, u32[]{:S(2)}, u32[]{:S(2)}) collective-permute-start(bf16[48,2048]{1,0:T(8,128)(2,1)S(1)} %get-tuple-element.119), channel_id=1, source_target_pairs={{0,3},{1,2},{2,1},{3,0},{4,7},{5,6},{6,5},{7,4},{8,11},{9,10},{10,... | collective-permute-start | bytes 589832 | tf_op jit(solution)/shard_map/ppermute | solution.py:27
  41.3 11.7 %collective-permute-start.9 = (bf16[48,2048]{1,0:T(8,128)(2,1)S(1)}, bf16[48,2048]{1,0:T(8,128)(2,1)S(1)}, u32[]{:S(2)}, u32[]{:S(2)}) collective-permute-start(bf16[48,2048]{1,0:T(8,128)(2,1)S(1)} %get-tuple-element.117), channel_id=1, source_target_pairs={{0,1},{1,0},{2,3},{3,2},{4,5},{5,4},{6,7},{7,6},{8,9},{9,8},{10,11... | collective-permute-start | bytes 589832 | tf_op jit(solution)/shard_map/ppermute | solution.py:27
  58.3 12.2 %collective-permute-start.15 = (bf16[48,2048]{1,0:T(8,128)(2,1)S(1)}, bf16[48,2048]{1,0:T(8,128)(2,1)S(1)}, u32[]{:S(2)}, u32[]{:S(2)}) collective-permute-start(bf16[48,2048]{1,0:T(8,128)(2,1)S(1)} %get-tuple-element.132), channel_id=1, source_target_pairs={{0,1},{1,0},{2,3},{3,2},{4,5},{5,4},{6,7},{7,6},{8,9},{9,8},{10,11... | collective-permute-start | bytes 589832 | tf_op jit(solution)/shard_map/ppermute | solution.py:27
  58.8 14.0 %collective-permute-start.16 = (bf16[48,2048]{1,0:T(8,128)(2,1)S(1)}, bf16[48,2048]{1,0:T(8,128)(2,1)S(1)}, u32[]{:S(2)}, u32[]{:S(2)}) collective-permute-start(bf16[48,2048]{1,0:T(8,128)(2,1)S(1)} %get-tuple-element.133), channel_id=1, source_target_pairs={{0,2},{1,3},{2,0},{3,1},{4,6},{5,7},{6,4},{7,5},{8,10},{9,11},{10,... | collective-permute-start | bytes 589832 | tf_op jit(solution)/shard_map/ppermute | solution.py:27
  60.5 15.2 %collective-permute-start.17 = (bf16[48,2048]{1,0:T(8,128)(2,1)S(1)}, bf16[48,2048]{1,0:T(8,128)(2,1)S(1)}, u32[]{:S(2)}, u32[]{:S(2)}) collective-permute-start(bf16[48,2048]{1,0:T(8,128)(2,1)S(1)} %get-tuple-element.134), channel_id=1, source_target_pairs={{0,3},{1,2},{2,1},{3,0},{4,7},{5,6},{6,5},{7,4},{8,11},{9,10},{10,... | collective-permute-start | bytes 589832 | tf_op jit(solution)/shard_map/ppermute | solution.py:27
  76.9 14.4 %collective-permute-start.21 = (bf16[128,2048]{1,0:T(8,128)(2,1)S(1)}, bf16[128,2048]{1,0:T(8,128)(2,1)S(1)}, u32[]{:S(2)}, u32[]{:S(2)}) collective-permute-start(bf16[128,2048]{1,0:T(8,128)(2,1)S(1)} %shard_map.126), channel_id=1, source_target_pairs={{0,4},{1,5},{2,6},{3,7},{4,0},{5,1},{6,2},{7,3},{8,12},{9,13},{10,... | collective-permute-start | bytes 1572872 | tf_op jit(solution)/shard_map/ppermute | solution.py:27
  95.5 27.8 %collective-permute-start.29 = (bf16[128,2048]{1,0:T(8,128)(2,1)}, bf16[128,2048]{1,0:T(8,128)(2,1)}, u32[]{:S(2)}, u32[]{:S(2)}) collective-permute-start(bf16[128,2048]{1,0:T(8,128)(2,1)} %shard_map.127), channel_id=1, source_target_pairs={{0,12},{1,13},{2,14},{3,15},{4,8},{5,9},{6,10},{7,11},{8,4},{9,5},... | collective-permute-start | bytes 1572872 | tf_op jit(solution)/shard_map/ppermute | solution.py:27
  106.9 16.4 %collective-permute-start.28 = (bf16[128,2048]{1,0:T(8,128)(2,1)}, bf16[128,2048]{1,0:T(8,128)(2,1)}, u32[]{:S(2)}, u32[]{:S(2)}) collective-permute-start(bf16[128,2048]{1,0:T(8,128)(2,1)} %shard_map.128), channel_id=1, source_target_pairs={{0,4},{1,5},{2,6},{3,7},{4,0},{5,1},{6,2},{7,3},{8,12},{9,13},{10,... | collective-permute-start | bytes 1572872 | tf_op jit(solution)/shard_map/ppermute | solution.py:27
  134.3 27.5 %collective-permute-start.33 = (bf16[128,2048]{1,0:T(8,128)(2,1)}, bf16[128,2048]{1,0:T(8,128)(2,1)}, u32[]{:S(2)}, u32[]{:S(2)}) collective-permute-start(bf16[128,2048]{1,0:T(8,128)(2,1)} %fusion.167.refs_0_), channel_id=1, source_target_pairs={{0,4},{1,5},{2,6},{3,7},{4,0},{5,1},{6,2},{7,3},{8,12},{9,13},{10,... | collective-permute-start | bytes 1572872 | tf_op jit(solution)/shard_map/ppermute | solution.py:27
  140.1 29.9 %collective-permute-start.32 = (bf16[128,2048]{1,0:T(8,128)(2,1)}, bf16[128,2048]{1,0:T(8,128)(2,1)}, u32[]{:S(2)}, u32[]{:S(2)}) collective-permute-start(bf16[128,2048]{1,0:T(8,128)(2,1)} %fusion.167.refs_0_), channel_id=1, source_target_pairs={{0,8},{1,9},{2,10},{3,11},{4,12},{5,13},{6,14},{7,15},{8,0},{9,1},... | collective-permute-start | bytes 1572872 | tf_op jit(solution)/shard_map/ppermute | solution.py:27
  150.3 11.5 %collective-permute-start.36 = (bf16[48,2048]{1,0:T(8,128)(2,1)}, bf16[48,2048]{1,0:T(8,128)(2,1)}, u32[]{:S(2)}, u32[]{:S(2)}) collective-permute-start(bf16[48,2048]{1,0:T(8,128)(2,1)} %get-tuple-element.156), channel_id=1, source_target_pairs={{0,3},{1,2},{2,1},{3,0},{4,7},{5,6},{6,5},{7,4},{8,11},{9,10},{10,... | collective-permute-start | bytes 589832 | tf_op jit(solution)/shard_map/ppermute | solution.py:27
  170.0 14.9 %collective-permute-start.41 = (bf16[128,2048]{1,0:T(8,128)(2,1)}, bf16[128,2048]{1,0:T(8,128)(2,1)S(1)}, u32[]{:S(2)}, u32[]{:S(2)}) collective-permute-start(bf16[128,2048]{1,0:T(8,128)(2,1)} %collective-permute-done.32.refs_0_), channel_id=1, source_target_pairs={{0,4},{1,5},{2,6},{3,7},{4,0},{5,1},{6,2},{7,3},{8,12},{9,13},{10,... | collective-permute-start | bytes 1572872 | tf_op jit(solution)/shard_map/ppermute | solution.py:27
  193.0 16.3 %collective-permute-start.48 = (bf16[48,2176]{1,0:T(8,128)(2,1)S(1)}, bf16[48,2176]{1,0:T(8,128)(2,1)S(1)}, u32[]{:S(2)}, u32[]{:S(2)}) collective-permute-start(bf16[48,2176]{1,0:T(8,128)(2,1)S(1)} %get-tuple-element.181), channel_id=1, source_target_pairs={{0,1},{1,0},{2,3},{3,2},{4,5},{5,4},{6,7},{7,6},{8,9},{9,8},{10,11... | collective-permute-start | bytes 626696 | tf_op jit(solution)/shard_map/ppermute | solution.py:27
  193.4 15.9 %collective-permute-start.49 = (bf16[48,2176]{1,0:T(8,128)(2,1)S(1)}, bf16[48,2176]{1,0:T(8,128)(2,1)S(1)}, u32[]{:S(2)}, u32[]{:S(2)}) collective-permute-start(bf16[48,2176]{1,0:T(8,128)(2,1)S(1)} %get-tuple-element.182), channel_id=1, source_target_pairs={{0,2},{1,3},{2,0},{3,1},{4,6},{5,7},{6,4},{7,5},{8,10},{9,11},{10,... | collective-permute-start | bytes 626696 | tf_op jit(solution)/shard_map/ppermute | solution.py:27
  194.6 14.7 %collective-permute-start.50 = (bf16[48,2176]{1,0:T(8,128)(2,1)S(1)}, bf16[48,2176]{1,0:T(8,128)(2,1)S(1)}, u32[]{:S(2)}, u32[]{:S(2)}) collective-permute-start(bf16[48,2176]{1,0:T(8,128)(2,1)S(1)} %get-tuple-element.183), channel_id=1, source_target_pairs={{0,3},{1,2},{2,1},{3,0},{4,7},{5,6},{6,5},{7,4},{8,11},{9,10},{10,... | collective-permute-start | bytes 626696 | tf_op jit(solution)/shard_map/ppermute | solution.py:27
  210.1 15.4 %collective-permute-start.54 = (bf16[128,2176]{1,0:T(8,128)(2,1)S(1)}, bf16[128,2176]{1,0:T(8,128)(2,1)S(1)}, u32[]{:S(2)}, u32[]{:S(2)}) collective-permute-start(bf16[128,2176]{1,0:T(8,128)(2,1)S(1)} %get-tuple-element.190), channel_id=1, source_target_pairs={{0,4},{1,5},{2,6},{3,7},{4,0},{5,1},{6,2},{7,3},{8,12},{9,13},{10,... | collective-permute-start | bytes 1671176 | tf_op jit(solution)/shard_map/ppermute | solution.py:27
  227.5 10.5 %collective-permute-start.57 = (bf16[48,2176]{1,0:T(8,128)(2,1)S(1)}, bf16[48,2176]{1,0:T(8,128)(2,1)S(1)}, u32[]{:S(2)}, u32[]{:S(2)}) collective-permute-start(bf16[48,2176]{1,0:T(8,128)(2,1)S(1)} %get-tuple-element.196), channel_id=1, source_target_pairs={{0,3},{1,2},{2,1},{3,0},{4,7},{5,6},{6,5},{7,4},{8,11},{9,10},{10,... | collective-permute-start | bytes 626696 | tf_op jit(solution)/shard_map/ppermute | solution.py:27
  228.3 24.5 %collective-permute-start.62 = (bf16[128,2176]{1,0:T(8,128)(2,1)S(1)}, bf16[128,2176]{1,0:T(8,128)(2,1)S(1)}, u32[]{:S(2)}, u32[]{:S(2)}) collective-permute-start(bf16[128,2176]{1,0:T(8,128)(2,1)S(1)} %shard_map.135), channel_id=1, source_target_pairs={{0,12},{1,13},{2,14},{3,15},{4,8},{5,9},{6,10},{7,11},{8,4},{9,5},... | collective-permute-start | bytes 1671176 | tf_op jit(solution)/shard_map/ppermute | solution.py:27
  238.8 18.5 %collective-permute-start.61 = (bf16[128,2176]{1,0:T(8,128)(2,1)S(1)}, bf16[128,2176]{1,0:T(8,128)(2,1)S(1)}, u32[]{:S(2)}, u32[]{:S(2)}) collective-permute-start(bf16[128,2176]{1,0:T(8,128)(2,1)S(1)} %shard_map.136), channel_id=1, source_target_pairs={{0,4},{1,5},{2,6},{3,7},{4,0},{5,1},{6,2},{7,3},{8,12},{9,13},{10,... | collective-permute-start | bytes 1671176 | tf_op jit(solution)/shard_map/ppermute | solution.py:27
  241.4 10.6 %collective-permute-start.60 = (bf16[48,2176]{1,0:T(8,128)(2,1)S(1)}, bf16[48,2176]{1,0:T(8,128)(2,1)S(1)}, u32[]{:S(2)}, u32[]{:S(2)}) collective-permute-start(bf16[48,2176]{1,0:T(8,128)(2,1)S(1)} %get-tuple-element.200), channel_id=1, source_target_pairs={{0,3},{1,2},{2,1},{3,0},{4,7},{5,6},{6,5},{7,4},{8,11},{9,10},{10,... | collective-permute-start | bytes 626696 | tf_op jit(solution)/shard_map/ppermute | solution.py:27
  (84 other events, 624.5 us)

commit v4 on v3

--- a/solution.py
+++ b/solution.py
@@ -8,9 +8,9 @@
 from jax.sharding import PartitionSpec as P
 
 forward_plan = (
-    "G", "c0", "t0", "c1", "r3", "c2", "t1", "e0", "e1", "t2", "e2", "b2",
-    "c3", "t3", "e3", "b3", "g2", "l2", "g3", "s3", "b1", "b0", "g1", "s1",
-    "g0",
+    "H", "c0", "z2", "t0", "c1", "r3", "c2", "t1", "e0", "e1", "t2", "c3",
+    "e2", "b2", "t3", "e3", "b3", "g2", "l2", "g3", "s3", "b1", "b0", "g1",
+    "s1", "g0",
 )
 backward_plan = (
     "G", "c0", "t0", "c1", "r3", "c2", "t1", "e0", "t2", "c3", "e2", "b2",
@@ -259,7 +259,7 @@
     def rounds(plan, rows, choose, expert, collect):
         scheme, plan = plan
         held = {0: [rows]}
-        for k in {"I": [1], "F": [1, 3], "G": [1, 2]}.get(scheme, range(1, layers)):
+        for k in {"I": [1], "F": [1, 3], "G": [1, 2], "H": [1]}.get(scheme, range(1, layers)):
             held[k] = [swap(rows, k * peers)]
         if scheme == "I":
             held[3] = [across(rows)]
@@ -280,8 +280,12 @@
             results[k] = exchange(list(rows[:peers]))
             return last
 
+        def do_spread(k, last):
+            held[k] = [swap(after(rows, *last), k * peers)]
+            return last
+
         def do_relay(k, last):
-            if scheme in "FG":
+            if scheme in "FGH":
                 held[k ^ 1] = [after(held[k ^ 1][0], *last)]
                 held[k] = [swap(held[k ^ 1][0], peers)]
                 return last
@@ -320,6 +324,7 @@
             "g": do_collect,
             "l": do_lend,
             "r": do_relay,
+            "z": do_spread,
             "t": do_touch,
             "s": do_send,
         }

time: 262 us -> 260 us (level)
  transfers between devices with their start and end apart: 63 -> 63, of which waited for: 33 -> 34; matrix products, arithmetic and copies ran while one was open for 12% -> 12% of each run, Pallas kernels for 6% -> 6%
where the time goes in v4:
time: 260 us; the launch traced here: 259 us
  waiting for transfers between devices  114 us (44%)
  starting transfers between devices  65.6 us (25%)
  matrix products  29.2 us (11%)
  Pallas kernels  21.5 us (8%)
  local copies, waits for them, and re-layouts  10.2 us (4%)
  other arithmetic  10.2 us (4%)
  between operations  8.37 us (3%)
    ppermute x60, waiting for transfers between devices, swap(): return lax.ppermute(block, 'ep', route)  113 us
    ppermute x60, starting transfers between devices, swap(): return lax.ppermute(block, 'ep', route)  57.1 us
    dot_general x26, matrix products, dot(): lax.dot_general(a, b, (dims, ((), ())), preferred_element_type=jnp.float32)  29.2 us
    pallas_call x17, Pallas kernels, kernel_call(): pl.pallas_call(body, out_shape=out_shape, in_specs=[pl.BlockSpec(memory_s...  21.5 us
    unnamed x102, local copies, waits for them, and re-layouts  6.01 us
  transfers between devices with their start and end apart: 63, of which 34 were waited for; matrix products, arithmetic and copies ran while one was open for 12% of the time, Pallas kernels for 6%

profile of v4, /device:TPU:0, one launch (start us, length us, event | category | flops | bytes accessed | tf_op | source)
XLA Modules:
  0.0 259.2 jit_solution(573685540475597993)
XLA Ops:
  4.1 3.0 %collective-permute-start.1 = (bf16[128,2176]{1,0:T(8,128)(2,1)}, bf16[128,2176]{1,0:T(8,128)(2,1)}, u32[]{:S(2)}, u32[]{:S(2)}) collective-permute-start(bf16[128,2176]{1,0:T(8,128)(2,1)} %shard_map.121.refs_0_), channel_id=1, source_target_pairs={{0,4},{1,5},{2,6},{3,7},{4,0},{5,1},{6,2},{7,3},{8,12},{9,13},{10,... | collective-permute-start | bytes 1671176 | tf_op jit(solution)/shard_map/ppermute | solution.py:27
  13.4 5.8 %collective-permute-done.3 = bf16[48,2048]{1,0:T(8,128)(2,1)S(1)} collective-permute-done((bf16[48,2048]{1,0:T(8,128)(2,1)S(1)}, bf16[48,2048]{1,0:T(8,128)(2,1)S(1)}, u32[]{:S(2)}, u32[]{:S(2)}) %collective-permute-start.3) | collective-permute-done | bytes 196640 | tf_op jit(solution)/shard_map/ppermute | solution.py:27
  19.3 3.4 %collective-permute-done.4 = bf16[48,2048]{1,0:T(8,128)(2,1)S(1)} collective-permute-done((bf16[48,2048]{1,0:T(8,128)(2,1)S(1)}, bf16[48,2048]{1,0:T(8,128)(2,1)S(1)}, u32[]{:S(2)}, u32[]{:S(2)}) %collective-permute-start.4) | collective-permute-done | bytes 196640 | tf_op jit(solution)/shard_map/ppermute | solution.py:27
  22.7 7.4 %collective-permute-done.1.refs_0_ = bf16[128,2176]{1,0:T(8,128)(2,1)} collective-permute-done((bf16[128,2176]{1,0:T(8,128)(2,1)}, bf16[128,2176]{1,0:T(8,128)(2,1)}, u32[]{:S(2)}, u32[]{:S(2)}) %collective-permute-start.1) | collective-permute-done | bytes 557088 | tf_op jit(solution)/shard_map/ppermute | solution.py:27
  39.5 3.4 %collective-permute-done.7 = bf16[48,2048]{1,0:T(8,128)(2,1)S(1)} collective-permute-done((bf16[48,2048]{1,0:T(8,128)(2,1)S(1)}, bf16[48,2048]{1,0:T(8,128)(2,1)S(1)}, u32[]{:S(2)}, u32[]{:S(2)}) %collective-permute-start.7) | collective-permute-done | bytes 196640 | tf_op jit(solution)/shard_map/ppermute | solution.py:27
  61.6 3.4 %collective-permute-done.14 = bf16[48,2048]{1,0:T(8,128)(2,1)S(1)} collective-permute-done((bf16[48,2048]{1,0:T(8,128)(2,1)S(1)}, bf16[48,2048]{1,0:T(8,128)(2,1)S(1)}, u32[]{:S(2)}, u32[]{:S(2)}) %collective-permute-start.14) | collective-permute-done | bytes 196640 | tf_op jit(solution)/shard_map/ppermute | solution.py:27
  76.5 6.1 %collective-permute-done.19.refs_2_ = bf16[48,2048]{1,0:T(8,128)(2,1)S(1)} collective-permute-done((bf16[48,2048]{1,0:T(8,128)(2,1)S(1)}, bf16[48,2048]{1,0:T(8,128)(2,1)S(1)}, u32[]{:S(2)}, u32[]{:S(2)}) %collective-permute-start.19) | collective-permute-done | bytes 196640 | tf_op jit(solution)/shard_map/ppermute | solution.py:27
  85.1 3.5 %collective-permute-done.21.refs_4_ = bf16[128,2048]{1,0:T(8,128)(2,1)S(1)} collective-permute-done((bf16[128,2048]{1,0:T(8,128)(2,1)S(1)}, bf16[128,2048]{1,0:T(8,128)(2,1)S(1)}, u32[]{:S(2)}, u32[]{:S(2)}) %collective-permute-start.21) | collective-permute-done | bytes 524320 | tf_op jit(solution)/shard_map/ppermute | solution.py:27
  95.4 3.2 %collective-permute-done.23.refs_2_ = bf16[48,2048]{1,0:T(8,128)(2,1)S(1)} collective-permute-done((bf16[48,2048]{1,0:T(8,128)(2,1)S(1)}, bf16[48,2048]{1,0:T(8,128)(2,1)S(1)}, u32[]{:S(2)}, u32[]{:S(2)}) %collective-permute-start.23) | collective-permute-done | bytes 196640 | tf_op jit(solution)/shard_map/ppermute | solution.py:27
  98.6 3.4 %collective-permute-done.24.refs_3_ = bf16[48,2048]{1,0:T(8,128)(2,1)S(1)} collective-permute-done((bf16[48,2048]{1,0:T(8,128)(2,1)S(1)}, bf16[48,2048]{1,0:T(8,128)(2,1)S(1)}, u32[]{:S(2)}, u32[]{:S(2)}) %collective-permute-start.24) | collective-permute-done | bytes 196640 | tf_op jit(solution)/shard_map/ppermute | solution.py:27
  109.3 6.3 %collective-permute-done.26.refs_2_ = bf16[48,2048]{1,0:T(8,128)(2,1)S(1)} collective-permute-done((bf16[48,2048]{1,0:T(8,128)(2,1)}, bf16[48,2048]{1,0:T(8,128)(2,1)S(1)}, u32[]{:S(2)}, u32[]{:S(2)}) %collective-permute-start.26) | collective-permute-done | bytes 196640 | tf_op jit(solution)/shard_map/ppermute | solution.py:27
  124.7 3.5 %collective-permute-start.30 = (f32[1,12]{1,0:T(1,128)S(1)}, f32[1,12]{1,0:T(1,128)S(1)}, u32[]{:S(2)}, u32[]{:S(2)}) collective-permute-start(f32[1,12]{1,0:T(1,128)S(1)} %get-tuple-element.242), channel_id=1, source_target_pairs={{0,1},{1,2},{2,3},{3,4},{4,5},{5,6},{6,7},{7,8},{8,9},{9,10},{10,1... | collective-permute-start | bytes 152 | tf_op jit(solution)/shard_map/feet/ppermute | solution.py:33
  131.5 5.7 %collective-permute-start.33 = (bf16[128,2048]{1,0:T(8,128)(2,1)}, bf16[128,2048]{1,0:T(8,128)(2,1)}, u32[]{:S(2)}, u32[]{:S(2)}) collective-permute-start(bf16[128,2048]{1,0:T(8,128)(2,1)} %fusion.167.refs_0_), channel_id=1, source_target_pairs={{0,4},{1,5},{2,6},{3,7},{4,0},{5,1},{6,2},{7,3},{8,12},{9,13},{10,... | collective-permute-start | bytes 1572872 | tf_op jit(solution)/shard_map/ppermute | solution.py:27
  141.0 3.7 %collective-permute-start.37 = (f32[]{:T(128)}, f32[]{:T(128)}, u32[]{:S(2)}, u32[]{:S(2)}) collective-permute-start(f32[]{:T(128)} %add.170), channel_id=1, source_target_pairs={{0,16},{16,0},{1,17},{17,1},{2,18},{18,2},{3,19},{19,3},{4,20},{20... | collective-permute-start | bytes 20 | tf_op jit(solution)/shard_map/ppermute | solution.py:430
  150.6 5.0 %collective-permute-done.35 = bf16[48,2048]{1,0:T(8,128)(2,1)} collective-permute-done((bf16[48,2048]{1,0:T(8,128)(2,1)}, bf16[48,2048]{1,0:T(8,128)(2,1)}, u32[]{:S(2)}, u32[]{:S(2)}) %collective-permute-start.35) | collective-permute-done | bytes 196640 | tf_op jit(solution)/shard_map/ppermute | solution.py:27
  155.5 3.5 %collective-permute-done.36 = bf16[48,2048]{1,0:T(8,128)(2,1)} collective-permute-done((bf16[48,2048]{1,0:T(8,128)(2,1)}, bf16[48,2048]{1,0:T(8,128)(2,1)}, u32[]{:S(2)}, u32[]{:S(2)}) %collective-permute-start.36) | collective-permute-done | bytes 196640 | tf_op jit(solution)/shard_map/ppermute | solution.py:27
  173.1 3.0 %multiply_reduce_fusion.5 = (f32[192]{0:T(256)S(1)}, f32[192,768]{1,0:T(8,128)S(1)}) fusion(f32[192,768]{1,0:T(8,128)} %copy-done.27, f32[192,768]{1,0:T(8,128)} %copy-done.29, bf16[1,768,2048]{2,1,0:T(8,128)(2,1)S(1)} %copy-done, bf16[48,2048]{1,0:T(8,128)(2,1)} %collective-permute-done.36, bf16[48,2048]{1,0:T(8,128)(2,1)} %collective-permute-done.35, ...), kind=kOutput, calls=%fused_computation.130 | convolution fusion | flops 608157504 | bytes 5702400 | tf_op jit(solution)/shard_map/dot_general | solution.py:41
  194.0 3.3 %collective-permute-done.47 = bf16[48,2048]{1,0:T(8,128)(2,1)S(1)} collective-permute-done((bf16[48,2048]{1,0:T(8,128)(2,1)S(1)}, bf16[48,2048]{1,0:T(8,128)(2,1)S(1)}, u32[]{:S(2)}, u32[]{:S(2)}) %collective-permute-start.47) | collective-permute-done | bytes 196640 | tf_op jit(solution)/shard_map/ppermute | solution.py:27
  211.1 6.7 %collective-permute-done.52.refs_2_ = bf16[48,2176]{1,0:T(8,128)(2,1)S(1)} collective-permute-done((bf16[48,2176]{1,0:T(8,128)(2,1)S(1)}, bf16[48,2176]{1,0:T(8,128)(2,1)S(1)}, u32[]{:S(2)}, u32[]{:S(2)}) %collective-permute-start.52) | collective-permute-done | bytes 208928 | tf_op jit(solution)/shard_map/ppermute | solution.py:27
  225.6 3.9 %collective-permute-start.62 = (bf16[128,2176]{1,0:T(8,128)(2,1)S(1)}, bf16[128,2176]{1,0:T(8,128)(2,1)S(1)}, u32[]{:S(2)}, u32[]{:S(2)}) collective-permute-start(bf16[128,2176]{1,0:T(8,128)(2,1)S(1)} %shard_map.135), channel_id=1, source_target_pairs={{0,12},{1,13},{2,14},{3,15},{4,8},{5,9},{6,10},{7,11},{8,4},{9,5},... | collective-permute-start | bytes 1671176 | tf_op jit(solution)/shard_map/ppermute | solution.py:27
  231.8 3.6 %collective-permute-done.57.refs_3_ = bf16[48,2176]{1,0:T(8,128)(2,1)S(1)} collective-permute-done((bf16[48,2176]{1,0:T(8,128)(2,1)S(1)}, bf16[48,2176]{1,0:T(8,128)(2,1)S(1)}, u32[]{:S(2)}, u32[]{:S(2)}) %collective-permute-start.57) | collective-permute-done | bytes 208928 | tf_op jit(solution)/shard_map/ppermute | solution.py:27
  239.8 6.4 %collective-permute-done.59.refs_2_ = bf16[48,2176]{1,0:T(8,128)(2,1)S(1)} collective-permute-done((bf16[48,2176]{1,0:T(8,128)(2,1)S(1)}, bf16[48,2176]{1,0:T(8,128)(2,1)S(1)}, u32[]{:S(2)}, u32[]{:S(2)}) %collective-permute-start.59) | collective-permute-done | bytes 208928 | tf_op jit(solution)/shard_map/ppermute | solution.py:27
  246.2 3.1 %collective-permute-done.60.refs_3_ = bf16[48,2176]{1,0:T(8,128)(2,1)S(1)} collective-permute-done((bf16[48,2176]{1,0:T(8,128)(2,1)S(1)}, bf16[48,2176]{1,0:T(8,128)(2,1)S(1)}, u32[]{:S(2)}, u32[]{:S(2)}) %collective-permute-start.60) | collective-permute-done | bytes 208928 | tf_op jit(solution)/shard_map/ppermute | solution.py:27
  250.1 4.6 %collective-permute-done.61 = bf16[128,2176]{1,0:T(8,128)(2,1)S(1)} collective-permute-done((bf16[128,2176]{1,0:T(8,128)(2,1)S(1)}, bf16[128,2176]{1,0:T(8,128)(2,1)S(1)}, u32[]{:S(2)}, u32[]{:S(2)}) %collective-permute-start.61) | collective-permute-done | bytes 557088 | tf_op jit(solution)/shard_map/ppermute | solution.py:27
  (301 shorter events, 146.0 us)
Async XLA Ops:
  4.1 26.0 %collective-permute-start.1 = (bf16[128,2176]{1,0:T(8,128)(2,1)}, bf16[128,2176]{1,0:T(8,128)(2,1)}, u32[]{:S(2)}, u32[]{:S(2)}) collective-permute-start(bf16[128,2176]{1,0:T(8,128)(2,1)} %shard_map.121.refs_0_), channel_id=1, source_target_pairs={{0,4},{1,5},{2,6},{3,7},{4,0},{5,1},{6,2},{7,3},{8,12},{9,13},{10,... | collective-permute-start | bytes 1671176 | tf_op jit(solution)/shard_map/ppermute | solution.py:27
  8.9 27.3 %collective-permute-start = (bf16[128,2176]{1,0:T(8,128)(2,1)}, bf16[128,2176]{1,0:T(8,128)(2,1)S(1)}, u32[]{:S(2)}, u32[]{:S(2)}) collective-permute-start(bf16[128,2176]{1,0:T(8,128)(2,1)} %shard_map.121.refs_0_), channel_id=1, source_target_pairs={{0,8},{1,9},{2,10},{3,11},{4,12},{5,13},{6,14},{7,15},{8,0},{9,1},... | collective-permute-start | bytes 1671176 | tf_op jit(solution)/shard_map/ppermute | solution.py:27
  36.2 15.1 %collective-permute-start.8 = (bf16[128,2176]{1,0:T(8,128)(2,1)S(1)}, bf16[128,2176]{1,0:T(8,128)(2,1)S(1)}, u32[]{:S(2)}, u32[]{:S(2)}) collective-permute-start(bf16[128,2176]{1,0:T(8,128)(2,1)S(1)} %collective-permute-done.refs_0_), channel_id=1, source_target_pairs={{0,4},{1,5},{2,6},{3,7},{4,0},{5,1},{6,2},{7,3},{8,12},{9,13},{10,... | collective-permute-start | bytes 1671176 | tf_op jit(solution)/shard_map/ppermute | solution.py:27
  36.7 12.5 %collective-permute-start.10 = (bf16[48,2048]{1,0:T(8,128)(2,1)S(1)}, bf16[48,2048]{1,0:T(8,128)(2,1)S(1)}, u32[]{:S(2)}, u32[]{:S(2)}) collective-permute-start(bf16[48,2048]{1,0:T(8,128)(2,1)S(1)} %get-tuple-element.120), channel_id=1, source_target_pairs={{0,2},{1,3},{2,0},{3,1},{4,6},{5,7},{6,4},{7,5},{8,10},{9,11},{10,... | collective-permute-start | bytes 589832 | tf_op jit(solution)/shard_map/ppermute | solution.py:27
  38.3 13.0 %collective-permute-start.11 = (bf16[48,2048]{1,0:T(8,128)(2,1)S(1)}, bf16[48,2048]{1,0:T(8,128)(2,1)S(1)}, u32[]{:S(2)}, u32[]{:S(2)}) collective-permute-start(bf16[48,2048]{1,0:T(8,128)(2,1)S(1)} %get-tuple-element.121), channel_id=1, source_target_pairs={{0,3},{1,2},{2,1},{3,0},{4,7},{5,6},{6,5},{7,4},{8,11},{9,10},{10,... | collective-permute-start | bytes 589832 | tf_op jit(solution)/shard_map/ppermute | solution.py:27
  39.5 11.7 %collective-permute-start.9 = (bf16[48,2048]{1,0:T(8,128)(2,1)S(1)}, bf16[48,2048]{1,0:T(8,128)(2,1)S(1)}, u32[]{:S(2)}, u32[]{:S(2)}) collective-permute-start(bf16[48,2048]{1,0:T(8,128)(2,1)S(1)} %get-tuple-element.119), channel_id=1, source_target_pairs={{0,1},{1,0},{2,3},{3,2},{4,5},{5,4},{6,7},{7,6},{8,9},{9,8},{10,11... | collective-permute-start | bytes 589832 | tf_op jit(solution)/shard_map/ppermute | solution.py:27
  56.5 11.2 %collective-permute-start.15 = (bf16[48,2048]{1,0:T(8,128)(2,1)S(1)}, bf16[48,2048]{1,0:T(8,128)(2,1)S(1)}, u32[]{:S(2)}, u32[]{:S(2)}) collective-permute-start(bf16[48,2048]{1,0:T(8,128)(2,1)S(1)} %get-tuple-element.134), channel_id=1, source_target_pairs={{0,1},{1,0},{2,3},{3,2},{4,5},{5,4},{6,7},{7,6},{8,9},{9,8},{10,11... | collective-permute-start | bytes 589832 | tf_op jit(solution)/shard_map/ppermute | solution.py:27
  57.0 13.0 %collective-permute-start.16 = (bf16[48,2048]{1,0:T(8,128)(2,1)S(1)}, bf16[48,2048]{1,0:T(8,128)(2,1)S(1)}, u32[]{:S(2)}, u32[]{:S(2)}) collective-permute-start(bf16[48,2048]{1,0:T(8,128)(2,1)S(1)} %get-tuple-element.135), channel_id=1, source_target_pairs={{0,2},{1,3},{2,0},{3,1},{4,6},{5,7},{6,4},{7,5},{8,10},{9,11},{10,... | collective-permute-start | bytes 589832 | tf_op jit(solution)/shard_map/ppermute | solution.py:27
  58.7 14.2 %collective-permute-start.17 = (bf16[48,2048]{1,0:T(8,128)(2,1)S(1)}, bf16[48,2048]{1,0:T(8,128)(2,1)S(1)}, u32[]{:S(2)}, u32[]{:S(2)}) collective-permute-start(bf16[48,2048]{1,0:T(8,128)(2,1)S(1)} %get-tuple-element.136), channel_id=1, source_target_pairs={{0,3},{1,2},{2,1},{3,0},{4,7},{5,6},{6,5},{7,4},{8,11},{9,10},{10,... | collective-permute-start | bytes 589832 | tf_op jit(solution)/shard_map/ppermute | solution.py:27
  74.2 14.4 %collective-permute-start.21 = (bf16[128,2048]{1,0:T(8,128)(2,1)S(1)}, bf16[128,2048]{1,0:T(8,128)(2,1)S(1)}, u32[]{:S(2)}, u32[]{:S(2)}) collective-permute-start(bf16[128,2048]{1,0:T(8,128)(2,1)S(1)} %shard_map.126), channel_id=1, source_target_pairs={{0,4},{1,5},{2,6},{3,7},{4,0},{5,1},{6,2},{7,3},{8,12},{9,13},{10,... | collective-permute-start | bytes 1572872 | tf_op jit(solution)/shard_map/ppermute | solution.py:27
  92.7 27.7 %collective-permute-start.29 = (bf16[128,2048]{1,0:T(8,128)(2,1)}, bf16[128,2048]{1,0:T(8,128)(2,1)}, u32[]{:S(2)}, u32[]{:S(2)}) collective-permute-start(bf16[128,2048]{1,0:T(8,128)(2,1)} %shard_map.127), channel_id=1, source_target_pairs={{0,12},{1,13},{2,14},{3,15},{4,8},{5,9},{6,10},{7,11},{8,4},{9,5},... | collective-permute-start | bytes 1572872 | tf_op jit(solution)/shard_map/ppermute | solution.py:27
  104.1 16.4 %collective-permute-start.28 = (bf16[128,2048]{1,0:T(8,128)(2,1)}, bf16[128,2048]{1,0:T(8,128)(2,1)}, u32[]{:S(2)}, u32[]{:S(2)}) collective-permute-start(bf16[128,2048]{1,0:T(8,128)(2,1)} %shard_map.128), channel_id=1, source_target_pairs={{0,4},{1,5},{2,6},{3,7},{4,0},{5,1},{6,2},{7,3},{8,12},{9,13},{10,... | collective-permute-start | bytes 1572872 | tf_op jit(solution)/shard_map/ppermute | solution.py:27
  131.5 27.5 %collective-permute-start.33 = (bf16[128,2048]{1,0:T(8,128)(2,1)}, bf16[128,2048]{1,0:T(8,128)(2,1)}, u32[]{:S(2)}, u32[]{:S(2)}) collective-permute-start(bf16[128,2048]{1,0:T(8,128)(2,1)} %fusion.167.refs_0_), channel_id=1, source_target_pairs={{0,4},{1,5},{2,6},{3,7},{4,0},{5,1},{6,2},{7,3},{8,12},{9,13},{10,... | collective-permute-start | bytes 1572872 | tf_op jit(solution)/shard_map/ppermute | solution.py:27
  137.3 29.9 %collective-permute-start.32 = (bf16[128,2048]{1,0:T(8,128)(2,1)}, bf16[128,2048]{1,0:T(8,128)(2,1)}, u32[]{:S(2)}, u32[]{:S(2)}) collective-permute-start(bf16[128,2048]{1,0:T(8,128)(2,1)} %fusion.167.refs_0_), channel_id=1, source_target_pairs={{0,8},{1,9},{2,10},{3,11},{4,12},{5,13},{6,14},{7,15},{8,0},{9,1},... | collective-permute-start | bytes 1572872 | tf_op jit(solution)/shard_map/ppermute | solution.py:27
  147.5 11.5 %collective-permute-start.36 = (bf16[48,2048]{1,0:T(8,128)(2,1)}, bf16[48,2048]{1,0:T(8,128)(2,1)}, u32[]{:S(2)}, u32[]{:S(2)}) collective-permute-start(bf16[48,2048]{1,0:T(8,128)(2,1)} %get-tuple-element.158), channel_id=1, source_target_pairs={{0,3},{1,2},{2,1},{3,0},{4,7},{5,6},{6,5},{7,4},{8,11},{9,10},{10,... | collective-permute-start | bytes 589832 | tf_op jit(solution)/shard_map/ppermute | solution.py:27
  167.2 14.9 %collective-permute-start.41 = (bf16[128,2048]{1,0:T(8,128)(2,1)}, bf16[128,2048]{1,0:T(8,128)(2,1)S(1)}, u32[]{:S(2)}, u32[]{:S(2)}) collective-permute-start(bf16[128,2048]{1,0:T(8,128)(2,1)} %collective-permute-done.32.refs_0_), channel_id=1, source_target_pairs={{0,4},{1,5},{2,6},{3,7},{4,0},{5,1},{6,2},{7,3},{8,12},{9,13},{10,... | collective-permute-start | bytes 1572872 | tf_op jit(solution)/shard_map/ppermute | solution.py:27
  190.2 16.4 %collective-permute-start.48 = (bf16[48,2176]{1,0:T(8,128)(2,1)S(1)}, bf16[48,2176]{1,0:T(8,128)(2,1)S(1)}, u32[]{:S(2)}, u32[]{:S(2)}) collective-permute-start(bf16[48,2176]{1,0:T(8,128)(2,1)S(1)} %get-tuple-element.183), channel_id=1, source_target_pairs={{0,1},{1,0},{2,3},{3,2},{4,5},{5,4},{6,7},{7,6},{8,9},{9,8},{10,11... | collective-permute-start | bytes 626696 | tf_op jit(solution)/shard_map/ppermute | solution.py:27
  190.6 16.0 %collective-permute-start.49 = (bf16[48,2176]{1,0:T(8,128)(2,1)S(1)}, bf16[48,2176]{1,0:T(8,128)(2,1)S(1)}, u32[]{:S(2)}, u32[]{:S(2)}) collective-permute-start(bf16[48,2176]{1,0:T(8,128)(2,1)S(1)} %get-tuple-element.184), channel_id=1, source_target_pairs={{0,2},{1,3},{2,0},{3,1},{4,6},{5,7},{6,4},{7,5},{8,10},{9,11},{10,... | collective-permute-start | bytes 626696 | tf_op jit(solution)/shard_map/ppermute | solution.py:27
  191.9 14.7 %collective-permute-start.50 = (bf16[48,2176]{1,0:T(8,128)(2,1)S(1)}, bf16[48,2176]{1,0:T(8,128)(2,1)S(1)}, u32[]{:S(2)}, u32[]{:S(2)}) collective-permute-start(bf16[48,2176]{1,0:T(8,128)(2,1)S(1)} %get-tuple-element.185), channel_id=1, source_target_pairs={{0,3},{1,2},{2,1},{3,0},{4,7},{5,6},{6,5},{7,4},{8,11},{9,10},{10,... | collective-permute-start | bytes 626696 | tf_op jit(solution)/shard_map/ppermute | solution.py:27
  207.4 15.4 %collective-permute-start.54 = (bf16[128,2176]{1,0:T(8,128)(2,1)S(1)}, bf16[128,2176]{1,0:T(8,128)(2,1)S(1)}, u32[]{:S(2)}, u32[]{:S(2)}) collective-permute-start(bf16[128,2176]{1,0:T(8,128)(2,1)S(1)} %get-tuple-element.192), channel_id=1, source_target_pairs={{0,4},{1,5},{2,6},{3,7},{4,0},{5,1},{6,2},{7,3},{8,12},{9,13},{10,... | collective-permute-start | bytes 1671176 | tf_op jit(solution)/shard_map/ppermute | solution.py:27
  224.8 10.5 %collective-permute-start.57 = (bf16[48,2176]{1,0:T(8,128)(2,1)S(1)}, bf16[48,2176]{1,0:T(8,128)(2,1)S(1)}, u32[]{:S(2)}, u32[]{:S(2)}) collective-permute-start(bf16[48,2176]{1,0:T(8,128)(2,1)S(1)} %get-tuple-element.198), channel_id=1, source_target_pairs={{0,3},{1,2},{2,1},{3,0},{4,7},{5,6},{6,5},{7,4},{8,11},{9,10},{10,... | collective-permute-start | bytes 626696 | tf_op jit(solution)/shard_map/ppermute | solution.py:27
  225.6 24.5 %collective-permute-start.62 = (bf16[128,2176]{1,0:T(8,128)(2,1)S(1)}, bf16[128,2176]{1,0:T(8,128)(2,1)S(1)}, u32[]{:S(2)}, u32[]{:S(2)}) collective-permute-start(bf16[128,2176]{1,0:T(8,128)(2,1)S(1)} %shard_map.135), channel_id=1, source_target_pairs={{0,12},{1,13},{2,14},{3,15},{4,8},{5,9},{6,10},{7,11},{8,4},{9,5},... | collective-permute-start | bytes 1671176 | tf_op jit(solution)/shard_map/ppermute | solution.py:27
  236.1 18.5 %collective-permute-start.61 = (bf16[128,2176]{1,0:T(8,128)(2,1)S(1)}, bf16[128,2176]{1,0:T(8,128)(2,1)S(1)}, u32[]{:S(2)}, u32[]{:S(2)}) collective-permute-start(bf16[128,2176]{1,0:T(8,128)(2,1)S(1)} %shard_map.136), channel_id=1, source_target_pairs={{0,4},{1,5},{2,6},{3,7},{4,0},{5,1},{6,2},{7,3},{8,12},{9,13},{10,... | collective-permute-start | bytes 1671176 | tf_op jit(solution)/shard_map/ppermute | solution.py:27
  238.6 10.7 %collective-permute-start.60 = (bf16[48,2176]{1,0:T(8,128)(2,1)S(1)}, bf16[48,2176]{1,0:T(8,128)(2,1)S(1)}, u32[]{:S(2)}, u32[]{:S(2)}) collective-permute-start(bf16[48,2176]{1,0:T(8,128)(2,1)S(1)} %get-tuple-element.202), channel_id=1, source_target_pairs={{0,3},{1,2},{2,1},{3,0},{4,7},{5,6},{6,5},{7,4},{8,11},{9,10},{10,... | collective-permute-start | bytes 626696 | tf_op jit(solution)/shard_map/ppermute | solution.py:27
  (84 other events, 628.5 us)

commit v5 on v4

--- a/solution.py
+++ b/solution.py
@@ -52,7 +52,7 @@
     return pl.CostEstimate(flops=0, bytes_accessed=0, transcendentals=0)
 
 
-def kernel_call(body, out_shape, *operands, scalars=()):
+def kernel_call(body, out_shape, *operands, scalars=(), mebibytes=8):
     return pl.pallas_call(
         body,
         out_shape=out_shape,
@@ -60,7 +60,7 @@
         + [pl.BlockSpec(memory_space=pltpu.VMEM)] * len(operands),
         out_specs=jax.tree.map(lambda _: pl.BlockSpec(memory_space=pltpu.VMEM), out_shape),
         cost_estimate=no_cost(),
-        compiler_params=pltpu.CompilerParams(vmem_limit_bytes=8 * 1024 * 1024),
+        compiler_params=pltpu.CompilerParams(vmem_limit_bytes=mebibytes * 1024 * 1024),
     )(*scalars, *operands)
 
 
@@ -238,6 +238,7 @@
         expert_ids.T,
         gate_values.T,
         frames_in,
+        mebibytes=56,
     )
     first_expert = (my_layer * peers).astype(jnp.int32).reshape(1)
     mine = my_peer.astype(jnp.int32).reshape(1)

time: 260 us -> 258 us (level)
    unnamed x102 -> x96, local copies, waits for them, and re-layouts: 6.01 us -> 3.42 us
where the time goes in v5:
time: 258 us
  waiting for transfers between devices  114 us (44%)
  starting transfers between devices  65.7 us (25%)
  matrix products  29.1 us (11%)
  Pallas kernels  22.8 us (9%)
  other arithmetic  10.2 us (4%)
  between operations  8.42 us (3%)
  local copies, waits for them, and re-layouts  7.63 us (3%)
    ppermute x60, waiting for transfers between devices, swap(): return lax.ppermute(block, 'ep', route)  113 us
    ppermute x60, starting transfers between devices, swap(): return lax.ppermute(block, 'ep', route)  57.2 us
    dot_general x26, matrix products, dot(): lax.dot_general(a, b, (dims, ((), ())), preferred_element_type=jnp.float32)  29.1 us
    pallas_call x17, Pallas kernels, kernel_call(): pl.pallas_call(body, out_shape=out_shape, in_specs=[pl.BlockSpec(memory_s...  22.8 us
  transfers between devices with their start and end apart: 63, of which 34 were waited for; matrix products, arithmetic and copies ran while one was open for 12% of the time, Pallas kernels for 6%

profile of v5, /device:TPU:0, one launch (start us, length us, event | category | flops | bytes accessed | tf_op | source)
XLA Modules:
  0.0 257.8 jit_solution(3788500385638246277)
XLA Ops:
  2.8 3.0 %collective-permute-start.1 = (bf16[128,2176]{1,0:T(8,128)(2,1)}, bf16[128,2176]{1,0:T(8,128)(2,1)}, u32[]{:S(2)}, u32[]{:S(2)}) collective-permute-start(bf16[128,2176]{1,0:T(8,128)(2,1)} %shard_map.121.refs_0_), channel_id=1, source_target_pairs={{0,4},{1,5},{2,6},{3,7},{4,0},{5,1},{6,2},{7,3},{8,12},{9,13},{10,... | collective-permute-start | bytes 1671176 | tf_op jit(solution)/shard_map/ppermute | solution.py:27
  12.1 5.8 %collective-permute-done.3 = bf16[48,2048]{1,0:T(8,128)(2,1)S(1)} collective-permute-done((bf16[48,2048]{1,0:T(8,128)(2,1)S(1)}, bf16[48,2048]{1,0:T(8,128)(2,1)S(1)}, u32[]{:S(2)}, u32[]{:S(2)}) %collective-permute-start.3) | collective-permute-done | bytes 196640 | tf_op jit(solution)/shard_map/ppermute | solution.py:27
  17.9 3.4 %collective-permute-done.4 = bf16[48,2048]{1,0:T(8,128)(2,1)S(1)} collective-permute-done((bf16[48,2048]{1,0:T(8,128)(2,1)S(1)}, bf16[48,2048]{1,0:T(8,128)(2,1)S(1)}, u32[]{:S(2)}, u32[]{:S(2)}) %collective-permute-start.4) | collective-permute-done | bytes 196640 | tf_op jit(solution)/shard_map/ppermute | solution.py:27
  21.4 7.4 %collective-permute-done.1.refs_0_ = bf16[128,2176]{1,0:T(8,128)(2,1)} collective-permute-done((bf16[128,2176]{1,0:T(8,128)(2,1)}, bf16[128,2176]{1,0:T(8,128)(2,1)}, u32[]{:S(2)}, u32[]{:S(2)}) %collective-permute-start.1) | collective-permute-done | bytes 557088 | tf_op jit(solution)/shard_map/ppermute | solution.py:27
  38.2 3.4 %collective-permute-done.7 = bf16[48,2048]{1,0:T(8,128)(2,1)S(1)} collective-permute-done((bf16[48,2048]{1,0:T(8,128)(2,1)S(1)}, bf16[48,2048]{1,0:T(8,128)(2,1)S(1)}, u32[]{:S(2)}, u32[]{:S(2)}) %collective-permute-start.7) | collective-permute-done | bytes 196640 | tf_op jit(solution)/shard_map/ppermute | solution.py:27
  60.3 3.4 %collective-permute-done.14 = bf16[48,2048]{1,0:T(8,128)(2,1)S(1)} collective-permute-done((bf16[48,2048]{1,0:T(8,128)(2,1)S(1)}, bf16[48,2048]{1,0:T(8,128)(2,1)S(1)}, u32[]{:S(2)}, u32[]{:S(2)}) %collective-permute-start.14) | collective-permute-done | bytes 196640 | tf_op jit(solution)/shard_map/ppermute | solution.py:27
  75.2 6.1 %collective-permute-done.19.refs_2_ = bf16[48,2048]{1,0:T(8,128)(2,1)S(1)} collective-permute-done((bf16[48,2048]{1,0:T(8,128)(2,1)S(1)}, bf16[48,2048]{1,0:T(8,128)(2,1)S(1)}, u32[]{:S(2)}, u32[]{:S(2)}) %collective-permute-start.19) | collective-permute-done | bytes 196640 | tf_op jit(solution)/shard_map/ppermute | solution.py:27
  83.8 3.5 %collective-permute-done.21.refs_4_ = bf16[128,2048]{1,0:T(8,128)(2,1)S(1)} collective-permute-done((bf16[128,2048]{1,0:T(8,128)(2,1)S(1)}, bf16[128,2048]{1,0:T(8,128)(2,1)S(1)}, u32[]{:S(2)}, u32[]{:S(2)}) %collective-permute-start.21) | collective-permute-done | bytes 524320 | tf_op jit(solution)/shard_map/ppermute | solution.py:27
  94.0 3.2 %collective-permute-done.23.refs_2_ = bf16[48,2048]{1,0:T(8,128)(2,1)S(1)} collective-permute-done((bf16[48,2048]{1,0:T(8,128)(2,1)S(1)}, bf16[48,2048]{1,0:T(8,128)(2,1)S(1)}, u32[]{:S(2)}, u32[]{:S(2)}) %collective-permute-start.23) | collective-permute-done | bytes 196640 | tf_op jit(solution)/shard_map/ppermute | solution.py:27
  97.2 3.4 %collective-permute-done.24.refs_3_ = bf16[48,2048]{1,0:T(8,128)(2,1)S(1)} collective-permute-done((bf16[48,2048]{1,0:T(8,128)(2,1)S(1)}, bf16[48,2048]{1,0:T(8,128)(2,1)S(1)}, u32[]{:S(2)}, u32[]{:S(2)}) %collective-permute-start.24) | collective-permute-done | bytes 196640 | tf_op jit(solution)/shard_map/ppermute | solution.py:27
  107.9 6.3 %collective-permute-done.26.refs_2_ = bf16[48,2048]{1,0:T(8,128)(2,1)S(1)} collective-permute-done((bf16[48,2048]{1,0:T(8,128)(2,1)}, bf16[48,2048]{1,0:T(8,128)(2,1)S(1)}, u32[]{:S(2)}, u32[]{:S(2)}) %collective-permute-start.26) | collective-permute-done | bytes 196640 | tf_op jit(solution)/shard_map/ppermute | solution.py:27
  123.3 3.5 %collective-permute-start.30 = (f32[1,12]{1,0:T(1,128)S(1)}, f32[1,12]{1,0:T(1,128)S(1)}, u32[]{:S(2)}, u32[]{:S(2)}) collective-permute-start(f32[1,12]{1,0:T(1,128)S(1)} %get-tuple-element.242), channel_id=1, source_target_pairs={{0,1},{1,2},{2,3},{3,4},{4,5},{5,6},{6,7},{7,8},{8,9},{9,10},{10,1... | collective-permute-start | bytes 152 | tf_op jit(solution)/shard_map/feet/ppermute | solution.py:33
  130.1 5.7 %collective-permute-start.33 = (bf16[128,2048]{1,0:T(8,128)(2,1)}, bf16[128,2048]{1,0:T(8,128)(2,1)}, u32[]{:S(2)}, u32[]{:S(2)}) collective-permute-start(bf16[128,2048]{1,0:T(8,128)(2,1)} %fusion.167.refs_0_), channel_id=1, source_target_pairs={{0,4},{1,5},{2,6},{3,7},{4,0},{5,1},{6,2},{7,3},{8,12},{9,13},{10,... | collective-permute-start | bytes 1572872 | tf_op jit(solution)/shard_map/ppermute | solution.py:27
  139.5 3.7 %collective-permute-start.37 = (f32[]{:T(128)}, f32[]{:T(128)}, u32[]{:S(2)}, u32[]{:S(2)}) collective-permute-start(f32[]{:T(128)} %add.170), channel_id=1, source_target_pairs={{0,16},{16,0},{1,17},{17,1},{2,18},{18,2},{3,19},{19,3},{4,20},{20... | collective-permute-start | bytes 20 | tf_op jit(solution)/shard_map/ppermute | solution.py:431
  149.2 4.9 %collective-permute-done.35 = bf16[48,2048]{1,0:T(8,128)(2,1)} collective-permute-done((bf16[48,2048]{1,0:T(8,128)(2,1)}, bf16[48,2048]{1,0:T(8,128)(2,1)}, u32[]{:S(2)}, u32[]{:S(2)}) %collective-permute-start.35) | collective-permute-done | bytes 196640 | tf_op jit(solution)/shard_map/ppermute | solution.py:27
  154.1 3.5 %collective-permute-done.36 = bf16[48,2048]{1,0:T(8,128)(2,1)} collective-permute-done((bf16[48,2048]{1,0:T(8,128)(2,1)}, bf16[48,2048]{1,0:T(8,128)(2,1)}, u32[]{:S(2)}, u32[]{:S(2)}) %collective-permute-start.36) | collective-permute-done | bytes 196640 | tf_op jit(solution)/shard_map/ppermute | solution.py:27
  171.7 3.0 %multiply_reduce_fusion.5 = (f32[192]{0:T(256)S(1)}, f32[192,768]{1,0:T(8,128)S(1)}) fusion(f32[192,768]{1,0:T(8,128)} %copy-done.22, f32[192,768]{1,0:T(8,128)} %copy-done.24, bf16[1,768,2048]{2,1,0:T(8,128)(2,1)S(1)} %copy-done, bf16[48,2048]{1,0:T(8,128)(2,1)} %collective-permute-done.36, bf16[48,2048]{1,0:T(8,128)(2,1)} %collective-permute-done.35, ...), kind=kOutput, calls=%fused_computation.130 | convolution fusion | flops 608157504 | bytes 5702400 | tf_op jit(solution)/shard_map/dot_general | solution.py:41
  192.7 3.3 %collective-permute-done.47 = bf16[48,2048]{1,0:T(8,128)(2,1)S(1)} collective-permute-done((bf16[48,2048]{1,0:T(8,128)(2,1)S(1)}, bf16[48,2048]{1,0:T(8,128)(2,1)S(1)}, u32[]{:S(2)}, u32[]{:S(2)}) %collective-permute-start.47) | collective-permute-done | bytes 196640 | tf_op jit(solution)/shard_map/ppermute | solution.py:27
  209.7 6.7 %collective-permute-done.52.refs_2_ = bf16[48,2176]{1,0:T(8,128)(2,1)S(1)} collective-permute-done((bf16[48,2176]{1,0:T(8,128)(2,1)S(1)}, bf16[48,2176]{1,0:T(8,128)(2,1)S(1)}, u32[]{:S(2)}, u32[]{:S(2)}) %collective-permute-start.52) | collective-permute-done | bytes 208928 | tf_op jit(solution)/shard_map/ppermute | solution.py:27
  224.2 4.0 %collective-permute-start.62 = (bf16[128,2176]{1,0:T(8,128)(2,1)S(1)}, bf16[128,2176]{1,0:T(8,128)(2,1)S(1)}, u32[]{:S(2)}, u32[]{:S(2)}) collective-permute-start(bf16[128,2176]{1,0:T(8,128)(2,1)S(1)} %shard_map.135), channel_id=1, source_target_pairs={{0,12},{1,13},{2,14},{3,15},{4,8},{5,9},{6,10},{7,11},{8,4},{9,5},... | collective-permute-start | bytes 1671176 | tf_op jit(solution)/shard_map/ppermute | solution.py:27
  230.3 3.6 %collective-permute-done.57.refs_3_ = bf16[48,2176]{1,0:T(8,128)(2,1)S(1)} collective-permute-done((bf16[48,2176]{1,0:T(8,128)(2,1)S(1)}, bf16[48,2176]{1,0:T(8,128)(2,1)S(1)}, u32[]{:S(2)}, u32[]{:S(2)}) %collective-permute-start.57) | collective-permute-done | bytes 208928 | tf_op jit(solution)/shard_map/ppermute | solution.py:27
  238.4 6.4 %collective-permute-done.59.refs_2_ = bf16[48,2176]{1,0:T(8,128)(2,1)S(1)} collective-permute-done((bf16[48,2176]{1,0:T(8,128)(2,1)S(1)}, bf16[48,2176]{1,0:T(8,128)(2,1)S(1)}, u32[]{:S(2)}, u32[]{:S(2)}) %collective-permute-start.59) | collective-permute-done | bytes 208928 | tf_op jit(solution)/shard_map/ppermute | solution.py:27
  244.8 3.1 %collective-permute-done.60.refs_3_ = bf16[48,2176]{1,0:T(8,128)(2,1)S(1)} collective-permute-done((bf16[48,2176]{1,0:T(8,128)(2,1)S(1)}, bf16[48,2176]{1,0:T(8,128)(2,1)S(1)}, u32[]{:S(2)}, u32[]{:S(2)}) %collective-permute-start.60) | collective-permute-done | bytes 208928 | tf_op jit(solution)/shard_map/ppermute | solution.py:27
  248.7 4.7 %collective-permute-done.61 = bf16[128,2176]{1,0:T(8,128)(2,1)S(1)} collective-permute-done((bf16[128,2176]{1,0:T(8,128)(2,1)S(1)}, bf16[128,2176]{1,0:T(8,128)(2,1)S(1)}, u32[]{:S(2)}, u32[]{:S(2)}) %collective-permute-start.61) | collective-permute-done | bytes 557088 | tf_op jit(solution)/shard_map/ppermute | solution.py:27
  (295 shorter events, 144.4 us)
Async XLA Ops:
  2.8 26.0 %collective-permute-start.1 = (bf16[128,2176]{1,0:T(8,128)(2,1)}, bf16[128,2176]{1,0:T(8,128)(2,1)}, u32[]{:S(2)}, u32[]{:S(2)}) collective-permute-start(bf16[128,2176]{1,0:T(8,128)(2,1)} %shard_map.121.refs_0_), channel_id=1, source_target_pairs={{0,4},{1,5},{2,6},{3,7},{4,0},{5,1},{6,2},{7,3},{8,12},{9,13},{10,... | collective-permute-start | bytes 1671176 | tf_op jit(solution)/shard_map/ppermute | solution.py:27
  7.5 27.3 %collective-permute-start = (bf16[128,2176]{1,0:T(8,128)(2,1)}, bf16[128,2176]{1,0:T(8,128)(2,1)S(1)}, u32[]{:S(2)}, u32[]{:S(2)}) collective-permute-start(bf16[128,2176]{1,0:T(8,128)(2,1)} %shard_map.121.refs_0_), channel_id=1, source_target_pairs={{0,8},{1,9},{2,10},{3,11},{4,12},{5,13},{6,14},{7,15},{8,0},{9,1},... | collective-permute-start | bytes 1671176 | tf_op jit(solution)/shard_map/ppermute | solution.py:27
  34.8 15.1 %collective-permute-start.8 = (bf16[128,2176]{1,0:T(8,128)(2,1)S(1)}, bf16[128,2176]{1,0:T(8,128)(2,1)S(1)}, u32[]{:S(2)}, u32[]{:S(2)}) collective-permute-start(bf16[128,2176]{1,0:T(8,128)(2,1)S(1)} %collective-permute-done.refs_0_), channel_id=1, source_target_pairs={{0,4},{1,5},{2,6},{3,7},{4,0},{5,1},{6,2},{7,3},{8,12},{9,13},{10,... | collective-permute-start | bytes 1671176 | tf_op jit(solution)/shard_map/ppermute | solution.py:27
  35.4 12.5 %collective-permute-start.10 = (bf16[48,2048]{1,0:T(8,128)(2,1)S(1)}, bf16[48,2048]{1,0:T(8,128)(2,1)S(1)}, u32[]{:S(2)}, u32[]{:S(2)}) collective-permute-start(bf16[48,2048]{1,0:T(8,128)(2,1)S(1)} %get-tuple-element.120), channel_id=1, source_target_pairs={{0,2},{1,3},{2,0},{3,1},{4,6},{5,7},{6,4},{7,5},{8,10},{9,11},{10,... | collective-permute-start | bytes 589832 | tf_op jit(solution)/shard_map/ppermute | solution.py:27
  36.9 13.0 %collective-permute-start.11 = (bf16[48,2048]{1,0:T(8,128)(2,1)S(1)}, bf16[48,2048]{1,0:T(8,128)(2,1)S(1)}, u32[]{:S(2)}, u32[]{:S(2)}) collective-permute-start(bf16[48,2048]{1,0:T(8,128)(2,1)S(1)} %get-tuple-element.121), channel_id=1, source_target_pairs={{0,3},{1,2},{2,1},{3,0},{4,7},{5,6},{6,5},{7,4},{8,11},{9,10},{10,... | collective-permute-start | bytes 589832 | tf_op jit(solution)/shard_map/ppermute | solution.py:27
  38.2 11.7 %collective-permute-start.9 = (bf16[48,2048]{1,0:T(8,128)(2,1)S(1)}, bf16[48,2048]{1,0:T(8,128)(2,1)S(1)}, u32[]{:S(2)}, u32[]{:S(2)}) collective-permute-start(bf16[48,2048]{1,0:T(8,128)(2,1)S(1)} %get-tuple-element.119), channel_id=1, source_target_pairs={{0,1},{1,0},{2,3},{3,2},{4,5},{5,4},{6,7},{7,6},{8,9},{9,8},{10,11... | collective-permute-start | bytes 589832 | tf_op jit(solution)/shard_map/ppermute | solution.py:27
  55.2 11.2 %collective-permute-start.15 = (bf16[48,2048]{1,0:T(8,128)(2,1)S(1)}, bf16[48,2048]{1,0:T(8,128)(2,1)S(1)}, u32[]{:S(2)}, u32[]{:S(2)}) collective-permute-start(bf16[48,2048]{1,0:T(8,128)(2,1)S(1)} %get-tuple-element.134), channel_id=1, source_target_pairs={{0,1},{1,0},{2,3},{3,2},{4,5},{5,4},{6,7},{7,6},{8,9},{9,8},{10,11... | collective-permute-start | bytes 589832 | tf_op jit(solution)/shard_map/ppermute | solution.py:27
  55.7 13.0 %collective-permute-start.16 = (bf16[48,2048]{1,0:T(8,128)(2,1)S(1)}, bf16[48,2048]{1,0:T(8,128)(2,1)S(1)}, u32[]{:S(2)}, u32[]{:S(2)}) collective-permute-start(bf16[48,2048]{1,0:T(8,128)(2,1)S(1)} %get-tuple-element.135), channel_id=1, source_target_pairs={{0,2},{1,3},{2,0},{3,1},{4,6},{5,7},{6,4},{7,5},{8,10},{9,11},{10,... | collective-permute-start | bytes 589832 | tf_op jit(solution)/shard_map/ppermute | solution.py:27
  57.4 14.2 %collective-permute-start.17 = (bf16[48,2048]{1,0:T(8,128)(2,1)S(1)}, bf16[48,2048]{1,0:T(8,128)(2,1)S(1)}, u32[]{:S(2)}, u32[]{:S(2)}) collective-permute-start(bf16[48,2048]{1,0:T(8,128)(2,1)S(1)} %get-tuple-element.136), channel_id=1, source_target_pairs={{0,3},{1,2},{2,1},{3,0},{4,7},{5,6},{6,5},{7,4},{8,11},{9,10},{10,... | collective-permute-start | bytes 589832 | tf_op jit(solution)/shard_map/ppermute | solution.py:27
  72.9 14.4 %collective-permute-start.21 = (bf16[128,2048]{1,0:T(8,128)(2,1)S(1)}, bf16[128,2048]{1,0:T(8,128)(2,1)S(1)}, u32[]{:S(2)}, u32[]{:S(2)}) collective-permute-start(bf16[128,2048]{1,0:T(8,128)(2,1)S(1)} %shard_map.126), channel_id=1, source_target_pairs={{0,4},{1,5},{2,6},{3,7},{4,0},{5,1},{6,2},{7,3},{8,12},{9,13},{10,... | collective-permute-start | bytes 1572872 | tf_op jit(solution)/shard_map/ppermute | solution.py:27
  91.4 27.7 %collective-permute-start.29 = (bf16[128,2048]{1,0:T(8,128)(2,1)}, bf16[128,2048]{1,0:T(8,128)(2,1)}, u32[]{:S(2)}, u32[]{:S(2)}) collective-permute-start(bf16[128,2048]{1,0:T(8,128)(2,1)} %shard_map.127), channel_id=1, source_target_pairs={{0,12},{1,13},{2,14},{3,15},{4,8},{5,9},{6,10},{7,11},{8,4},{9,5},... | collective-permute-start | bytes 1572872 | tf_op jit(solution)/shard_map/ppermute | solution.py:27
  102.8 16.3 %collective-permute-start.28 = (bf16[128,2048]{1,0:T(8,128)(2,1)}, bf16[128,2048]{1,0:T(8,128)(2,1)}, u32[]{:S(2)}, u32[]{:S(2)}) collective-permute-start(bf16[128,2048]{1,0:T(8,128)(2,1)} %shard_map.128), channel_id=1, source_target_pairs={{0,4},{1,5},{2,6},{3,7},{4,0},{5,1},{6,2},{7,3},{8,12},{9,13},{10,... | collective-permute-start | bytes 1572872 | tf_op jit(solution)/shard_map/ppermute | solution.py:27
  130.1 27.5 %collective-permute-start.33 = (bf16[128,2048]{1,0:T(8,128)(2,1)}, bf16[128,2048]{1,0:T(8,128)(2,1)}, u32[]{:S(2)}, u32[]{:S(2)}) collective-permute-start(bf16[128,2048]{1,0:T(8,128)(2,1)} %fusion.167.refs_0_), channel_id=1, source_target_pairs={{0,4},{1,5},{2,6},{3,7},{4,0},{5,1},{6,2},{7,3},{8,12},{9,13},{10,... | collective-permute-start | bytes 1572872 | tf_op jit(solution)/shard_map/ppermute | solution.py:27
  135.9 29.9 %collective-permute-start.32 = (bf16[128,2048]{1,0:T(8,128)(2,1)}, bf16[128,2048]{1,0:T(8,128)(2,1)}, u32[]{:S(2)}, u32[]{:S(2)}) collective-permute-start(bf16[128,2048]{1,0:T(8,128)(2,1)} %fusion.167.refs_0_), channel_id=1, source_target_pairs={{0,8},{1,9},{2,10},{3,11},{4,12},{5,13},{6,14},{7,15},{8,0},{9,1},... | collective-permute-start | bytes 1572872 | tf_op jit(solution)/shard_map/ppermute | solution.py:27
  146.1 11.5 %collective-permute-start.36 = (bf16[48,2048]{1,0:T(8,128)(2,1)}, bf16[48,2048]{1,0:T(8,128)(2,1)}, u32[]{:S(2)}, u32[]{:S(2)}) collective-permute-start(bf16[48,2048]{1,0:T(8,128)(2,1)} %get-tuple-element.158), channel_id=1, source_target_pairs={{0,3},{1,2},{2,1},{3,0},{4,7},{5,6},{6,5},{7,4},{8,11},{9,10},{10,... | collective-permute-start | bytes 589832 | tf_op jit(solution)/shard_map/ppermute | solution.py:27
  165.8 14.9 %collective-permute-start.41 = (bf16[128,2048]{1,0:T(8,128)(2,1)}, bf16[128,2048]{1,0:T(8,128)(2,1)S(1)}, u32[]{:S(2)}, u32[]{:S(2)}) collective-permute-start(bf16[128,2048]{1,0:T(8,128)(2,1)} %collective-permute-done.32.refs_0_), channel_id=1, source_target_pairs={{0,4},{1,5},{2,6},{3,7},{4,0},{5,1},{6,2},{7,3},{8,12},{9,13},{10,... | collective-permute-start | bytes 1572872 | tf_op jit(solution)/shard_map/ppermute | solution.py:27
  188.9 16.3 %collective-permute-start.48 = (bf16[48,2176]{1,0:T(8,128)(2,1)S(1)}, bf16[48,2176]{1,0:T(8,128)(2,1)S(1)}, u32[]{:S(2)}, u32[]{:S(2)}) collective-permute-start(bf16[48,2176]{1,0:T(8,128)(2,1)S(1)} %get-tuple-element.183), channel_id=1, source_target_pairs={{0,1},{1,0},{2,3},{3,2},{4,5},{5,4},{6,7},{7,6},{8,9},{9,8},{10,11... | collective-permute-start | bytes 626696 | tf_op jit(solution)/shard_map/ppermute | solution.py:27
  189.3 15.9 %collective-permute-start.49 = (bf16[48,2176]{1,0:T(8,128)(2,1)S(1)}, bf16[48,2176]{1,0:T(8,128)(2,1)S(1)}, u32[]{:S(2)}, u32[]{:S(2)}) collective-permute-start(bf16[48,2176]{1,0:T(8,128)(2,1)S(1)} %get-tuple-element.184), channel_id=1, source_target_pairs={{0,2},{1,3},{2,0},{3,1},{4,6},{5,7},{6,4},{7,5},{8,10},{9,11},{10,... | collective-permute-start | bytes 626696 | tf_op jit(solution)/shard_map/ppermute | solution.py:27
  190.5 14.7 %collective-permute-start.50 = (bf16[48,2176]{1,0:T(8,128)(2,1)S(1)}, bf16[48,2176]{1,0:T(8,128)(2,1)S(1)}, u32[]{:S(2)}, u32[]{:S(2)}) collective-permute-start(bf16[48,2176]{1,0:T(8,128)(2,1)S(1)} %get-tuple-element.185), channel_id=1, source_target_pairs={{0,3},{1,2},{2,1},{3,0},{4,7},{5,6},{6,5},{7,4},{8,11},{9,10},{10,... | collective-permute-start | bytes 626696 | tf_op jit(solution)/shard_map/ppermute | solution.py:27
  206.0 15.4 %collective-permute-start.54 = (bf16[128,2176]{1,0:T(8,128)(2,1)S(1)}, bf16[128,2176]{1,0:T(8,128)(2,1)S(1)}, u32[]{:S(2)}, u32[]{:S(2)}) collective-permute-start(bf16[128,2176]{1,0:T(8,128)(2,1)S(1)} %get-tuple-element.192), channel_id=1, source_target_pairs={{0,4},{1,5},{2,6},{3,7},{4,0},{5,1},{6,2},{7,3},{8,12},{9,13},{10,... | collective-permute-start | bytes 1671176 | tf_op jit(solution)/shard_map/ppermute | solution.py:27
  223.4 10.5 %collective-permute-start.57 = (bf16[48,2176]{1,0:T(8,128)(2,1)S(1)}, bf16[48,2176]{1,0:T(8,128)(2,1)S(1)}, u32[]{:S(2)}, u32[]{:S(2)}) collective-permute-start(bf16[48,2176]{1,0:T(8,128)(2,1)S(1)} %get-tuple-element.198), channel_id=1, source_target_pairs={{0,3},{1,2},{2,1},{3,0},{4,7},{5,6},{6,5},{7,4},{8,11},{9,10},{10,... | collective-permute-start | bytes 626696 | tf_op jit(solution)/shard_map/ppermute | solution.py:27
  224.2 24.5 %collective-permute-start.62 = (bf16[128,2176]{1,0:T(8,128)(2,1)S(1)}, bf16[128,2176]{1,0:T(8,128)(2,1)S(1)}, u32[]{:S(2)}, u32[]{:S(2)}) collective-permute-start(bf16[128,2176]{1,0:T(8,128)(2,1)S(1)} %shard_map.135), channel_id=1, source_target_pairs={{0,12},{1,13},{2,14},{3,15},{4,8},{5,9},{6,10},{7,11},{8,4},{9,5},... | collective-permute-start | bytes 1671176 | tf_op jit(solution)/shard_map/ppermute | solution.py:27
  234.7 18.6 %collective-permute-start.61 = (bf16[128,2176]{1,0:T(8,128)(2,1)S(1)}, bf16[128,2176]{1,0:T(8,128)(2,1)S(1)}, u32[]{:S(2)}, u32[]{:S(2)}) collective-permute-start(bf16[128,2176]{1,0:T(8,128)(2,1)S(1)} %shard_map.136), channel_id=1, source_target_pairs={{0,4},{1,5},{2,6},{3,7},{4,0},{5,1},{6,2},{7,3},{8,12},{9,13},{10,... | collective-permute-start | bytes 1671176 | tf_op jit(solution)/shard_map/ppermute | solution.py:27
  237.2 10.7 %collective-permute-start.60 = (bf16[48,2176]{1,0:T(8,128)(2,1)S(1)}, bf16[48,2176]{1,0:T(8,128)(2,1)S(1)}, u32[]{:S(2)}, u32[]{:S(2)}) collective-permute-start(bf16[48,2176]{1,0:T(8,128)(2,1)S(1)} %get-tuple-element.202), channel_id=1, source_target_pairs={{0,3},{1,2},{2,1},{3,0},{4,7},{5,6},{6,5},{7,4},{8,11},{9,10},{10,... | collective-permute-start | bytes 626696 | tf_op jit(solution)/shard_map/ppermute | solution.py:27
  (81 other events, 625.2 us)
